TPU v7x, 512 devices: a whole 4x8x8 slice. The times are simulated.
512 devices in a mesh: row: 32 (over y, z_hi, core), col: 16 (over x, z_lo).
Axes of the slice: x: 4, y: 8, z: 8 (z_hi: 2, z_lo: 4; z = z_hi * 4 + z_lo), core: 2. Of those that a mesh axis runs over, the one named last changes fastest.
Arguments:
- precision_matrix: float32 [12288, 12288], P('row', 'col'), may hold values from -1 to 3, as said below
- sample_rows: float32 [12288, 1024], P('row'), may hold values from -6 to 6
Outputs:
- updated_matrix: float32 [12288, 12288], P('row', 'col')
- next_product: float32 [12288, 1024], P(('row', 'col'))
Inputs may be any that keep to these rules, and one draw needn't show every extreme that they name: `precision_matrix`: Symmetric; diagonal entries between 1 and 3.
All inputs are finite; a program needn't handle non-finite values.
Results may differ from a plain program's by a relative error of at most 0.0003.
Values sent between devices are 32-bit elements; how exact they have to be, the bound alone decides.
No kernel may reach another device: no remote copies, remote signals or barrier semaphores. Data moves between devices by JAX's collectives and lax.ppermute only.
A program may use at most 64 MiB of HBM per device.

v0:
```python
import jax
import jax.numpy as jnp
from jax import lax
from jax.sharding import PartitionSpec as P

step_length = 0.5
penalty = 0.02


def filled_up(lines, peers):
    spare = -lines.shape[0] % peers
    if not spare:
        return lines
    return jnp.concatenate([lines, jnp.zeros((spare, *lines.shape[1:]), lines.dtype)])


def broadcast_by_parts(x, axis, root):
    lines = jnp.where(lax.axis_index(axis) == root, x, jnp.zeros_like(x)).reshape(
        -1, *x.shape[1:][-1:]
    )
    padded = filled_up(lines, lax.axis_size(axis))
    own = lax.psum_scatter(padded, axis, scatter_dimension=0, tiled=True)
    return lax.all_gather(own, axis, axis=0, tiled=True)[: len(lines)].reshape(x.shape)


def split_up(x, dim, peers):
    before, after = (x.shape[:dim], x.shape[dim + 1 :])
    return jnp.moveaxis(x.reshape(*before, peers, -1, *after), dim, 0)


def sum_at_owner(x, axis, dim):
    peers = lax.axis_size(axis)
    parts = lax.all_to_all(split_up(x, dim, peers), axis, 0, 0, tiled=True)
    return jnp.sum(parts, axis=0)


def from_everyone(x, axis):
    peers = lax.axis_size(axis)
    return lax.all_to_all(jnp.broadcast_to(x[None], (peers, *x.shape)), axis, 0, 0, tiled=True)


def in_order(parts, dim):
    parts = jnp.moveaxis(parts, 0, dim)
    shape = parts.shape
    return parts.reshape(*shape[:dim], shape[dim] * shape[dim + 1], *shape[dim + 2 :])


def collect(x, axis, dim):
    parts = from_everyone(x, axis)
    return in_order(parts, dim)


def mirror_tile(forward):
    rows = forward.shape[0]
    half = forward.shape[1] // 2
    groups = lax.axis_size("col")
    depth = rows // groups
    first = forward.reshape(groups, depth, 1, 2, half)
    first = lax.all_to_all(first, "col", split_axis=0, concat_axis=2, tiled=True)
    middle = first.reshape(depth, 2 * groups, 1, half)
    middle = lax.all_to_all(middle, "row", split_axis=1, concat_axis=2, tiled=True)
    final = middle.reshape(1, depth, groups, 2, half)
    final = lax.all_to_all(final, "col", split_axis=2, concat_axis=0, tiled=True)
    final = final.reshape(rows, 2, half)
    return jnp.transpose(final, (2, 1, 0)).reshape(half, 2 * rows)


def on_device(precision_matrix, sample_rows):
    highest = lax.Precision.HIGHEST
    row_count = precision_matrix.shape[0]
    col_count = precision_matrix.shape[1]
    samples = sample_rows.shape[1]
    row_index = lax.axis_index("row")
    col_index = lax.axis_index("col")
    pieces = [broadcast_by_parts(sample_rows, "row", 2 * col_index + half) for half in range(2)]
    data_cols = jnp.concatenate(pieces, axis=0)
    partial_value = jnp.dot(
        precision_matrix, data_cols, precision=highest, preferred_element_type=jnp.float32
    )
    piece = sum_at_owner(partial_value, "col", 0)
    product_rows = collect(piece, "col", 0)
    contract = (((1,), (1,)), ((), ()))
    forward = (
        lax.dot_general(
            product_rows, data_cols, contract, precision=highest, preferred_element_type=jnp.float32
        )
        / samples
    )
    mirrored = mirror_tile(forward)
    gradient = 0.5 * (forward + mirrored)
    global_rows = row_index * row_count + lax.broadcasted_iota(jnp.int32, (row_count, col_count), 0)
    global_cols = col_index * col_count + lax.broadcasted_iota(jnp.int32, (row_count, col_count), 1)
    on_diagonal = global_rows == global_cols
    inverse = 1.0 / jnp.where(on_diagonal, precision_matrix, 1.0)
    gradient = gradient - jnp.where(on_diagonal, inverse, 0.0)
    moved = precision_matrix - step_length * gradient
    shrunk = jnp.sign(moved) * jnp.maximum(jnp.abs(moved) - step_length * penalty, 0.0)
    updated = jnp.where(on_diagonal, moved, shrunk)
    next_partial = jnp.dot(
        updated, data_cols, precision=highest, preferred_element_type=jnp.float32
    )
    next_product = sum_at_owner(next_partial, "col", 0)
    return (updated, next_product)


def solution(mesh):
    placed = (P("row", "col"), P("row", None))
    return jax.shard_map(
        on_device,
        mesh=mesh,
        in_specs=placed,
        out_specs=(P("row", "col"), P(("row", "col"), None)),
        check_vma=False,
    )
```

profile of v0, /device:TPU:8, one launch (start us, length us, event | category | flops | bytes accessed | tf_op | source)
XLA Modules:
  0.0 646.0 jit_solution(8218770662339812741)
XLA Ops:
  9.0 131.8 %fusion.6 = (f32[16,1024]{1,0:T(8,128)S(1)}, f32[16,1024]{1,0:T(8,128)S(1)}) fusion(f32[384,1024]{1,0:T(8,128)S(1)} %get-tuple-element.7, f32[384,1024]{1,0:T(8,128)S(1)} %get-tuple-element.6), kind=kCustom, calls=%all-reduce-scatter.2 | all-reduce-scatter fusion | flops 1048577 | bytes 3278848
  144.7 7.2 %collective-permute-start.7 = (f32[12,1024]{1,0:T(8,128)S(1)}, f32[12,1024]{1,0:T(8,128)S(1)}, u32[]{:S(2)}, u32[]{:S(2)}) collective-permute-start(f32[12,1024]{1,0:T(8,128)S(1)} %slice), channel_id=1, source_target_pairs={{0,128},{16,144},{32,160},{48,176},{64,192},{80,208},{96,224},{112... | collective-permute-start | bytes 147464
  151.9 2.4 collective-permute-start.2
  154.4 6.8 %collective-permute-start.3 = (f32[16,1024]{1,0:T(8,128)S(1)}, f32[16,1024]{1,0:T(8,128)S(1)}, u32[]{:S(2)}, u32[]{:S(2)}) collective-permute-start(f32[16,1024]{1,0:T(8,128)S(1)} %get-tuple-element.4), channel_id=1, source_target_pairs={{0,64},{16,80},{32,96},{48,112},{64,128},{80,144},{96,160},{112,17... | collective-permute-start | bytes 196616
  162.5 3.0 collective-permute-start.5
  165.5 4.8 collective-permute-start.6
  174.2 6.9 %collective-permute-start.10 = (f32[16,1024]{1,0:T(8,128)S(1)}, f32[16,1024]{1,0:T(8,128)S(1)}, u32[]{:S(2)}, u32[]{:S(2)}) collective-permute-start(f32[16,1024]{1,0:T(8,128)S(1)} %get-tuple-element.5), channel_id=1, source_target_pairs={{0,48},{16,64},{32,80},{48,96},{64,112},{80,128},{96,144},{112,160... | collective-permute-start | bytes 196616
  181.0 4.0 collective-permute-start.11
  186.4 2.7 collective-permute-start.12
  189.0 5.4 collective-permute-start.13
  194.4 2.5 collective-permute-start.14
  198.9 6.4 collective-permute-start.9
  205.3 2.5 collective-permute-done.8
  207.8 2.6 collective-permute-done.9
  212.2 63.4 %all-gather.5.cloned.1.call-done = f32[32,12,1024]{2,1,0:T(8,128)} async-done(((f32[1,12,1024]{2,1,0:T(8,128)}), f32[32,12,1024]{2,1,0:T(8,128)}) %all-gather.5.cloned.1.call-update) | async-done | bytes 1572880 | tf_op jit(solution)/shard_map/all_gather | solution.py:23
  275.6 2.6 reshape.44
  279.7 87.6 %all-gather.7.cloned.1.call-done = f32[32,12,1024]{2,1,0:T(8,128)} async-done(((f32[1,12,1024]{2,1,0:T(8,128)}), f32[32,12,1024]{2,1,0:T(8,128)}) %all-gather.7.cloned.1.call-update) | async-done | bytes 1572880 | tf_op jit(solution)/shard_map/all_gather | solution.py:23
  367.3 2.6 reshape.46
  371.6 4.0 fusion.7
  375.7 44.1 %all_to_all.54 = f32[16,24,1024]{2,1,0:T(8,128)} all-to-all(f32[16,24,1024]{2,1,0:T(8,128)S(1)} %bitcast.42), channel_id=1, replica_groups=mesh['row'=32,'col'=16] {'col'}, dimensions={0} | all-to-all | bytes 3145728 | tf_op jit(solution)/shard_map/all_to_all | solution.py:33
  421.4 42.1 %all_to_all.55 = f32[16,24,1024]{2,1,0:T(8,128)S(1)} all-to-all(f32[16,24,1024]{2,1,0:T(8,128)S(1)} %broadcast_in_dim.11), channel_id=1, replica_groups=mesh['row'=32,'col'=16] {'col'}, dimensions={0} | all-to-all | bytes 3145728 | tf_op jit(solution)/shard_map/all_to_all | solution.py:39
  463.5 5.1 convolution_multiply_fusion
  468.6 2.9 reshape.37
  472.8 33.6 %all_to_all.56 = f32[16,24,1,2,384]{4,1,3,2,0:T(8,128)S(1)} all-to-all(f32[16,24,1,2,384]{4,1,3,2,0:T(8,128)S(1)} %copy.7), channel_id=1, replica_groups=mesh['row'=32,'col'=16] {'col'}, dimensions={0} | all-to-all | bytes 2359296 | tf_op jit(solution)/shard_map/all_to_all | solution.py:59
  506.4 42.2 %all_to_all.57 = f32[24,32,1,384]{3,0,2,1:T(8,128)} all-to-all(f32[24,32,1,384]{3,0,2,1:T(8,128)S(1)} %bitcast.44), channel_id=1, replica_groups=mesh['row'=32,'col'=16] {'row'}, dimensions={1} | all-to-all | bytes 2359296 | tf_op jit(solution)/shard_map/all_to_all | solution.py:61
  548.6 4.4 all-to-all-start.4
  553.0 30.9 %all-to-all-done.4 = f32[1,24,16,2,384]{4,1,3,0,2:T(8,128)} async-done(((f32[1,24,16,2,384]{4,1,3,0,2:T(8,128)}), f32[1,24,16,2,384]{4,1,3,0,2:T(8,128)}, u32[]{:S(2)}, u32[]{:S(2)}) %all-to-all-start.4) | async-done | bytes 1179680 | tf_op jit(solution)/shard_map/all_to_all | solution.py:63
  583.9 2.3 copy.10
  586.3 2.7 copy.12
  589.0 2.8 compare_select_fusion
  591.9 4.0 fusion.8
  595.9 42.5 %all_to_all.58 = f32[16,24,1024]{2,1,0:T(8,128)S(1)} all-to-all(f32[16,24,1024]{2,1,0:T(8,128)S(1)} %bitcast.41), channel_id=1, replica_groups=mesh['row'=32,'col'=16] {'col'}, dimensions={0} | all-to-all | bytes 3145728 | tf_op jit(solution)/shard_map/all_to_all | solution.py:33
  (43 shorter events, 22.1 us)
Async XLA Ops:
  7.2 268.4 %all-gather.5.cloned.1.call-start = ((), (), s32[]{:S(2)}) async-start(), calls=%async_computation.6 | async-start | bytes 2162688 | tf_op jit(solution)/shard_map/all_gather | solution.py:23
  140.9 21.6 %collective-permute-start = (f32[16,1024]{1,0:T(8,128)S(1)}, f32[16,1024]{1,0:T(8,128)S(1)}, u32[]{:S(2)}, u32[]{:S(2)}) collective-permute-start(f32[16,1024]{1,0:T(8,128)S(1)} %get-tuple-element.4), channel_id=1, source_target_pairs={{0,16},{16,32},{32,48},{48,64},{64,80},{80,96},{96,112},{112,128},... | collective-permute-start | bytes 196616
  142.8 22.8 %collective-permute-start.1 = (f32[16,1024]{1,0:T(8,128)S(1)}, f32[16,1024]{1,0:T(8,128)S(1)}, u32[]{:S(2)}, u32[]{:S(2)}) collective-permute-start(f32[16,1024]{1,0:T(8,128)S(1)} %get-tuple-element.4), channel_id=1, source_target_pairs={{0,32},{16,48},{32,64},{48,80},{64,96},{80,112},{96,128},{112,144}... | collective-permute-start | bytes 196616
  144.7 16.4 %collective-permute-start.7 = (f32[12,1024]{1,0:T(8,128)S(1)}, f32[12,1024]{1,0:T(8,128)S(1)}, u32[]{:S(2)}, u32[]{:S(2)}) collective-permute-start(f32[12,1024]{1,0:T(8,128)S(1)} %slice), channel_id=1, source_target_pairs={{0,128},{16,144},{32,160},{48,176},{64,192},{80,208},{96,224},{112... | collective-permute-start | bytes 147464
  151.9 20.3 %collective-permute-start.2 = (f32[16,1024]{1,0:T(8,128)S(1)}, f32[16,1024]{1,0:T(8,128)S(1)}, u32[]{:S(2)}, u32[]{:S(2)}) collective-permute-start(f32[16,1024]{1,0:T(8,128)S(1)} %get-tuple-element.4), channel_id=1, source_target_pairs={{0,48},{16,64},{32,80},{48,96},{64,112},{80,128},{96,144},{112,160... | collective-permute-start | bytes 196616
  154.4 17.9 %collective-permute-start.3 = (f32[16,1024]{1,0:T(8,128)S(1)}, f32[16,1024]{1,0:T(8,128)S(1)}, u32[]{:S(2)}, u32[]{:S(2)}) collective-permute-start(f32[16,1024]{1,0:T(8,128)S(1)} %get-tuple-element.4), channel_id=1, source_target_pairs={{0,64},{16,80},{32,96},{48,112},{64,128},{80,144},{96,160},{112,17... | collective-permute-start | bytes 196616
  161.2 11.1 %collective-permute-start.4 = (f32[16,1024]{1,0:T(8,128)S(1)}, f32[16,1024]{1,0:T(8,128)S(1)}, u32[]{:S(2)}, u32[]{:S(2)}) collective-permute-start(f32[16,1024]{1,0:T(8,128)S(1)} %get-tuple-element.4), channel_id=1, source_target_pairs={{0,80},{16,96},{32,112},{48,128},{64,144},{80,160},{96,176},{112,1... | collective-permute-start | bytes 196616
  162.5 9.8 %collective-permute-start.5 = (f32[16,1024]{1,0:T(8,128)S(1)}, f32[16,1024]{1,0:T(8,128)S(1)}, u32[]{:S(2)}, u32[]{:S(2)}) collective-permute-start(f32[16,1024]{1,0:T(8,128)S(1)} %get-tuple-element.4), channel_id=1, source_target_pairs={{0,96},{16,112},{32,128},{48,144},{64,160},{80,176},{96,192},{112,... | collective-permute-start | bytes 196616
  165.5 6.8 %collective-permute-start.6 = (f32[16,1024]{1,0:T(8,128)S(1)}, f32[16,1024]{1,0:T(8,128)S(1)}, u32[]{:S(2)}, u32[]{:S(2)}) collective-permute-start(f32[16,1024]{1,0:T(8,128)S(1)} %get-tuple-element.4), channel_id=1, source_target_pairs={{0,112},{16,128},{32,144},{48,160},{64,176},{80,192},{96,208},{112... | collective-permute-start | bytes 196616
  174.1 193.2 %all-gather.7.cloned.1.call-start = ((), (), s32[]{:S(2)}) async-start(), calls=%async_computation.7 | async-start | bytes 2162688 | tf_op jit(solution)/shard_map/all_gather | solution.py:23
  174.2 22.8 %collective-permute-start.10 = (f32[16,1024]{1,0:T(8,128)S(1)}, f32[16,1024]{1,0:T(8,128)S(1)}, u32[]{:S(2)}, u32[]{:S(2)}) collective-permute-start(f32[16,1024]{1,0:T(8,128)S(1)} %get-tuple-element.5), channel_id=1, source_target_pairs={{0,48},{16,64},{32,80},{48,96},{64,112},{80,128},{96,144},{112,160... | collective-permute-start | bytes 196616
  181.0 17.9 %collective-permute-start.11 = (f32[16,1024]{1,0:T(8,128)S(1)}, f32[16,1024]{1,0:T(8,128)S(1)}, u32[]{:S(2)}, u32[]{:S(2)}) collective-permute-start(f32[16,1024]{1,0:T(8,128)S(1)} %get-tuple-element.5), channel_id=1, source_target_pairs={{0,64},{16,80},{32,96},{48,112},{64,128},{80,144},{96,160},{112,17... | collective-permute-start | bytes 196616
  185.1 9.4 %collective-permute-start.15 = (f32[12,1024]{1,0:T(8,128)S(1)}, f32[12,1024]{1,0:T(8,128)S(1)}, u32[]{:S(2)}, u32[]{:S(2)}) collective-permute-start(f32[12,1024]{1,0:T(8,128)S(1)} %slice.1), channel_id=1, source_target_pairs={{0,128},{16,144},{32,160},{48,176},{64,192},{80,208},{96,224},{112... | collective-permute-start | bytes 147464
  186.4 18.9 %collective-permute-start.12 = (f32[16,1024]{1,0:T(8,128)S(1)}, f32[16,1024]{1,0:T(8,128)S(1)}, u32[]{:S(2)}, u32[]{:S(2)}) collective-permute-start(f32[16,1024]{1,0:T(8,128)S(1)} %get-tuple-element.5), channel_id=1, source_target_pairs={{0,80},{16,96},{32,112},{48,128},{64,144},{80,160},{96,176},{112,1... | collective-permute-start | bytes 196616
  189.0 16.2 %collective-permute-start.13 = (f32[16,1024]{1,0:T(8,128)S(1)}, f32[16,1024]{1,0:T(8,128)S(1)}, u32[]{:S(2)}, u32[]{:S(2)}) collective-permute-start(f32[16,1024]{1,0:T(8,128)S(1)} %get-tuple-element.5), channel_id=1, source_target_pairs={{0,96},{16,112},{32,128},{48,144},{64,160},{80,176},{96,192},{112,... | collective-permute-start | bytes 196616
  194.4 10.9 %collective-permute-start.14 = (f32[16,1024]{1,0:T(8,128)S(1)}, f32[16,1024]{1,0:T(8,128)S(1)}, u32[]{:S(2)}, u32[]{:S(2)}) collective-permute-start(f32[16,1024]{1,0:T(8,128)S(1)} %get-tuple-element.5), channel_id=1, source_target_pairs={{0,112},{16,128},{32,144},{48,160},{64,176},{80,192},{96,208},{112... | collective-permute-start | bytes 196616
  197.0 10.9 %collective-permute-start.8 = (f32[16,1024]{1,0:T(8,128)S(1)}, f32[16,1024]{1,0:T(8,128)S(1)}, u32[]{:S(2)}, u32[]{:S(2)}) collective-permute-start(f32[16,1024]{1,0:T(8,128)S(1)} %get-tuple-element.5), channel_id=1, source_target_pairs={{0,16},{16,32},{32,48},{48,64},{64,80},{80,96},{96,112},{112,128},... | collective-permute-start | bytes 196616
  198.9 11.5 %collective-permute-start.9 = (f32[16,1024]{1,0:T(8,128)S(1)}, f32[16,1024]{1,0:T(8,128)S(1)}, u32[]{:S(2)}, u32[]{:S(2)}) collective-permute-start(f32[16,1024]{1,0:T(8,128)S(1)} %get-tuple-element.5), channel_id=1, source_target_pairs={{0,32},{16,48},{32,64},{48,80},{64,96},{80,112},{96,128},{112,144}... | collective-permute-start | bytes 196616
  369.9 1.7 copy-start
  548.6 35.3 %all-to-all-start.4 = ((f32[1,24,16,2,384]{4,1,3,0,2:T(8,128)}), f32[1,24,16,2,384]{4,1,3,0,2:T(8,128)}, u32[]{:S(2)}, u32[]{:S(2)}) async-start(f32[1,24,16,2,384]{4,1,3,0,2:T(8,128)} %bitcast.43), calls=%async_computation.4 | async-start | bytes 2359296 | tf_op jit(solution)/shard_map/all_to_all | solution.py:63
  591.8 4.0 copy-start.1
Sparse Core Ops, SparseCore 0:
  174.2 101.3 all-gather.4
  279.5 87.7 all-gather.6
where the time goes:
time: 647 us; the launch traced here: 646 us
  blocking collectives  336 us (52%)
  waiting for transfers between devices  187 us (29%)
  starting transfers between devices  64.9 us (10%)
  local copies, waits for them, and re-layouts  22.7 us (4%)
  between operations  15.1 us (2%)
  matrix products  13.1 us (2%)
  other arithmetic  6.87 us (1%)
    all_gather x2, waiting for transfers between devices, broadcast_by_parts(): lax.all_gather(own, axis, axis=0, tiled=True)[:len(lines)].reshape(x.shape)  151 us
    unnamed x1, blocking collectives  132 us
    all_to_all x2, blocking collectives, sum_at_owner(): parts = lax.all_to_all(split_up(x, dim, peers), axis, 0, 0, tiled=True)  86.6 us
    unnamed x16, starting transfers between devices  60.4 us
    all_to_all x1, blocking collectives, mirror_tile(): lax.all_to_all(middle, 'row', split_axis=1, concat_axis=2, tiled=True)  42.2 us
    all_to_all x1, blocking collectives, from_everyone(): lax.all_to_all(jnp.broadcast_to(x[None], (peers, *x.shape)), axis, 0, 0,...  42.1 us
    all_to_all x1, blocking collectives, mirror_tile(): lax.all_to_all(first, 'col', split_axis=0, concat_axis=2, tiled=True)  33.6 us
    all_to_all x1, waiting for transfers between devices, mirror_tile(): lax.all_to_all(final, 'col', split_axis=2, concat_axis=0, tiled=True)  30.9 us
  transfers between devices with their start and end apart: 19, of which 5 were waited for; matrix products, arithmetic and copies ran while one was open for 1% of the time, Pallas kernels for 0%

commit v1 on v0

v1 whole, which is shorter than its diff:
```python
import jax
import jax.numpy as jnp
import numpy as np
from jax import lax
from jax.sharding import Mesh, PartitionSpec as P

step_length = 0.5
penalty = 0.02

PARTS = {"y": 8, "zh": 2, "c": 2, "x": 4, "zl": 4}
AXES = tuple(PARTS)
SIZES = tuple(PARTS.values())
PREC = lax.Precision.HIGH


def permute(v, move):
    count = int(np.prod(SIZES))
    pairs = []
    for k in range(count):
        at = [int(p) for p in np.unravel_index(k, SIZES)]
        pairs.append((k, int(np.ravel_multi_index(move(*at), SIZES))))
    return lax.ppermute(v, AXES, pairs)


def swap_core(v):
    return permute(v, lambda y, zh, c, x, zl: (y, zh, 1 - c, x, zl))


def swap_zh(v):
    return permute(v, lambda y, zh, c, x, zl: (y, 1 - zh, c, x, zl))


def transpose_chips(v):
    def move(y, zh, c, x, zl):
        i, j = 2 * y + zh, 4 * x + zl
        return (j // 2, j % 2, c, i // 4, i % 4)

    return permute(v, move)


def transpose_shifted(v):
    def move(y, zh, c, x, zl):
        i, j = 2 * ((y - c) % 8) + zh, 4 * x + zl
        return (j // 2, j % 2, c, i // 4, i % 4)

    return permute(v, move)


def pair_swap(v, axis, odd_step):
    at = AXES.index(axis)
    n = PARTS[axis]

    def move(*place):
        place = list(place)
        parity = (place[at] - place[2]) % 2
        step = 1 if parity == odd_step else -1
        place[at] = (place[at] + step) % n
        return tuple(place)

    return permute(v, move)


def take(v, start, size):
    return lax.dynamic_slice_in_dim(v, start, size, 0)


def put(v, part, start):
    return lax.dynamic_update_slice_in_dim(v, part, start, 0)


def sum_ring8(v, y, c):
    b = v.shape[0] // 8
    p = (y - c) % 8
    k, odd = p // 2, p % 2

    def pair(j):
        return take(v, (j % 4) * (2 * b), 2 * b)

    near = jnp.where(odd == 0, k + 1, k - 1)
    other = jnp.where(odd == 0, k - 1, k + 1)
    got = pair_swap(pair(k + 2), "y", 1)
    got = pair_swap(pair(near) + got, "y", 0)
    got = pair_swap(pair(other) + got, "y", 1)
    mine = pair(k) + got
    got = pair_swap(take(mine, (1 - odd) * b, b), "y", 0)
    return take(mine, odd * b, b) + got


def gather_ring8(v, y, c):
    b = v.shape[0]
    p = (y - c) % 8
    k, odd = p // 2, p % 2
    got = pair_swap(v, "y", 0)
    own = put(put(jnp.zeros((2 * b, *v.shape[1:]), v.dtype), v, odd * b), got, (1 - odd) * b)
    second = pair_swap(own, "y", 1)
    third = pair_swap(second, "y", 0)
    fourth = pair_swap(third, "y", 1)
    out = jnp.zeros((8 * b, *v.shape[1:]), v.dtype)
    near = jnp.where(odd == 0, k + 1, k - 1)
    other = jnp.where(odd == 0, k - 1, k + 1)
    for part, j in ((own, k), (second, other), (third, near), (fourth, k + 2)):
        out = put(out, part, (j % 4) * (2 * b))
    return out


def gather_ring4(v, x, c):
    b = v.shape[0]
    p = (x - c) % 4
    odd = p % 2
    first = pair_swap(v, "x", 0)
    second = pair_swap(jnp.concatenate([v, first]), "x", 1)
    out = jnp.zeros((4 * b, *v.shape[1:]), v.dtype)
    partner = jnp.where(odd == 0, x + 1, x - 1)
    far = jnp.where(odd == 0, x - 1, x + 1)
    for part, j in ((v, x), (first, partner), (second[:b], far), (second[b:], x + 2)):
        out = put(out, part, (j % 4) * b)
    return out


def scatter_sum(v, axis):
    n = PARTS[axis]
    parts = lax.all_to_all(v.reshape(n, -1, v.shape[1]), axis, 0, 0, tiled=True)
    return jnp.sum(parts, axis=0)


def both_cores(v, c):
    other = swap_core(v)
    out = jnp.zeros((2 * v.shape[0], *v.shape[1:]), v.dtype)
    return put(put(out, v, c * v.shape[0]), other, (1 - c) * v.shape[0])


def dot(a, b, contract):
    return lax.dot_general(
        a, b, (contract, ((), ())), precision=PREC, preferred_element_type=jnp.float32
    )


def on_device(precision_matrix, sample_rows):
    row_count, col_count = precision_matrix.shape
    samples = sample_rows.shape[1]
    y, zh, c, x, zl = (lax.axis_index(a) for a in AXES)
    row_chip, col_chip = 2 * y + zh, 4 * x + zl
    half = col_count // 2
    block = half // 8

    slices = transpose_chips(take(sample_rows, (col_chip // 2) * block, block))

    def partial_rows(h):
        cols = lax.dynamic_slice_in_dim(precision_matrix, h * half, half, 1)
        return dot(cols, sample_rows, ((0,), (0,)))

    got = swap_core(partial_rows(1 - c))
    partial_value = partial_rows(c) + got

    data_half = lax.all_gather(slices, "y", axis=0, tiled=True)

    product = sum_ring8(partial_value, y, c)
    product = product + swap_zh(product)

    own = transpose_shifted(take(product, zh * (block // 2), block // 2))
    own = lax.all_gather(own, "zl", axis=0, tiled=True)
    product_rows = gather_ring4(own, x, c)
    product_cols = both_cores(gather_ring8(product, y, c), c)
    data_cols = both_cores(data_half, c)

    last = ((1,), (1,))
    cross = dot(sample_rows, product_cols, last) + dot(product_rows, data_cols, last)
    gradient = cross * (0.5 / samples)

    global_rows = (2 * row_chip + c) * row_count + lax.broadcasted_iota(
        jnp.int32, (row_count, col_count), 0
    )
    global_cols = col_chip * col_count + lax.broadcasted_iota(
        jnp.int32, (row_count, col_count), 1
    )
    on_diagonal = global_rows == global_cols
    inverse = 1.0 / jnp.where(on_diagonal, precision_matrix, 1.0)
    gradient = gradient - jnp.where(on_diagonal, inverse, 0.0)
    moved = precision_matrix - step_length * gradient
    shrunk = jnp.sign(moved) * jnp.maximum(jnp.abs(moved) - step_length * penalty, 0.0)
    updated = jnp.where(on_diagonal, moved, shrunk)
    next_partial = dot(updated, data_cols, ((1,), (0,)))
    next_product = scatter_sum(scatter_sum(next_partial, "x"), "zl")
    return updated, next_product


def solution(mesh):
    parts = Mesh(mesh.devices.reshape(SIZES), AXES)
    row, col = ("y", "zh", "c"), ("x", "zl")
    return jax.shard_map(
        on_device,
        mesh=parts,
        in_specs=(P(row, col), P(row, None)),
        out_specs=(P(row, col), P(row + col, None)),
        check_vma=False,
    )
```

time: 647 us -> 247 us (0.38)
  the two profiles are of different devices: /device:TPU:8 before, /device:TPU:2 now
where the time goes in v1:
time: 247 us; the launch traced here: 246 us
  starting transfers between devices  87.4 us (35%)
  waiting for transfers between devices  68 us (28%)
  blocking collectives  36.6 us (15%)
  local copies, waits for them, and re-layouts  18.3 us (7%)
  between operations  14.8 us (6%)
  matrix products  13.9 us (6%)
  other arithmetic  6.74 us (3%)
    ppermute x16, starting transfers between devices, permute(): return lax.ppermute(v, AXES, pairs)  82.6 us
    ppermute x16, waiting for transfers between devices, permute(): return lax.ppermute(v, AXES, pairs)  60.8 us
    all_to_all x1, blocking collectives, scatter_sum(): parts = lax.all_to_all(v.reshape(n, -1, v.shape[1]), axis, 0, 0, tiled=True)  22.3 us
    all_gather x1, blocking collectives, on_device(): own = lax.all_gather(own, 'zl', axis=0, tiled=True)  14.3 us
    dot_general x5, matrix products, dot(): lax.dot_general(a, b, (contract, ((), ())), precision=PREC, preferred_ele...  13.9 us
    unnamed x18, local copies, waits for them, and re-layouts  8.63 us
    dynamic_update_slice x13, local copies, waits for them, and re-layouts, put(): return lax.dynamic_update_slice_in_dim(v, part, start, 0)  7.75 us
    all_to_all x1, waiting for transfers between devices, scatter_sum(): parts = lax.all_to_all(v.reshape(n, -1, v.shape[1]), axis, 0, 0, tiled=True)  7.2 us
  transfers between devices with their start and end apart: 18, of which 10 were waited for; matrix products, arithmetic and copies ran while one was open for 8% of the time, Pallas kernels for 0%

profile of v1, /device:TPU:2, one launch (start us, length us, event | category | flops | bytes accessed | tf_op | source)
XLA Modules:
  0.0 245.8 jit_solution(16221215767729838949)
XLA Ops:
  8.6 2.5 %fusion.6 = f32[384,1024]{1,0:T(8,128)S(1)} fusion(f32[384,1024]{1,0:T(8,128)S(1)} %copy-done, f32[384,768]{1,0:T(8,128)} %param.2, s32[]{:T(128)S(6)} %select_n.149), kind=kOutput, calls=%fused_computation.12 | convolution fusion | flops 905969664 | bytes 3735556 | tf_op jit(solution)/shard_map/dot_general | solution.py:133
  11.1 1.9 collective-permute-start
  13.1 3.4 %collective-permute-done = f32[384,1024]{1,0:T(8,128)} collective-permute-done((f32[384,1024]{1,0:T(8,128)S(1)}, f32[384,1024]{1,0:T(8,128)}, u32[]{:S(2)}, u32[]{:S(2)}) %collective-permute-start) | collective-permute-done | bytes 1572896 | tf_op jit(solution)/shard_map/ppermute | solution.py:22
  16.5 3.1 %convolution_add_fusion = f32[384,1024]{1,0:T(8,128)S(1)} fusion(f32[384,1024]{1,0:T(8,128)} %collective-permute-done, f32[384,1024]{1,0:T(8,128)S(1)} %copy-done, f32[384,768]{1,0:T(8,128)} %param.2, s32[]{:T(128)S(6)} %select_n.148), kind=kOutput, calls=%fused_computation.3 | convolution fusion | flops 906362880 | bytes 5308420 | tf_op jit(solution)/shard_map/dot_general | solution.py:133
  19.6 5.4 %collective-permute-start.1 = (f32[96,1024]{1,0:T(8,128)S(1)}, f32[96,1024]{1,0:T(8,128)}, u32[]{:S(2)}, u32[]{:S(2)}) collective-permute-start(f32[96,1024]{1,0:T(8,128)S(1)} %constant_dynamic-slice_fusion.3), channel_id=1, source_target_pairs={{0,448},{1,449},{2,450},{3,451},{4,452},{5,453},{6,454},{7,455},{8... | collective-permute-start | bytes 1179656 | tf_op jit(solution)/shard_map/ppermute | solution.py:22
  25.1 5.8 %collective-permute-done.1 = f32[96,1024]{1,0:T(8,128)} collective-permute-done((f32[96,1024]{1,0:T(8,128)S(1)}, f32[96,1024]{1,0:T(8,128)}, u32[]{:S(2)}, u32[]{:S(2)}) %collective-permute-start.1) | collective-permute-done | bytes 393248 | tf_op jit(solution)/shard_map/ppermute | solution.py:22
  31.9 2.0 collective-permute-start.2
  34.7 5.7 %collective-permute-start.14 = (f32[48,1024]{1,0:T(8,128)}, f32[48,1024]{1,0:T(8,128)}, u32[]{:S(2)}, u32[]{:S(2)}) collective-permute-start(f32[48,1024]{1,0:T(8,128)} %constant_dynamic-slice_fusion), channel_id=1, source_target_pairs={{0,0},{1,32},{2,64},{3,96},{4,128},{5,160},{6,192},{7,224},{8,256}... | collective-permute-start | bytes 589832 | tf_op jit(solution)/shard_map/ppermute | solution.py:22
  40.4 23.3 %collective-permute-done.14 = f32[48,1024]{1,0:T(8,128)} collective-permute-done((f32[48,1024]{1,0:T(8,128)}, f32[48,1024]{1,0:T(8,128)}, u32[]{:S(2)}, u32[]{:S(2)}) %collective-permute-start.14) | collective-permute-done | bytes 196640 | tf_op jit(solution)/shard_map/ppermute | solution.py:22
  66.8 9.0 %collective-permute-done.3 = f32[96,1024]{1,0:T(8,128)} collective-permute-done((f32[96,1024]{1,0:T(8,128)S(1)}, f32[96,1024]{1,0:T(8,128)}, u32[]{:S(2)}, u32[]{:S(2)}) %collective-permute-start.3) | collective-permute-done | bytes 393248 | tf_op jit(solution)/shard_map/ppermute | solution.py:22
  76.9 7.6 %collective-permute-start.4 = (f32[48,1024]{1,0:T(8,128)S(1)}, f32[48,1024]{1,0:T(8,128)S(1)}, u32[]{:S(2)}, u32[]{:S(2)}) collective-permute-start(f32[48,1024]{1,0:T(8,128)S(1)} %constant_dynamic-slice_fusion.2), channel_id=1, source_target_pairs={{0,64},{1,65},{2,66},{3,67},{4,68},{5,69},{6,70},{7,71},{8,72},{9,... | collective-permute-start | bytes 589832 | tf_op jit(solution)/shard_map/ppermute | solution.py:22
  84.4 3.6 %collective-permute-done.4 = f32[48,1024]{1,0:T(8,128)S(1)} collective-permute-done((f32[48,1024]{1,0:T(8,128)S(1)}, f32[48,1024]{1,0:T(8,128)S(1)}, u32[]{:S(2)}, u32[]{:S(2)}) %collective-permute-start.4) | collective-permute-done | bytes 196640 | tf_op jit(solution)/shard_map/ppermute | solution.py:22
  88.1 15.1 %collective-permute-start.5 = (f32[48,1024]{1,0:T(8,128)S(1)}, f32[48,1024]{1,0:T(8,128)S(1)}, u32[]{:S(2)}, u32[]{:S(2)}) collective-permute-start(f32[48,1024]{1,0:T(8,128)S(1)} %dynamic-slice_add_fusion.3), channel_id=1, source_target_pairs={{0,32},{1,33},{2,34},{3,35},{4,36},{5,37},{6,38},{7,39},{8,40},{9,... | collective-permute-start | bytes 589832 | tf_op jit(solution)/shard_map/ppermute | solution.py:22
  103.2 5.6 %collective-permute-done.5 = f32[48,1024]{1,0:T(8,128)S(1)} collective-permute-done((f32[48,1024]{1,0:T(8,128)S(1)}, f32[48,1024]{1,0:T(8,128)S(1)}, u32[]{:S(2)}, u32[]{:S(2)}) %collective-permute-start.5) | collective-permute-done | bytes 196640 | tf_op jit(solution)/shard_map/ppermute | solution.py:22
  108.9 3.3 %collective-permute-start.6 = (f32[48,1024]{1,0:T(8,128)S(1)}, f32[48,1024]{1,0:T(8,128)S(1)}, u32[]{:S(2)}, u32[]{:S(2)}) collective-permute-start(f32[48,1024]{1,0:T(8,128)S(1)} %get-tuple-element.7), channel_id=1, source_target_pairs={{0,64},{1,65},{2,66},{3,67},{4,68},{5,69},{6,70},{7,71},{8,72},{9,... | collective-permute-start | bytes 589832 | tf_op jit(solution)/shard_map/ppermute | solution.py:22
  112.2 6.6 %collective-permute-done.6 = f32[48,1024]{1,0:T(8,128)S(1)} collective-permute-done((f32[48,1024]{1,0:T(8,128)S(1)}, f32[48,1024]{1,0:T(8,128)S(1)}, u32[]{:S(2)}, u32[]{:S(2)}) %collective-permute-start.6) | collective-permute-done | bytes 196640 | tf_op jit(solution)/shard_map/ppermute | solution.py:22
  120.7 11.1 %collective-permute-start.11 = (f32[24,1024]{1,0:T(8,128)S(1)}, f32[24,1024]{1,0:T(8,128)S(1)}, u32[]{:S(2)}, u32[]{:S(2)}) collective-permute-start(f32[24,1024]{1,0:T(8,128)S(1)} %constant_dynamic-slice_fusion.1), channel_id=1, source_target_pairs={{0,0},{1,32},{2,64},{3,96},{4,128},{5,160},{6,192},{7,224},{8,256}... | collective-permute-start | bytes 294920 | tf_op jit(solution)/shard_map/ppermute | solution.py:22
  131.9 11.6 %collective-permute-start.8 = (f32[96,1024]{1,0:T(8,128)S(1)}, f32[96,1024]{1,0:T(8,128)}, u32[]{:S(2)}, u32[]{:S(2)}) collective-permute-start(f32[96,1024]{1,0:T(8,128)S(1)} %collective-permute-done.7), channel_id=1, source_target_pairs={{0,64},{1,65},{2,66},{3,67},{4,68},{5,69},{6,70},{7,71},{8,72},{9,... | collective-permute-start | bytes 1179656 | tf_op jit(solution)/shard_map/ppermute | solution.py:22
  143.5 14.3 %all_gather.6 = f32[96,1024]{1,0:T(8,128)S(1)} all-gather(f32[24,1024]{1,0:T(8,128)S(1)} %collective-permute-done.11), channel_id=1, replica_groups=mesh['y'=8,'zh'=2,'c'=2,'x'=4,'zl'=4] {'zl'}, dimensions={0}, use_global_device_ids=true | all-gather | bytes 491520 | tf_op jit(solution)/shard_map/all_gather | solution.py:161
  157.8 4.4 %collective-permute-start.12 = (f32[96,1024]{1,0:T(8,128)S(1)}, f32[96,1024]{1,0:T(8,128)}, u32[]{:S(2)}, u32[]{:S(2)}) collective-permute-start(f32[96,1024]{1,0:T(8,128)S(1)} %all_gather.6), channel_id=1, source_target_pairs={{0,4},{1,5},{2,6},{3,7},{4,0},{5,1},{6,2},{7,3},{8,12},{9,13},{10,... | collective-permute-start | bytes 1179656 | tf_op jit(solution)/shard_map/ppermute | solution.py:22
  164.2 4.7 %collective-permute-start.9 = (f32[96,1024]{1,0:T(8,128)}, f32[96,1024]{1,0:T(8,128)S(1)}, u32[]{:S(2)}, u32[]{:S(2)}) collective-permute-start(f32[96,1024]{1,0:T(8,128)} %collective-permute-done.8), channel_id=1, source_target_pairs={{0,448},{1,449},{2,450},{3,451},{4,452},{5,453},{6,454},{7,455},{8... | collective-permute-start | bytes 1179656 | tf_op jit(solution)/shard_map/ppermute | solution.py:22
  169.9 2.0 pad_maximum_fusion
  175.3 2.1 collective-permute-start.10
  177.5 2.7 %copy.10 = f32[384,768]{0,1:T(8,128)} copy(f32[384,768]{1,0:T(8,128)} %param.2) | data formatting | bytes 2359296 | tf_op args[0]
  183.0 3.1 %collective-permute-done.13 = f32[192,1024]{1,0:T(8,128)} collective-permute-done((f32[192,1024]{1,0:T(8,128)}, f32[192,1024]{1,0:T(8,128)}, u32[]{:S(2)}, u32[]{:S(2)}) %collective-permute-start.13) | collective-permute-done | bytes 786464 | tf_op jit(solution)/shard_map/ppermute | solution.py:22
  189.7 2.7 %fusion.11 = f32[384,768]{0,1:T(8,128)S(1)} fusion(f32[384,1024]{1,0:T(8,128)S(1)} %slice_dynamic-update-slice_fusion, f32[768,1024]{1,0:T(8,128)S(1)} %constant_dynamic-update-slice_fusion), kind=kOutput, calls=%fused_computation.41 | convolution fusion | flops 1811939328 | bytes 5898240 | tf_op jit(solution)/shard_map/dot_general | solution.py:133
  194.8 3.3 %compare_select_fusion = f32[384,768]{0,1:T(8,128)S(1)} fusion(f32[384,768]{0,1:T(8,128)S(1)} %copy-done.5, f32[384,768]{0,1:T(8,128)S(1)} %fusion.11, f32[768,1024]{1,0:T(8,128)S(1)} %constant_dynamic-update-slice_fusion.4, f32[384,1024]{1,0:T(8,128)S(1)} %copy-done, s32[384]{0:T(512)S(1)} %iota_add_fusion.1, s32[768]{0:T(1024)S(1)} %iota_add_fusion), kind=kOutput, calls=%fused_computation | convolution fusion | flops 1816363008 | bytes 8262144 | tf_op jit(solution)/shard_map/dot_general | solution.py:133
  198.1 2.3 fusion.12
  200.4 22.3 %all_to_all.10 = f32[4,96,1024]{2,1,0:T(8,128)S(1)} all-to-all(f32[4,96,1024]{2,1,0:T(8,128)S(1)} %bitcast.24), channel_id=1, replica_groups=mesh['y'=8,'zh'=2,'c'=2,'x'=4,'zl'=4] {'x'}, dimensions={0} | all-to-all | bytes 3145728 | tf_op jit(solution)/shard_map/all_to_all | solution.py:122
  223.6 4.8 %all-to-all-start.1 = ((f32[4,24,1024]{2,1,0:T(8,128)}), f32[4,24,1024]{2,1,0:T(8,128)S(1)}, u32[]{:S(2)}, u32[]{:S(2)}) async-start(f32[4,24,1024]{2,1,0:T(8,128)} %bitcast.2), calls=%async_computation.1 | async-start | bytes 786432 | tf_op jit(solution)/shard_map/all_to_all | solution.py:122
  228.4 2.7 %copy.11 = f32[384,768]{1,0:T(8,128)} copy(f32[384,768]{0,1:T(8,128)} %copy-done.1) | data formatting | bytes 2359296
  231.1 7.2 %all-to-all-done.1 = f32[4,24,1024]{2,1,0:T(8,128)S(1)} async-done(((f32[4,24,1024]{2,1,0:T(8,128)}), f32[4,24,1024]{2,1,0:T(8,128)S(1)}, u32[]{:S(2)}, u32[]{:S(2)}) %all-to-all-start.1) | async-done | bytes 393248 | tf_op jit(solution)/shard_map/all_to_all | solution.py:122
  (62 shorter events, 25.8 us)
Async XLA Ops:
  7.2 1.4 copy-start
  7.2 155.0 %all-gather.2.cloned.1.call-start = ((), (), s32[]{:S(2)}) async-start(), calls=%async_computation.2 | async-start | bytes 1769472 | tf_op jit(solution)/shard_map/all_gather | solution.py:155
  11.1 5.4 %collective-permute-start = (f32[384,1024]{1,0:T(8,128)S(1)}, f32[384,1024]{1,0:T(8,128)}, u32[]{:S(2)}, u32[]{:S(2)}) collective-permute-start(f32[384,1024]{1,0:T(8,128)S(1)} %fusion.6), channel_id=1, source_target_pairs={{0,16},{1,17},{2,18},{3,19},{4,20},{5,21},{6,22},{7,23},{8,24},{9,... | collective-permute-start | bytes 4718600 | tf_op jit(solution)/shard_map/ppermute | solution.py:22
  19.6 11.2 %collective-permute-start.1 = (f32[96,1024]{1,0:T(8,128)S(1)}, f32[96,1024]{1,0:T(8,128)}, u32[]{:S(2)}, u32[]{:S(2)}) collective-permute-start(f32[96,1024]{1,0:T(8,128)S(1)} %constant_dynamic-slice_fusion.3), channel_id=1, source_target_pairs={{0,448},{1,449},{2,450},{3,451},{4,452},{5,453},{6,454},{7,455},{8... | collective-permute-start | bytes 1179656 | tf_op jit(solution)/shard_map/ppermute | solution.py:22
  31.9 31.8 %collective-permute-start.2 = (f32[96,1024]{1,0:T(8,128)S(1)}, f32[96,1024]{1,0:T(8,128)}, u32[]{:S(2)}, u32[]{:S(2)}) collective-permute-start(f32[96,1024]{1,0:T(8,128)S(1)} %dynamic-slice_add_fusion), channel_id=1, source_target_pairs={{0,64},{1,65},{2,66},{3,67},{4,68},{5,69},{6,70},{7,71},{8,72},{9,... | collective-permute-start | bytes 1179656 | tf_op jit(solution)/shard_map/ppermute | solution.py:22
  34.7 29.0 %collective-permute-start.14 = (f32[48,1024]{1,0:T(8,128)}, f32[48,1024]{1,0:T(8,128)}, u32[]{:S(2)}, u32[]{:S(2)}) collective-permute-start(f32[48,1024]{1,0:T(8,128)} %constant_dynamic-slice_fusion), channel_id=1, source_target_pairs={{0,0},{1,32},{2,64},{3,96},{4,128},{5,160},{6,192},{7,224},{8,256}... | collective-permute-start | bytes 589832 | tf_op jit(solution)/shard_map/ppermute | solution.py:22
  64.8 11.0 %collective-permute-start.3 = (f32[96,1024]{1,0:T(8,128)S(1)}, f32[96,1024]{1,0:T(8,128)}, u32[]{:S(2)}, u32[]{:S(2)}) collective-permute-start(f32[96,1024]{1,0:T(8,128)S(1)} %dynamic-slice_add_fusion.1), channel_id=1, source_target_pairs={{0,448},{1,449},{2,450},{3,451},{4,452},{5,453},{6,454},{7,455},{8... | collective-permute-start | bytes 1179656 | tf_op jit(solution)/shard_map/ppermute | solution.py:22
  76.9 11.2 %collective-permute-start.4 = (f32[48,1024]{1,0:T(8,128)S(1)}, f32[48,1024]{1,0:T(8,128)S(1)}, u32[]{:S(2)}, u32[]{:S(2)}) collective-permute-start(f32[48,1024]{1,0:T(8,128)S(1)} %constant_dynamic-slice_fusion.2), channel_id=1, source_target_pairs={{0,64},{1,65},{2,66},{3,67},{4,68},{5,69},{6,70},{7,71},{8,72},{9,... | collective-permute-start | bytes 589832 | tf_op jit(solution)/shard_map/ppermute | solution.py:22
  88.1 20.7 %collective-permute-start.5 = (f32[48,1024]{1,0:T(8,128)S(1)}, f32[48,1024]{1,0:T(8,128)S(1)}, u32[]{:S(2)}, u32[]{:S(2)}) collective-permute-start(f32[48,1024]{1,0:T(8,128)S(1)} %dynamic-slice_add_fusion.3), channel_id=1, source_target_pairs={{0,32},{1,33},{2,34},{3,35},{4,36},{5,37},{6,38},{7,39},{8,40},{9,... | collective-permute-start | bytes 589832 | tf_op jit(solution)/shard_map/ppermute | solution.py:22
  108.9 9.9 %collective-permute-start.6 = (f32[48,1024]{1,0:T(8,128)S(1)}, f32[48,1024]{1,0:T(8,128)S(1)}, u32[]{:S(2)}, u32[]{:S(2)}) collective-permute-start(f32[48,1024]{1,0:T(8,128)S(1)} %get-tuple-element.7), channel_id=1, source_target_pairs={{0,64},{1,65},{2,66},{3,67},{4,68},{5,69},{6,70},{7,71},{8,72},{9,... | collective-permute-start | bytes 589832 | tf_op jit(solution)/shard_map/ppermute | solution.py:22
  118.8 45.4 %copy-start.2 = (f32[96,1024]{1,0:T(8,128)}, f32[96,1024]{1,0:T(8,128)S(1)}, u32[]{:S(2)}) copy-start(f32[96,1024]{1,0:T(8,128)S(1)} %constant_dynamic-update-slice_fusion.10) | copy-start | bytes 1179652
  118.8 13.1 %collective-permute-start.7 = (f32[96,1024]{1,0:T(8,128)S(1)}, f32[96,1024]{1,0:T(8,128)S(1)}, u32[]{:S(2)}, u32[]{:S(2)}) collective-permute-start(f32[96,1024]{1,0:T(8,128)S(1)} %constant_dynamic-update-slice_fusion.10), channel_id=1, source_target_pairs={{0,448},{1,449},{2,450},{3,451},{4,452},{5,453},{6,454},{7,455},{8... | collective-permute-start | bytes 1179656 | tf_op jit(solution)/shard_map/ppermute | solution.py:22
  120.7 22.8 %collective-permute-start.11 = (f32[24,1024]{1,0:T(8,128)S(1)}, f32[24,1024]{1,0:T(8,128)S(1)}, u32[]{:S(2)}, u32[]{:S(2)}) collective-permute-start(f32[24,1024]{1,0:T(8,128)S(1)} %constant_dynamic-slice_fusion.1), channel_id=1, source_target_pairs={{0,0},{1,32},{2,64},{3,96},{4,128},{5,160},{6,192},{7,224},{8,256}... | collective-permute-start | bytes 294920 | tf_op jit(solution)/shard_map/ppermute | solution.py:22
  131.9 32.3 %copy-start.6 = (f32[96,1024]{1,0:T(8,128)}, f32[96,1024]{1,0:T(8,128)S(1)}, u32[]{:S(2)}) copy-start(f32[96,1024]{1,0:T(8,128)S(1)} %collective-permute-done.7) | copy-start | bytes 1179652
  131.9 32.3 %collective-permute-start.8 = (f32[96,1024]{1,0:T(8,128)S(1)}, f32[96,1024]{1,0:T(8,128)}, u32[]{:S(2)}, u32[]{:S(2)}) collective-permute-start(f32[96,1024]{1,0:T(8,128)S(1)} %collective-permute-done.7), channel_id=1, source_target_pairs={{0,64},{1,65},{2,66},{3,67},{4,68},{5,69},{6,70},{7,71},{8,72},{9,... | collective-permute-start | bytes 1179656 | tf_op jit(solution)/shard_map/ppermute | solution.py:22
  157.8 12.2 %collective-permute-start.12 = (f32[96,1024]{1,0:T(8,128)S(1)}, f32[96,1024]{1,0:T(8,128)}, u32[]{:S(2)}, u32[]{:S(2)}) collective-permute-start(f32[96,1024]{1,0:T(8,128)S(1)} %all_gather.6), channel_id=1, source_target_pairs={{0,4},{1,5},{2,6},{3,7},{4,0},{5,1},{6,2},{7,3},{8,12},{9,13},{10,... | collective-permute-start | bytes 1179656 | tf_op jit(solution)/shard_map/ppermute | solution.py:22
  162.2 26.0 %collective-permute-start.15 = (f32[384,1024]{1,0:T(8,128)}, f32[384,1024]{1,0:T(8,128)}, u32[]{:S(2)}, u32[]{:S(2)}) collective-permute-start(f32[384,1024]{1,0:T(8,128)} %all-gather.2.cloned.1.call-done), channel_id=1, source_target_pairs={{0,16},{1,17},{2,18},{3,19},{4,20},{5,21},{6,22},{7,23},{8,24},{9,... | collective-permute-start | bytes 4718600 | tf_op jit(solution)/shard_map/ppermute | solution.py:22
  164.2 11.1 %collective-permute-start.9 = (f32[96,1024]{1,0:T(8,128)}, f32[96,1024]{1,0:T(8,128)S(1)}, u32[]{:S(2)}, u32[]{:S(2)}) collective-permute-start(f32[96,1024]{1,0:T(8,128)} %collective-permute-done.8), channel_id=1, source_target_pairs={{0,448},{1,449},{2,450},{3,451},{4,452},{5,453},{6,454},{7,455},{8... | collective-permute-start | bytes 1179656 | tf_op jit(solution)/shard_map/ppermute | solution.py:22
  168.9 1.0 copy-start.3
  169.9 4.0 %copy-start.7 = (f32[96,1024]{1,0:T(8,128)S(1)}, f32[96,1024]{1,0:T(8,128)}, u32[]{:S(2)}) copy-start(f32[96,1024]{1,0:T(8,128)} %copy-done.6) | copy-start | bytes 1179652
  172.0 14.2 %collective-permute-start.13 = (f32[192,1024]{1,0:T(8,128)}, f32[192,1024]{1,0:T(8,128)}, u32[]{:S(2)}, u32[]{:S(2)}) collective-permute-start(f32[192,1024]{1,0:T(8,128)} %pad_maximum_fusion), channel_id=1, source_target_pairs={{0,12},{1,13},{2,14},{3,15},{4,8},{5,9},{6,10},{7,11},{8,4},{9,5},... | collective-permute-start | bytes 2359304 | tf_op jit(solution)/shard_map/ppermute | solution.py:22
  175.3 17.7 %collective-permute-start.10 = (f32[384,1024]{1,0:T(8,128)S(1)}, f32[384,1024]{1,0:T(8,128)}, u32[]{:S(2)}, u32[]{:S(2)}) collective-permute-start(f32[384,1024]{1,0:T(8,128)S(1)} %constant_dynamic-update-slice_fusion.6), channel_id=1, source_target_pairs={{0,16},{1,17},{2,18},{3,19},{4,20},{5,21},{6,22},{7,23},{8,24},{9,... | collective-permute-start | bytes 4718600 | tf_op jit(solution)/shard_map/ppermute | solution.py:22
  180.2 1.4 copy-start.4
  193.0 1.7 copy-start.5
  198.1 2.3 copy-start.1
  223.6 14.7 %all-to-all-start.1 = ((f32[4,24,1024]{2,1,0:T(8,128)}), f32[4,24,1024]{2,1,0:T(8,128)S(1)}, u32[]{:S(2)}, u32[]{:S(2)}) async-start(f32[4,24,1024]{2,1,0:T(8,128)} %bitcast.2), calls=%async_computation.1 | async-start | bytes 786432 | tf_op jit(solution)/shard_map/all_to_all | solution.py:122
Sparse Core Ops, SparseCore 0:
  63.9 56.9 all-gather.1

commit v2 on v1

v2 whole, which is shorter than its diff:
```python
import jax
import jax.numpy as jnp
import numpy as np
from jax import lax
from jax.sharding import Mesh, PartitionSpec as P

step_length = 0.5
penalty = 0.02

PARTS = {"y": 8, "zh": 2, "c": 2, "x": 4, "zl": 4}
AXES = tuple(PARTS)
SIZES = tuple(PARTS.values())
PREC = lax.Precision.HIGH


def permute(v, move):
    count = int(np.prod(SIZES))
    pairs = []
    for k in range(count):
        at = [int(p) for p in np.unravel_index(k, SIZES)]
        pairs.append((k, int(np.ravel_multi_index(move(*at), SIZES))))
    return lax.ppermute(v, AXES, pairs)


def swap_core(v):
    return permute(v, lambda y, zh, c, x, zl: (y, zh, 1 - c, x, zl))


def swap_zh(v):
    return permute(v, lambda y, zh, c, x, zl: (y, 1 - zh, c, x, zl))


def data_target(y, zh, x, zl):
    return (2 * x + zl // 2 - y) % 8, zl % 2


def transpose_data(v):
    def move(y, zh, c, x, zl):
        row_y, row_zh = data_target(y, zh, x, zl)
        return (row_y, row_zh, c, y // 2, 2 * (y % 2) + zh)

    return permute(v, move)


def transpose_in_plane(v):
    def move(y, zh, c, x, zl):
        p = (y - c) % 8
        return (y, zl % 2, c, (p // 2 + x) % 4, 2 * (p % 2 ^ zl // 2) + zh)

    return permute(v, move)


def transpose_along_y(v):
    def move(y, zh, c, x, zl):
        p = (y - c) % 8
        return (2 * ((x - p // 2) % 4) + (p % 2 ^ zl // 2), zh, c, x, zl)

    return permute(v, move)


def pair_swap(v, axis, odd_step, flip=0):
    at = AXES.index(axis)
    n = PARTS[axis]

    def move(*place):
        place = list(place)
        parity = (place[at] - (place[2] ^ flip)) % 2
        step = 1 if parity == odd_step else -1
        place[at] = (place[at] + step) % n
        return tuple(place)

    return permute(v, move)


def take(v, start, size):
    return lax.dynamic_slice_in_dim(v, start, size, 0)


def put(v, part, start):
    return lax.dynamic_update_slice_in_dim(v, part, start, 0)


def in_pair(own, got, odd):
    return jnp.where(odd == 0, jnp.concatenate([own, got]), jnp.concatenate([got, own]))


def place_pairs(parts, k, odd):
    near = jnp.where(odd == 0, k + 1, k - 1)
    other = jnp.where(odd == 0, k - 1, k + 1)
    rows = parts[0].shape[0]
    out = jnp.zeros((4 * rows, *parts[0].shape[1:]), parts[0].dtype)
    for part, j in zip(parts, (k, other, near, k + 2)):
        out = put(out, part, (j % 4) * rows)
    return out


def scatter_sum(v, axis):
    n = PARTS[axis]
    parts = lax.all_to_all(v.reshape(n, -1, v.shape[1]), axis, 0, 0, tiled=True)
    return jnp.sum(parts, axis=0)


def both_cores(v, c):
    other = swap_core(v)
    out = jnp.zeros((2 * v.shape[0], *v.shape[1:]), v.dtype)
    return put(put(out, v, c * v.shape[0]), other, (1 - c) * v.shape[0])


def together(*parts):
    return lax.optimization_barrier(parts)


def dot(a, b, contract):
    return lax.dot_general(
        a, b, (contract, ((), ())), precision=PREC, preferred_element_type=jnp.float32
    )


def on_device(precision_matrix, sample_rows):
    row_count, col_count = precision_matrix.shape
    samples = sample_rows.shape[1]
    y, zh, c, x, zl = (lax.axis_index(a) for a in AXES)
    row_chip, col_chip = 2 * y + zh, 4 * x + zl
    half = col_count // 2
    block = half // 8
    place = (y - c) % 8
    pair, odd = place // 2, place % 2

    target, _ = data_target(y, zh, x, zl)
    share = take(sample_rows, target * block, block)

    def partial_rows(h):
        cols = lax.dynamic_slice_in_dim(precision_matrix, h * half, half, 1)
        return dot(cols, sample_rows, ((0,), (0,)))

    got = swap_core(partial_rows(1 - c))
    (kept,) = together(partial_rows(c))

    def sums(at):
        start = (at % 4) * (2 * block)
        return take(kept, start, 2 * block) + take(got, start, 2 * block)

    near = jnp.where(odd == 0, pair + 1, pair - 1)
    other = jnp.where(odd == 0, pair - 1, pair + 1)
    sending, share = together(sums(pair + 2), share)
    passed = pair_swap(sending, "y", 1)
    data = transpose_data(share)
    passed = pair_swap(sums(near) + passed, "y", 0)
    sending, data = together(sums(other) + passed, data)
    data_half = lax.all_gather(data, "y", axis=0, tiled=True)
    passed = pair_swap(sending, "y", 1)
    mine = sums(pair) + passed
    passed = pair_swap(take(mine, (1 - odd) * block, block), "y", 0)
    product = take(mine, odd * block, block) + passed
    product = product + swap_zh(product)

    own = take(product, zh * (block // 2), block // 2)
    product, own = together(product, own)
    own = transpose_in_plane(own)
    pair0 = in_pair(product, pair_swap(product, "y", 0), odd)
    pair0, own = together(pair0, own)
    own = transpose_along_y(own)
    pair1 = pair_swap(pair0, "y", 1)
    pair1, own = together(pair1, own)
    pair2 = pair_swap(pair1, "y", 0)
    own = lax.all_gather(own, "zl", axis=0, tiled=True)
    own = in_pair(own[:block], own[block:], row_chip // 2 % 2)
    pair2, own, data_half = together(pair2, own, data_half)
    pair3 = pair_swap(pair2, "y", 1)
    x_odd = (x - c) % 2
    rows0 = in_pair(own, pair_swap(own, "x", 0), x_odd)
    data_cols = both_cores(data_half, c)
    pair3, rows0 = together(pair3, rows0)
    rows1 = pair_swap(rows0, "x", 1)
    product_cols = both_cores(place_pairs([pair0, pair1, pair2, pair3], pair, odd), c)
    product_rows = jnp.zeros_like(sample_rows)
    first = x - x_odd - row_chip // 4
    for part, at in (
        (rows0[: 2 * block], first),
        (rows0[2 * block :], first + 1),
        (rows1[: 2 * block], first + 2),
        (rows1[2 * block :], first + 3),
    ):
        product_rows = put(product_rows, part, (at % 4) * (2 * block))

    last = ((1,), (1,))
    cross = dot(sample_rows, product_cols, last) + dot(product_rows, data_cols, last)
    gradient = cross * (0.5 / samples)

    global_rows = (2 * row_chip + c) * row_count + lax.broadcasted_iota(
        jnp.int32, (row_count, col_count), 0
    )
    global_cols = col_chip * col_count + lax.broadcasted_iota(
        jnp.int32, (row_count, col_count), 1
    )
    on_diagonal = global_rows == global_cols
    inverse = 1.0 / jnp.where(on_diagonal, precision_matrix, 1.0)
    gradient = gradient - jnp.where(on_diagonal, inverse, 0.0)
    moved = precision_matrix - step_length * gradient
    shrunk = jnp.sign(moved) * jnp.maximum(jnp.abs(moved) - step_length * penalty, 0.0)
    updated = jnp.where(on_diagonal, moved, shrunk)
    next_partial = dot(updated, data_cols, ((1,), (0,)))
    next_product = scatter_sum(scatter_sum(next_partial, "x"), "zl")
    return updated, next_product


def solution(mesh):
    parts = Mesh(mesh.devices.reshape(SIZES), AXES)
    row, col = ("y", "zh", "c"), ("x", "zl")
    return jax.shard_map(
        on_device,
        mesh=parts,
        in_specs=(P(row, col), P(row, None)),
        out_specs=(P(row, col), P(row + col, None)),
        check_vma=False,
    )
```

time: 247 us -> 223 us (0.903)
  the two profiles are of different devices: /device:TPU:2 before, /device:TPU:24 now
where the time goes in v2:
time: 223 us; the launch traced here: 222 us
  starting transfers between devices  76.2 us (34%)
  waiting for transfers between devices  63 us (28%)
  blocking collectives  36.3 us (16%)
  between operations  14.9 us (7%)
  matrix products  14.5 us (7%)
  local copies, waits for them, and re-layouts  9.4 us (4%)
  other arithmetic  7.69 us (3%)
    ppermute x17, starting transfers between devices, permute(): return lax.ppermute(v, AXES, pairs)  70.9 us
    ppermute x17, waiting for transfers between devices, permute(): return lax.ppermute(v, AXES, pairs)  56.7 us
    all_to_all x1, blocking collectives, scatter_sum(): parts = lax.all_to_all(v.reshape(n, -1, v.shape[1]), axis, 0, 0, tiled=True)  20.4 us
    all_gather x1, blocking collectives, on_device(): own = lax.all_gather(own, 'zl', axis=0, tiled=True)  15.9 us
    dot_general x5, matrix products, dot(): lax.dot_general(a, b, (contract, ((), ())), precision=PREC, preferred_ele...  14.5 us
    unnamed x12, local copies, waits for them, and re-layouts  6.47 us
    all_to_all x1, waiting for transfers between devices, scatter_sum(): parts = lax.all_to_all(v.reshape(n, -1, v.shape[1]), axis, 0, 0, tiled=True)  6.23 us
    all_to_all x1, starting transfers between devices, scatter_sum(): parts = lax.all_to_all(v.reshape(n, -1, v.shape[1]), axis, 0, 0, tiled=True)  5.28 us
  transfers between devices with their start and end apart: 19, of which 13 were waited for; matrix products, arithmetic and copies ran while one was open for 7% of the time, Pallas kernels for 0%

profile of v2, /device:TPU:24, one launch (start us, length us, event | category | flops | bytes accessed | tf_op | source)
XLA Modules:
  0.0 221.9 jit_solution(5890316501615311535)
XLA Ops:
  8.6 3.7 %fusion.6 = f32[384,1024]{1,0:T(8,128)} fusion(f32[384,1024]{1,0:T(8,128)S(1)} %copy-done, f32[384,768]{1,0:T(8,128)} %param.2, s32[]{:T(128)S(6)} %select_n.178), kind=kOutput, calls=%fused_computation.11 | convolution fusion | flops 905969664 | bytes 3735556 | tf_op jit(solution)/shard_map/dot_general | solution.py:114
  14.3 2.5 %fusion.8 = f32[384,1024]{1,0:T(8,128)S(1)} fusion(f32[384,1024]{1,0:T(8,128)S(1)} %copy-done, f32[384,768]{1,0:T(8,128)} %param.2, s32[]{:T(128)S(6)} %select_n.174), kind=kOutput, calls=%fused_computation.13 | convolution fusion | flops 905969664 | bytes 3735556 | tf_op jit(solution)/shard_map/dot_general | solution.py:114
  19.7 4.7 %collective-permute-start.1 = (f32[96,1024]{1,0:T(8,128)}, f32[96,1024]{1,0:T(8,128)S(1)}, u32[]{:S(2)}, u32[]{:S(2)}) collective-permute-start(f32[96,1024]{1,0:T(8,128)} %dynamic-slice_add_fusion), channel_id=1, source_target_pairs={{0,448},{1,449},{2,450},{3,451},{4,452},{5,453},{6,454},{7,455},{8... | collective-permute-start | bytes 1179656 | tf_op jit(solution)/shard_map/ppermute | solution.py:22
  24.4 6.3 %collective-permute-done.1 = f32[96,1024]{1,0:T(8,128)S(1)} collective-permute-done((f32[96,1024]{1,0:T(8,128)}, f32[96,1024]{1,0:T(8,128)S(1)}, u32[]{:S(2)}, u32[]{:S(2)}) %collective-permute-start.1) | collective-permute-done | bytes 393248 | tf_op jit(solution)/shard_map/ppermute | solution.py:22
  34.5 10.7 %collective-permute-start.3 = (f32[48,1024]{1,0:T(8,128)}, f32[48,1024]{1,0:T(8,128)}, u32[]{:S(2)}, u32[]{:S(2)}) collective-permute-start(f32[48,1024]{1,0:T(8,128)} %constant_dynamic-slice_fusion.2), channel_id=1, source_target_pairs={{0,0},{1,32},{2,64},{3,96},{4,128},{5,160},{6,192},{7,224},{8,256}... | collective-permute-start | bytes 589832 | tf_op jit(solution)/shard_map/ppermute | solution.py:22
  46.4 3.9 %collective-permute-done.3 = f32[48,1024]{1,0:T(8,128)} collective-permute-done((f32[48,1024]{1,0:T(8,128)}, f32[48,1024]{1,0:T(8,128)}, u32[]{:S(2)}, u32[]{:S(2)}) %collective-permute-start.3) | collective-permute-done | bytes 196640 | tf_op jit(solution)/shard_map/ppermute | solution.py:22
  50.3 3.3 %collective-permute-start.4 = (f32[96,1024]{1,0:T(8,128)S(1)}, f32[96,1024]{1,0:T(8,128)}, u32[]{:S(2)}, u32[]{:S(2)}) collective-permute-start(f32[96,1024]{1,0:T(8,128)S(1)} %add_add_fusion.1), channel_id=1, source_target_pairs={{0,448},{1,449},{2,450},{3,451},{4,452},{5,453},{6,454},{7,455},{8... | collective-permute-start | bytes 1179656 | tf_op jit(solution)/shard_map/ppermute | solution.py:22
  53.6 7.7 %collective-permute-done.4 = f32[96,1024]{1,0:T(8,128)} collective-permute-done((f32[96,1024]{1,0:T(8,128)S(1)}, f32[96,1024]{1,0:T(8,128)}, u32[]{:S(2)}, u32[]{:S(2)}) %collective-permute-start.4) | collective-permute-done | bytes 393248 | tf_op jit(solution)/shard_map/ppermute | solution.py:22
  62.5 4.7 %collective-permute-start.5 = (f32[48,1024]{1,0:T(8,128)S(1)}, f32[48,1024]{1,0:T(8,128)S(1)}, u32[]{:S(2)}, u32[]{:S(2)}) collective-permute-start(f32[48,1024]{1,0:T(8,128)S(1)} %constant_dynamic-slice_fusion.1), channel_id=1, source_target_pairs={{0,64},{1,65},{2,66},{3,67},{4,68},{5,69},{6,70},{7,71},{8,72},{9,... | collective-permute-start | bytes 589832 | tf_op jit(solution)/shard_map/ppermute | solution.py:22
  67.3 3.6 %collective-permute-done.5 = f32[48,1024]{1,0:T(8,128)S(1)} collective-permute-done((f32[48,1024]{1,0:T(8,128)S(1)}, f32[48,1024]{1,0:T(8,128)S(1)}, u32[]{:S(2)}, u32[]{:S(2)}) %collective-permute-start.5) | collective-permute-done | bytes 196640 | tf_op jit(solution)/shard_map/ppermute | solution.py:22
  70.9 16.5 %collective-permute-start.6 = (f32[48,1024]{1,0:T(8,128)S(1)}, f32[48,1024]{1,0:T(8,128)S(1)}, u32[]{:S(2)}, u32[]{:S(2)}) collective-permute-start(f32[48,1024]{1,0:T(8,128)S(1)} %dynamic-slice_add_fusion.1), channel_id=1, source_target_pairs={{0,32},{1,33},{2,34},{3,35},{4,36},{5,37},{6,38},{7,39},{8,40},{9,... | collective-permute-start | bytes 589832 | tf_op jit(solution)/shard_map/ppermute | solution.py:22
  87.4 6.8 %collective-permute-done.6 = f32[48,1024]{1,0:T(8,128)S(1)} collective-permute-done((f32[48,1024]{1,0:T(8,128)S(1)}, f32[48,1024]{1,0:T(8,128)S(1)}, u32[]{:S(2)}, u32[]{:S(2)}) %collective-permute-start.6) | collective-permute-done | bytes 196640 | tf_op jit(solution)/shard_map/ppermute | solution.py:22
  96.2 2.0 collective-permute-start.8
  98.2 4.4 %collective-permute-done.7 = f32[48,1024]{1,0:T(8,128)S(1)} collective-permute-done((f32[48,1024]{1,0:T(8,128)S(1)}, f32[48,1024]{1,0:T(8,128)S(1)}, u32[]{:S(2)}, u32[]{:S(2)}) %collective-permute-start.7) | collective-permute-done | bytes 196640 | tf_op jit(solution)/shard_map/ppermute | solution.py:22
  102.6 3.2 %collective-permute-done.8 = f32[24,1024]{1,0:T(8,128)} collective-permute-done((f32[24,1024]{1,0:T(8,128)S(1)}, f32[24,1024]{1,0:T(8,128)}, u32[]{:S(2)}, u32[]{:S(2)}) %collective-permute-start.8) | collective-permute-done | bytes 98336 | tf_op jit(solution)/shard_map/ppermute | solution.py:22
  105.8 3.6 %collective-permute-start.9 = (f32[96,1024]{1,0:T(8,128)S(1)}, f32[96,1024]{1,0:T(8,128)S(1)}, u32[]{:S(2)}, u32[]{:S(2)}) collective-permute-start(f32[96,1024]{1,0:T(8,128)S(1)} %maximum_select_fusion.1), channel_id=1, source_target_pairs={{0,448},{1,449},{2,450},{3,451},{4,452},{5,453},{6,454},{7,455},{8... | collective-permute-start | bytes 1179656 | tf_op jit(solution)/shard_map/ppermute | solution.py:22
  113.0 8.8 %collective-permute-done.10 = f32[24,1024]{1,0:T(8,128)S(1)} collective-permute-done((f32[24,1024]{1,0:T(8,128)}, f32[24,1024]{1,0:T(8,128)S(1)}, u32[]{:S(2)}, u32[]{:S(2)}) %collective-permute-start.10) | collective-permute-done | bytes 98336 | tf_op jit(solution)/shard_map/ppermute | solution.py:22
  121.8 2.2 collective-permute-start.11
  124.0 15.9 %all_gather.6 = f32[96,1024]{1,0:T(8,128)S(1)} all-gather(f32[24,1024]{1,0:T(8,128)S(1)} %collective-permute-done.10), channel_id=1, replica_groups=mesh['y'=8,'zh'=2,'c'=2,'x'=4,'zl'=4] {'zl'}, dimensions={0}, use_global_device_ids=true | all-gather | bytes 491520 | tf_op jit(solution)/shard_map/all_gather | solution.py:166
  140.0 2.8 %collective-permute-start.13 = (f32[96,1024]{1,0:T(8,128)S(1)}, f32[96,1024]{1,0:T(8,128)S(1)}, u32[]{:S(2)}, u32[]{:S(2)}) collective-permute-start(f32[96,1024]{1,0:T(8,128)S(1)} %maximum_select_fusion.2), channel_id=1, source_target_pairs={{0,4},{1,5},{2,6},{3,7},{4,0},{5,1},{6,2},{7,3},{8,12},{9,13},{10,... | collective-permute-start | bytes 1179656 | tf_op jit(solution)/shard_map/ppermute | solution.py:22
  143.0 3.7 %collective-permute-start.12 = (f32[96,1024]{1,0:T(8,128)S(1)}, f32[96,1024]{1,0:T(8,128)S(1)}, u32[]{:S(2)}, u32[]{:S(2)}) collective-permute-start(f32[96,1024]{1,0:T(8,128)S(1)} %collective-permute-done.11), channel_id=1, source_target_pairs={{0,448},{1,449},{2,450},{3,451},{4,452},{5,453},{6,454},{7,455},{8... | collective-permute-start | bytes 1179656 | tf_op jit(solution)/shard_map/ppermute | solution.py:22
  149.8 4.1 %collective-permute-done.12 = f32[96,1024]{1,0:T(8,128)S(1)} collective-permute-done((f32[96,1024]{1,0:T(8,128)S(1)}, f32[96,1024]{1,0:T(8,128)S(1)}, u32[]{:S(2)}, u32[]{:S(2)}) %collective-permute-start.12) | collective-permute-done | bytes 393248 | tf_op jit(solution)/shard_map/ppermute | solution.py:22
  153.9 5.0 %collective-permute-start.15 = (f32[192,1024]{1,0:T(8,128)S(1)}, f32[192,1024]{1,0:T(8,128)S(1)}, u32[]{:S(2)}, u32[]{:S(2)}) collective-permute-start(f32[192,1024]{1,0:T(8,128)S(1)} %maximum_select_fusion), channel_id=1, source_target_pairs={{0,12},{1,13},{2,14},{3,15},{4,8},{5,9},{6,10},{7,11},{8,4},{9,5},... | collective-permute-start | bytes 2359304 | tf_op jit(solution)/shard_map/ppermute | solution.py:22
  159.0 2.1 collective-permute-start.14
  162.0 7.0 %collective-permute-done.15 = f32[192,1024]{1,0:T(8,128)S(1)} collective-permute-done((f32[192,1024]{1,0:T(8,128)S(1)}, f32[192,1024]{1,0:T(8,128)S(1)}, u32[]{:S(2)}, u32[]{:S(2)}) %collective-permute-start.15) | collective-permute-done | bytes 786464 | tf_op jit(solution)/shard_map/ppermute | solution.py:22
  169.3 2.7 %fusion.13 = f32[384,768]{0,1:T(8,128)S(1)} fusion(f32[384,1024]{1,0:T(8,128)S(1)} %slice_dynamic-update-slice_fusion, f32[768,1024]{1,0:T(8,128)S(1)} %constant_dynamic-update-slice_fusion.6), kind=kOutput, calls=%fused_computation.42 | convolution fusion | flops 1811939328 | bytes 5898240 | tf_op jit(solution)/shard_map/dot_general | solution.py:114
  173.3 3.3 %compare_select_fusion = f32[384,768]{0,1:T(8,128)S(1)} fusion(f32[384,768]{0,1:T(8,128)S(1)} %copy-done.4, f32[384,768]{0,1:T(8,128)S(1)} %fusion.13, f32[768,1024]{1,0:T(8,128)S(1)} %constant_dynamic-update-slice_fusion, f32[384,1024]{1,0:T(8,128)S(1)} %copy-done, s32[384]{0:T(512)S(1)} %iota_add_fusion.1, s32[768]{0:T(1024)S(1)} %iota_add_fusion), kind=kOutput, calls=%fused_computation | convolution fusion | flops 1816363008 | bytes 8262144 | tf_op jit(solution)/shard_map/dot_general | solution.py:114
  176.6 2.3 %fusion.14 = f32[384,1024]{1,0:T(8,128)S(1)} fusion(f32[384,768]{0,1:T(8,128)S(1)} %compare_select_fusion, f32[768,1024]{1,0:T(8,128)S(1)} %constant_dynamic-update-slice_fusion.6), kind=kOutput, calls=%fused_computation.43 | convolution fusion | flops 1811939328 | bytes 5898240 | tf_op jit(solution)/shard_map/dot_general | solution.py:114
  179.0 20.4 %all_to_all.10 = f32[4,96,1024]{2,1,0:T(8,128)S(1)} all-to-all(f32[4,96,1024]{2,1,0:T(8,128)S(1)} %bitcast.24), channel_id=1, replica_groups=mesh['y'=8,'zh'=2,'c'=2,'x'=4,'zl'=4] {'x'}, dimensions={0} | all-to-all | bytes 3145728 | tf_op jit(solution)/shard_map/all_to_all | solution.py:99
  200.3 5.3 %all-to-all-start.1 = ((f32[4,24,1024]{2,1,0:T(8,128)}), f32[4,24,1024]{2,1,0:T(8,128)S(1)}, u32[]{:S(2)}, u32[]{:S(2)}) async-start(f32[4,24,1024]{2,1,0:T(8,128)} %bitcast.2), calls=%async_computation.1 | async-start | bytes 786432 | tf_op jit(solution)/shard_map/all_to_all | solution.py:99
  205.5 2.7 %copy.11 = f32[384,768]{1,0:T(8,128)} copy(f32[384,768]{0,1:T(8,128)} %copy-done.2) | data formatting | bytes 2359296
  208.2 6.2 %all-to-all-done.1 = f32[4,24,1024]{2,1,0:T(8,128)S(1)} async-done(((f32[4,24,1024]{2,1,0:T(8,128)}), f32[4,24,1024]{2,1,0:T(8,128)S(1)}, u32[]{:S(2)}, u32[]{:S(2)}) %all-to-all-start.1) | async-done | bytes 393248 | tf_op jit(solution)/shard_map/all_to_all | solution.py:99
  (59 shorter events, 24.9 us)
Async XLA Ops:
  7.2 1.4 copy-start
  7.2 132.8 %all-gather.2.cloned.1.call-start = ((), (), s32[]{:S(2)}) async-start(), calls=%async_computation.2 | async-start | bytes 1769472 | tf_op jit(solution)/shard_map/all_gather | solution.py:150
  12.2 5.6 %collective-permute-start = (f32[384,1024]{1,0:T(8,128)}, f32[384,1024]{1,0:T(8,128)}, u32[]{:S(2)}, u32[]{:S(2)}) collective-permute-start(f32[384,1024]{1,0:T(8,128)} %fusion.6), channel_id=1, source_target_pairs={{0,16},{1,17},{2,18},{3,19},{4,20},{5,21},{6,22},{7,23},{8,24},{9,... | collective-permute-start | bytes 4718600 | tf_op jit(solution)/shard_map/ppermute | solution.py:22
  19.7 11.1 %collective-permute-start.1 = (f32[96,1024]{1,0:T(8,128)}, f32[96,1024]{1,0:T(8,128)S(1)}, u32[]{:S(2)}, u32[]{:S(2)}) collective-permute-start(f32[96,1024]{1,0:T(8,128)} %dynamic-slice_add_fusion), channel_id=1, source_target_pairs={{0,448},{1,449},{2,450},{3,451},{4,452},{5,453},{6,454},{7,455},{8... | collective-permute-start | bytes 1179656 | tf_op jit(solution)/shard_map/ppermute | solution.py:22
  32.5 12.6 %collective-permute-start.2 = (f32[96,1024]{1,0:T(8,128)}, f32[96,1024]{1,0:T(8,128)}, u32[]{:S(2)}, u32[]{:S(2)}) collective-permute-start(f32[96,1024]{1,0:T(8,128)} %add_add_fusion), channel_id=1, source_target_pairs={{0,64},{1,65},{2,66},{3,67},{4,68},{5,69},{6,70},{7,71},{8,72},{9,... | collective-permute-start | bytes 1179656 | tf_op jit(solution)/shard_map/ppermute | solution.py:22
  34.5 15.8 %collective-permute-start.3 = (f32[48,1024]{1,0:T(8,128)}, f32[48,1024]{1,0:T(8,128)}, u32[]{:S(2)}, u32[]{:S(2)}) collective-permute-start(f32[48,1024]{1,0:T(8,128)} %constant_dynamic-slice_fusion.2), channel_id=1, source_target_pairs={{0,0},{1,32},{2,64},{3,96},{4,128},{5,160},{6,192},{7,224},{8,256}... | collective-permute-start | bytes 589832 | tf_op jit(solution)/shard_map/ppermute | solution.py:22
  50.3 11.0 %collective-permute-start.4 = (f32[96,1024]{1,0:T(8,128)S(1)}, f32[96,1024]{1,0:T(8,128)}, u32[]{:S(2)}, u32[]{:S(2)}) collective-permute-start(f32[96,1024]{1,0:T(8,128)S(1)} %add_add_fusion.1), channel_id=1, source_target_pairs={{0,448},{1,449},{2,450},{3,451},{4,452},{5,453},{6,454},{7,455},{8... | collective-permute-start | bytes 1179656 | tf_op jit(solution)/shard_map/ppermute | solution.py:22
  62.5 47.2 %copy-start.1 = (f32[384,768]{1,0:T(8,128)S(1)}, f32[384,768]{1,0:T(8,128)}, u32[]{:S(2)}) copy-start(f32[384,768]{1,0:T(8,128)} %param.2) | copy-start | bytes 3538948
  62.5 8.4 %collective-permute-start.5 = (f32[48,1024]{1,0:T(8,128)S(1)}, f32[48,1024]{1,0:T(8,128)S(1)}, u32[]{:S(2)}, u32[]{:S(2)}) collective-permute-start(f32[48,1024]{1,0:T(8,128)S(1)} %constant_dynamic-slice_fusion.1), channel_id=1, source_target_pairs={{0,64},{1,65},{2,66},{3,67},{4,68},{5,69},{6,70},{7,71},{8,72},{9,... | collective-permute-start | bytes 589832 | tf_op jit(solution)/shard_map/ppermute | solution.py:22
  70.9 23.3 %collective-permute-start.6 = (f32[48,1024]{1,0:T(8,128)S(1)}, f32[48,1024]{1,0:T(8,128)S(1)}, u32[]{:S(2)}, u32[]{:S(2)}) collective-permute-start(f32[48,1024]{1,0:T(8,128)S(1)} %dynamic-slice_add_fusion.1), channel_id=1, source_target_pairs={{0,32},{1,33},{2,34},{3,35},{4,36},{5,37},{6,38},{7,39},{8,40},{9,... | collective-permute-start | bytes 589832 | tf_op jit(solution)/shard_map/ppermute | solution.py:22
  94.3 8.3 %collective-permute-start.7 = (f32[48,1024]{1,0:T(8,128)S(1)}, f32[48,1024]{1,0:T(8,128)S(1)}, u32[]{:S(2)}, u32[]{:S(2)}) collective-permute-start(f32[48,1024]{1,0:T(8,128)S(1)} %add.213), channel_id=1, source_target_pairs={{0,64},{1,65},{2,66},{3,67},{4,68},{5,69},{6,70},{7,71},{8,72},{9,... | collective-permute-start | bytes 589832 | tf_op jit(solution)/shard_map/ppermute | solution.py:22
  96.2 9.6 %collective-permute-start.8 = (f32[24,1024]{1,0:T(8,128)S(1)}, f32[24,1024]{1,0:T(8,128)}, u32[]{:S(2)}, u32[]{:S(2)}) collective-permute-start(f32[24,1024]{1,0:T(8,128)S(1)} %constant_dynamic-slice_fusion), channel_id=1, source_target_pairs={{0,0},{1,32},{2,2},{3,34},{4,4},{5,36},{6,6},{7,38},{8,8},{9,40},{... | collective-permute-start | bytes 294920 | tf_op jit(solution)/shard_map/ppermute | solution.py:22
  105.8 16.0 %collective-permute-start.9 = (f32[96,1024]{1,0:T(8,128)S(1)}, f32[96,1024]{1,0:T(8,128)S(1)}, u32[]{:S(2)}, u32[]{:S(2)}) collective-permute-start(f32[96,1024]{1,0:T(8,128)S(1)} %maximum_select_fusion.1), channel_id=1, source_target_pairs={{0,448},{1,449},{2,450},{3,451},{4,452},{5,453},{6,454},{7,455},{8... | collective-permute-start | bytes 1179656 | tf_op jit(solution)/shard_map/ppermute | solution.py:22
  111.0 10.8 %collective-permute-start.10 = (f32[24,1024]{1,0:T(8,128)}, f32[24,1024]{1,0:T(8,128)S(1)}, u32[]{:S(2)}, u32[]{:S(2)}) collective-permute-start(f32[24,1024]{1,0:T(8,128)} %collective-permute-done.8), channel_id=1, source_target_pairs={{0,0},{1,1},{2,66},{3,67},{4,132},{5,133},{6,198},{7,199},{8,264},... | collective-permute-start | bytes 294920 | tf_op jit(solution)/shard_map/ppermute | solution.py:22
  121.8 18.1 %collective-permute-start.11 = (f32[96,1024]{1,0:T(8,128)S(1)}, f32[96,1024]{1,0:T(8,128)S(1)}, u32[]{:S(2)}, u32[]{:S(2)}) collective-permute-start(f32[96,1024]{1,0:T(8,128)S(1)} %collective-permute-done.9), channel_id=1, source_target_pairs={{0,64},{1,65},{2,66},{3,67},{4,68},{5,69},{6,70},{7,71},{8,72},{9,... | collective-permute-start | bytes 1179656 | tf_op jit(solution)/shard_map/ppermute | solution.py:22
  140.0 6.8 %copy-start.3 = (f32[384,1024]{1,0:T(8,128)S(1)}, f32[384,1024]{1,0:T(8,128)}, u32[]{:S(2)}) copy-start(f32[384,1024]{1,0:T(8,128)} %all-gather.2.cloned.1.call-done) | copy-start | bytes 4718596
  140.0 9.8 %collective-permute-start.13 = (f32[96,1024]{1,0:T(8,128)S(1)}, f32[96,1024]{1,0:T(8,128)S(1)}, u32[]{:S(2)}, u32[]{:S(2)}) collective-permute-start(f32[96,1024]{1,0:T(8,128)S(1)} %maximum_select_fusion.2), channel_id=1, source_target_pairs={{0,4},{1,5},{2,6},{3,7},{4,0},{5,1},{6,2},{7,3},{8,12},{9,13},{10,... | collective-permute-start | bytes 1179656 | tf_op jit(solution)/shard_map/ppermute | solution.py:22
  143.0 10.9 %collective-permute-start.12 = (f32[96,1024]{1,0:T(8,128)S(1)}, f32[96,1024]{1,0:T(8,128)S(1)}, u32[]{:S(2)}, u32[]{:S(2)}) collective-permute-start(f32[96,1024]{1,0:T(8,128)S(1)} %collective-permute-done.11), channel_id=1, source_target_pairs={{0,448},{1,449},{2,450},{3,451},{4,452},{5,453},{6,454},{7,455},{8... | collective-permute-start | bytes 1179656 | tf_op jit(solution)/shard_map/ppermute | solution.py:22
  146.8 22.3 %collective-permute-start.16 = (f32[384,1024]{1,0:T(8,128)S(1)}, f32[384,1024]{1,0:T(8,128)S(1)}, u32[]{:S(2)}, u32[]{:S(2)}) collective-permute-start(f32[384,1024]{1,0:T(8,128)S(1)} %copy-done.3), channel_id=1, source_target_pairs={{0,16},{1,17},{2,18},{3,19},{4,20},{5,21},{6,22},{7,23},{8,24},{9,... | collective-permute-start | bytes 4718600 | tf_op jit(solution)/shard_map/ppermute | solution.py:22
  153.9 15.1 %collective-permute-start.15 = (f32[192,1024]{1,0:T(8,128)S(1)}, f32[192,1024]{1,0:T(8,128)S(1)}, u32[]{:S(2)}, u32[]{:S(2)}) collective-permute-start(f32[192,1024]{1,0:T(8,128)S(1)} %maximum_select_fusion), channel_id=1, source_target_pairs={{0,12},{1,13},{2,14},{3,15},{4,8},{5,9},{6,10},{7,11},{8,4},{9,5},... | collective-permute-start | bytes 2359304 | tf_op jit(solution)/shard_map/ppermute | solution.py:22
  159.0 13.0 %collective-permute-start.14 = (f32[384,1024]{1,0:T(8,128)S(1)}, f32[384,1024]{1,0:T(8,128)S(1)}, u32[]{:S(2)}, u32[]{:S(2)}) collective-permute-start(f32[384,1024]{1,0:T(8,128)S(1)} %constant_dynamic-update-slice_fusion.2), channel_id=1, source_target_pairs={{0,16},{1,17},{2,18},{3,19},{4,20},{5,21},{6,22},{7,23},{8,24},{9,... | collective-permute-start | bytes 4718600 | tf_op jit(solution)/shard_map/ppermute | solution.py:22
  172.0 1.3 copy-start.4
  176.6 2.3 %copy-start.2 = (f32[384,768]{0,1:T(8,128)}, f32[384,768]{0,1:T(8,128)S(1)}, u32[]{:S(2)}) copy-start(f32[384,768]{0,1:T(8,128)S(1)} %compare_select_fusion) | copy-start | bytes 3538948
  200.3 14.2 %all-to-all-start.1 = ((f32[4,24,1024]{2,1,0:T(8,128)}), f32[4,24,1024]{2,1,0:T(8,128)S(1)}, u32[]{:S(2)}, u32[]{:S(2)}) async-start(f32[4,24,1024]{2,1,0:T(8,128)} %bitcast.2), calls=%async_computation.1 | async-start | bytes 786432 | tf_op jit(solution)/shard_map/all_to_all | solution.py:99
Sparse Core Ops, SparseCore 0:
  53.7 50.5 all-gather.1

commit v3 on v2

--- a/solution.py
+++ b/solution.py
@@ -84,16 +84,6 @@
     return jnp.where(odd == 0, jnp.concatenate([own, got]), jnp.concatenate([got, own]))
 
 
-def place_pairs(parts, k, odd):
-    near = jnp.where(odd == 0, k + 1, k - 1)
-    other = jnp.where(odd == 0, k - 1, k + 1)
-    rows = parts[0].shape[0]
-    out = jnp.zeros((4 * rows, *parts[0].shape[1:]), parts[0].dtype)
-    for part, j in zip(parts, (k, other, near, k + 2)):
-        out = put(out, part, (j % 4) * rows)
-    return out
-
-
 def scatter_sum(v, axis):
     n = PARTS[axis]
     parts = lax.all_to_all(v.reshape(n, -1, v.shape[1]), axis, 0, 0, tiled=True)
@@ -155,24 +145,17 @@
     product = product + swap_zh(product)
 
     own = take(product, zh * (block // 2), block // 2)
-    product, own = together(product, own)
-    own = transpose_in_plane(own)
-    pair0 = in_pair(product, pair_swap(product, "y", 0), odd)
-    pair0, own = together(pair0, own)
-    own = transpose_along_y(own)
-    pair1 = pair_swap(pair0, "y", 1)
-    pair1, own = together(pair1, own)
-    pair2 = pair_swap(pair1, "y", 0)
+    product_half = lax.all_gather(product, "y", axis=0, tiled=True)
+    own = transpose_along_y(transpose_in_plane(own))
     own = lax.all_gather(own, "zl", axis=0, tiled=True)
     own = in_pair(own[:block], own[block:], row_chip // 2 % 2)
-    pair2, own, data_half = together(pair2, own, data_half)
-    pair3 = pair_swap(pair2, "y", 1)
+    own, data_half = together(own, data_half)
     x_odd = (x - c) % 2
     rows0 = in_pair(own, pair_swap(own, "x", 0), x_odd)
     data_cols = both_cores(data_half, c)
-    pair3, rows0 = together(pair3, rows0)
     rows1 = pair_swap(rows0, "x", 1)
-    product_cols = both_cores(place_pairs([pair0, pair1, pair2, pair3], pair, odd), c)
+    shifted = jnp.concatenate([product_half[block:], product_half[:block]])
+    product_cols = both_cores(jnp.where(c == 0, product_half, shifted), c)
     product_rows = jnp.zeros_like(sample_rows)
     first = x - x_odd - row_chip // 4
     for part, at in (

time: 223 us -> 213 us (0.955)
  the two profiles are of different devices: /device:TPU:24 before, /device:TPU:40 now
where the time goes in v3:
time: 213 us; the launch traced here: 212 us
  starting transfers between devices  68.8 us (32%)
  waiting for transfers between devices  49.7 us (23%)
  blocking collectives  43.8 us (21%)
  between operations  14.8 us (7%)
  matrix products  14.5 us (7%)
  local copies, waits for them, and re-layouts  12.6 us (6%)
  other arithmetic  7.49 us (4%)
    ppermute x13, starting transfers between devices, permute(): return lax.ppermute(v, AXES, pairs)  63.4 us
    ppermute x13, waiting for transfers between devices, permute(): return lax.ppermute(v, AXES, pairs)  43.4 us
    all_gather x1, blocking collectives, on_device(): own = lax.all_gather(own, 'zl', axis=0, tiled=True)  22.5 us
    all_to_all x1, blocking collectives, scatter_sum(): parts = lax.all_to_all(v.reshape(n, -1, v.shape[1]), axis, 0, 0, tiled=True)  21.3 us
    dot_general x5, matrix products, dot(): lax.dot_general(a, b, (contract, ((), ())), precision=PREC, preferred_ele...  14.5 us
    unnamed x14, local copies, waits for them, and re-layouts  7.53 us
    all_to_all x1, waiting for transfers between devices, scatter_sum(): parts = lax.all_to_all(v.reshape(n, -1, v.shape[1]), axis, 0, 0, tiled=True)  6.23 us
    all_to_all x1, starting transfers between devices, scatter_sum(): parts = lax.all_to_all(v.reshape(n, -1, v.shape[1]), axis, 0, 0, tiled=True)  5.29 us
  transfers between devices with their start and end apart: 16, of which 10 were waited for; matrix products, arithmetic and copies ran while one was open for 8% of the time, Pallas kernels for 0%

profile of v3, /device:TPU:40, one launch (start us, length us, event | category | flops | bytes accessed | tf_op | source)
XLA Modules:
  0.0 211.7 jit_solution(8631998164327673693)
XLA Ops:
  8.6 3.7 %fusion.6 = f32[384,1024]{1,0:T(8,128)} fusion(f32[384,1024]{1,0:T(8,128)S(1)} %copy-done, f32[384,768]{1,0:T(8,128)} %param.2, s32[]{:T(128)S(6)} %select_n.165), kind=kOutput, calls=%fused_computation.12 | convolution fusion | flops 905969664 | bytes 3735556 | tf_op jit(solution)/shard_map/dot_general | solution.py:104
  12.3 1.9 collective-permute-start
  14.3 2.5 %fusion.8 = f32[384,1024]{1,0:T(8,128)S(1)} fusion(f32[384,1024]{1,0:T(8,128)S(1)} %copy-done, f32[384,768]{1,0:T(8,128)} %param.2, s32[]{:T(128)S(6)} %select_n.160), kind=kOutput, calls=%fused_computation.14 | convolution fusion | flops 905969664 | bytes 3735556 | tf_op jit(solution)/shard_map/dot_general | solution.py:104
  19.0 2.6 %collective-permute-start.1 = (f32[96,1024]{1,0:T(8,128)S(1)}, f32[96,1024]{1,0:T(8,128)}, u32[]{:S(2)}, u32[]{:S(2)}) collective-permute-start(f32[96,1024]{1,0:T(8,128)S(1)} %dynamic-slice_add_fusion), channel_id=1, source_target_pairs={{0,448},{1,449},{2,450},{3,451},{4,452},{5,453},{6,454},{7,455},{8... | collective-permute-start | bytes 1179656 | tf_op jit(solution)/shard_map/ppermute | solution.py:22
  21.6 7.1 %collective-permute-done.1 = f32[96,1024]{1,0:T(8,128)} collective-permute-done((f32[96,1024]{1,0:T(8,128)S(1)}, f32[96,1024]{1,0:T(8,128)}, u32[]{:S(2)}, u32[]{:S(2)}) %collective-permute-start.1) | collective-permute-done | bytes 393248 | tf_op jit(solution)/shard_map/ppermute | solution.py:22
  29.9 4.5 %collective-permute-start.2 = (f32[96,1024]{1,0:T(8,128)S(1)}, f32[96,1024]{1,0:T(8,128)}, u32[]{:S(2)}, u32[]{:S(2)}) collective-permute-start(f32[96,1024]{1,0:T(8,128)S(1)} %add_add_fusion), channel_id=1, source_target_pairs={{0,64},{1,65},{2,66},{3,67},{4,68},{5,69},{6,70},{7,71},{8,72},{9,... | collective-permute-start | bytes 1179656 | tf_op jit(solution)/shard_map/ppermute | solution.py:22
  34.4 7.9 %collective-permute-start.3 = (f32[48,1024]{1,0:T(8,128)}, f32[48,1024]{1,0:T(8,128)}, u32[]{:S(2)}, u32[]{:S(2)}) collective-permute-start(f32[48,1024]{1,0:T(8,128)} %constant_dynamic-slice_fusion.2), channel_id=1, source_target_pairs={{0,0},{1,32},{2,64},{3,96},{4,128},{5,160},{6,192},{7,224},{8,256}... | collective-permute-start | bytes 589832 | tf_op jit(solution)/shard_map/ppermute | solution.py:22
  43.5 6.4 %collective-permute-done.3 = f32[48,1024]{1,0:T(8,128)} collective-permute-done((f32[48,1024]{1,0:T(8,128)}, f32[48,1024]{1,0:T(8,128)}, u32[]{:S(2)}, u32[]{:S(2)}) %collective-permute-start.3) | collective-permute-done | bytes 196640 | tf_op jit(solution)/shard_map/ppermute | solution.py:22
  50.0 4.6 %collective-permute-start.4 = (f32[96,1024]{1,0:T(8,128)S(1)}, f32[96,1024]{1,0:T(8,128)}, u32[]{:S(2)}, u32[]{:S(2)}) collective-permute-start(f32[96,1024]{1,0:T(8,128)S(1)} %add_add_fusion.1), channel_id=1, source_target_pairs={{0,448},{1,449},{2,450},{3,451},{4,452},{5,453},{6,454},{7,455},{8... | collective-permute-start | bytes 1179656 | tf_op jit(solution)/shard_map/ppermute | solution.py:22
  54.7 5.8 %collective-permute-done.4 = f32[96,1024]{1,0:T(8,128)} collective-permute-done((f32[96,1024]{1,0:T(8,128)S(1)}, f32[96,1024]{1,0:T(8,128)}, u32[]{:S(2)}, u32[]{:S(2)}) %collective-permute-start.4) | collective-permute-done | bytes 393248 | tf_op jit(solution)/shard_map/ppermute | solution.py:22
  61.7 1.9 collective-permute-start.5
  63.6 5.6 %collective-permute-done.5 = f32[48,1024]{1,0:T(8,128)S(1)} collective-permute-done((f32[48,1024]{1,0:T(8,128)S(1)}, f32[48,1024]{1,0:T(8,128)S(1)}, u32[]{:S(2)}, u32[]{:S(2)}) %collective-permute-start.5) | collective-permute-done | bytes 196640 | tf_op jit(solution)/shard_map/ppermute | solution.py:22
  69.3 18.5 %collective-permute-start.6 = (f32[48,1024]{1,0:T(8,128)S(1)}, f32[48,1024]{1,0:T(8,128)S(1)}, u32[]{:S(2)}, u32[]{:S(2)}) collective-permute-start(f32[48,1024]{1,0:T(8,128)S(1)} %dynamic-slice_add_fusion.1), channel_id=1, source_target_pairs={{0,32},{1,33},{2,34},{3,35},{4,36},{5,37},{6,38},{7,39},{8,40},{9,... | collective-permute-start | bytes 589832 | tf_op jit(solution)/shard_map/ppermute | solution.py:22
  87.8 4.4 %collective-permute-done.6 = f32[48,1024]{1,0:T(8,128)S(1)} collective-permute-done((f32[48,1024]{1,0:T(8,128)S(1)}, f32[48,1024]{1,0:T(8,128)S(1)}, u32[]{:S(2)}, u32[]{:S(2)}) %collective-permute-start.6) | collective-permute-done | bytes 196640 | tf_op jit(solution)/shard_map/ppermute | solution.py:22
  93.9 3.8 %collective-permute-start.8 = (f32[24,1024]{1,0:T(8,128)S(1)}, f32[24,1024]{1,0:T(8,128)S(1)}, u32[]{:S(2)}, u32[]{:S(2)}) collective-permute-start(f32[24,1024]{1,0:T(8,128)S(1)} %constant_dynamic-slice_fusion), channel_id=1, source_target_pairs={{0,0},{1,32},{2,2},{3,34},{4,4},{5,36},{6,6},{7,38},{8,8},{9,40},{... | collective-permute-start | bytes 294920 | tf_op jit(solution)/shard_map/ppermute | solution.py:22
  97.7 6.0 %collective-permute-done.8 = f32[24,1024]{1,0:T(8,128)S(1)} collective-permute-done((f32[24,1024]{1,0:T(8,128)S(1)}, f32[24,1024]{1,0:T(8,128)S(1)}, u32[]{:S(2)}, u32[]{:S(2)}) %collective-permute-start.8) | collective-permute-done | bytes 98336 | tf_op jit(solution)/shard_map/ppermute | solution.py:22
  104.4 22.5 %all_gather.10 = f32[96,1024]{1,0:T(8,128)S(1)} all-gather(f32[24,1024]{1,0:T(8,128)S(1)} %collective-permute-done.9), channel_id=1, replica_groups=mesh['y'=8,'zh'=2,'c'=2,'x'=4,'zl'=4] {'zl'}, dimensions={0}, use_global_device_ids=true | all-gather | bytes 491520 | tf_op jit(solution)/shard_map/all_gather | solution.py:150
  127.0 3.0 %collective-permute-start.10 = (f32[96,1024]{1,0:T(8,128)S(1)}, f32[96,1024]{1,0:T(8,128)S(1)}, u32[]{:S(2)}, u32[]{:S(2)}) collective-permute-start(f32[96,1024]{1,0:T(8,128)S(1)} %maximum_select_fusion.2), channel_id=1, source_target_pairs={{0,4},{1,5},{2,6},{3,7},{4,0},{5,1},{6,2},{7,3},{8,12},{9,13},{10,... | collective-permute-start | bytes 1179656 | tf_op jit(solution)/shard_map/ppermute | solution.py:22
  130.2 1.4 copy.10
  131.6 1.9 collective-permute-start.12
  133.5 3.2 %collective-permute-done.10 = f32[96,1024]{1,0:T(8,128)S(1)} collective-permute-done((f32[96,1024]{1,0:T(8,128)S(1)}, f32[96,1024]{1,0:T(8,128)S(1)}, u32[]{:S(2)}, u32[]{:S(2)}) %collective-permute-start.10) | collective-permute-done | bytes 393248 | tf_op jit(solution)/shard_map/ppermute | solution.py:22
  136.7 9.9 %collective-permute-start.11 = (f32[192,1024]{1,0:T(8,128)S(1)}, f32[192,1024]{1,0:T(8,128)S(1)}, u32[]{:S(2)}, u32[]{:S(2)}) collective-permute-start(f32[192,1024]{1,0:T(8,128)S(1)} %maximum_select_fusion.1), channel_id=1, source_target_pairs={{0,12},{1,13},{2,14},{3,15},{4,8},{5,9},{6,10},{7,11},{8,4},{9,5},... | collective-permute-start | bytes 2359304 | tf_op jit(solution)/shard_map/ppermute | solution.py:22
  149.0 2.2 %collective-permute-start.7 = (f32[384,1024]{1,0:T(8,128)S(1)}, f32[384,1024]{1,0:T(8,128)S(1)}, u32[]{:S(2)}, u32[]{:S(2)}) collective-permute-start(f32[384,1024]{1,0:T(8,128)S(1)} %get-tuple-element.19), channel_id=1, source_target_pairs={{0,16},{1,17},{2,18},{3,19},{4,20},{5,21},{6,22},{7,23},{8,24},{9,... | collective-permute-start | bytes 4718600 | tf_op jit(solution)/shard_map/ppermute | solution.py:22
  152.1 4.5 %collective-permute-done.11 = f32[192,1024]{1,0:T(8,128)S(1)} collective-permute-done((f32[192,1024]{1,0:T(8,128)S(1)}, f32[192,1024]{1,0:T(8,128)S(1)}, u32[]{:S(2)}, u32[]{:S(2)}) %collective-permute-start.11) | collective-permute-done | bytes 786464 | tf_op jit(solution)/shard_map/ppermute | solution.py:22
  156.7 1.5 constant_dynamic-update-slice_fusion.2
  158.2 2.7 %fusion.13 = f32[384,768]{0,1:T(8,128)S(1)} fusion(f32[384,1024]{1,0:T(8,128)S(1)} %slice_dynamic-update-slice_fusion, f32[768,1024]{1,0:T(8,128)S(1)} %constant_dynamic-update-slice_fusion.2), kind=kOutput, calls=%fused_computation.38 | convolution fusion | flops 1811939328 | bytes 5898240 | tf_op jit(solution)/shard_map/dot_general | solution.py:104
  162.2 3.3 %compare_select_fusion = f32[384,768]{0,1:T(8,128)S(1)} fusion(f32[384,768]{0,1:T(8,128)S(1)} %copy-done.5, f32[384,768]{0,1:T(8,128)S(1)} %fusion.13, f32[768,1024]{1,0:T(8,128)S(1)} %constant_dynamic-update-slice_fusion, f32[384,1024]{1,0:T(8,128)S(1)} %copy-done, s32[384]{0:T(512)S(1)} %iota_add_fusion.1, s32[768]{0:T(1024)S(1)} %iota_add_fusion), kind=kOutput, calls=%fused_computation | convolution fusion | flops 1816363008 | bytes 8262144 | tf_op jit(solution)/shard_map/dot_general | solution.py:104
  165.5 2.3 %fusion.14 = f32[384,1024]{1,0:T(8,128)S(1)} fusion(f32[384,768]{0,1:T(8,128)S(1)} %compare_select_fusion, f32[768,1024]{1,0:T(8,128)S(1)} %constant_dynamic-update-slice_fusion.2), kind=kOutput, calls=%fused_computation.39 | convolution fusion | flops 1811939328 | bytes 5898240 | tf_op jit(solution)/shard_map/dot_general | solution.py:104
  167.9 21.3 %all_to_all.10 = f32[4,96,1024]{2,1,0:T(8,128)S(1)} all-to-all(f32[4,96,1024]{2,1,0:T(8,128)S(1)} %bitcast.24), channel_id=1, replica_groups=mesh['y'=8,'zh'=2,'c'=2,'x'=4,'zl'=4] {'x'}, dimensions={0} | all-to-all | bytes 3145728 | tf_op jit(solution)/shard_map/all_to_all | solution.py:89
  190.0 5.3 %all-to-all-start.1 = ((f32[4,24,1024]{2,1,0:T(8,128)}), f32[4,24,1024]{2,1,0:T(8,128)S(1)}, u32[]{:S(2)}, u32[]{:S(2)}) async-start(f32[4,24,1024]{2,1,0:T(8,128)} %bitcast.2), calls=%async_computation.1 | async-start | bytes 786432 | tf_op jit(solution)/shard_map/all_to_all | solution.py:89
  195.3 2.7 %copy.11 = f32[384,768]{1,0:T(8,128)} copy(f32[384,768]{0,1:T(8,128)} %copy-done.3) | data formatting | bytes 2359296
  198.0 6.2 %all-to-all-done.1 = f32[4,24,1024]{2,1,0:T(8,128)S(1)} async-done(((f32[4,24,1024]{2,1,0:T(8,128)}), f32[4,24,1024]{2,1,0:T(8,128)S(1)}, u32[]{:S(2)}, u32[]{:S(2)}) %all-to-all-start.1) | async-done | bytes 393248 | tf_op jit(solution)/shard_map/all_to_all | solution.py:89
  (54 shorter events, 15.8 us)
Async XLA Ops:
  7.2 1.4 copy-start
  7.2 119.8 %all-gather.5.cloned.1.call-start = ((), (), s32[]{:S(2)}) async-start(), calls=%async_computation.3 | async-start | bytes 1769472 | tf_op jit(solution)/shard_map/all_gather | solution.py:140
  12.3 5.6 %collective-permute-start = (f32[384,1024]{1,0:T(8,128)}, f32[384,1024]{1,0:T(8,128)}, u32[]{:S(2)}, u32[]{:S(2)}) collective-permute-start(f32[384,1024]{1,0:T(8,128)} %fusion.6), channel_id=1, source_target_pairs={{0,16},{1,17},{2,18},{3,19},{4,20},{5,21},{6,22},{7,23},{8,24},{9,... | collective-permute-start | bytes 4718600 | tf_op jit(solution)/shard_map/ppermute | solution.py:22
  19.0 9.8 %collective-permute-start.1 = (f32[96,1024]{1,0:T(8,128)S(1)}, f32[96,1024]{1,0:T(8,128)}, u32[]{:S(2)}, u32[]{:S(2)}) collective-permute-start(f32[96,1024]{1,0:T(8,128)S(1)} %dynamic-slice_add_fusion), channel_id=1, source_target_pairs={{0,448},{1,449},{2,450},{3,451},{4,452},{5,453},{6,454},{7,455},{8... | collective-permute-start | bytes 1179656 | tf_op jit(solution)/shard_map/ppermute | solution.py:22
  29.9 12.4 %collective-permute-start.2 = (f32[96,1024]{1,0:T(8,128)S(1)}, f32[96,1024]{1,0:T(8,128)}, u32[]{:S(2)}, u32[]{:S(2)}) collective-permute-start(f32[96,1024]{1,0:T(8,128)S(1)} %add_add_fusion), channel_id=1, source_target_pairs={{0,64},{1,65},{2,66},{3,67},{4,68},{5,69},{6,70},{7,71},{8,72},{9,... | collective-permute-start | bytes 1179656 | tf_op jit(solution)/shard_map/ppermute | solution.py:22
  34.4 15.5 %collective-permute-start.3 = (f32[48,1024]{1,0:T(8,128)}, f32[48,1024]{1,0:T(8,128)}, u32[]{:S(2)}, u32[]{:S(2)}) collective-permute-start(f32[48,1024]{1,0:T(8,128)} %constant_dynamic-slice_fusion.2), channel_id=1, source_target_pairs={{0,0},{1,32},{2,64},{3,96},{4,128},{5,160},{6,192},{7,224},{8,256}... | collective-permute-start | bytes 589832 | tf_op jit(solution)/shard_map/ppermute | solution.py:22
  50.0 96.7 %all-gather.3.cloned.1.call-start = ((), (), s32[]{:S(2)}) async-start(), calls=%async_computation.2 | async-start | bytes 1769472 | tf_op jit(solution)/shard_map/all_gather | solution.py:148
  50.0 10.5 %collective-permute-start.4 = (f32[96,1024]{1,0:T(8,128)S(1)}, f32[96,1024]{1,0:T(8,128)}, u32[]{:S(2)}, u32[]{:S(2)}) collective-permute-start(f32[96,1024]{1,0:T(8,128)S(1)} %add_add_fusion.1), channel_id=1, source_target_pairs={{0,448},{1,449},{2,450},{3,451},{4,452},{5,453},{6,454},{7,455},{8... | collective-permute-start | bytes 1179656 | tf_op jit(solution)/shard_map/ppermute | solution.py:22
  61.7 7.6 %collective-permute-start.5 = (f32[48,1024]{1,0:T(8,128)S(1)}, f32[48,1024]{1,0:T(8,128)S(1)}, u32[]{:S(2)}, u32[]{:S(2)}) collective-permute-start(f32[48,1024]{1,0:T(8,128)S(1)} %constant_dynamic-slice_fusion.1), channel_id=1, source_target_pairs={{0,64},{1,65},{2,66},{3,67},{4,68},{5,69},{6,70},{7,71},{8,72},{9,... | collective-permute-start | bytes 589832 | tf_op jit(solution)/shard_map/ppermute | solution.py:22
  69.3 22.8 %collective-permute-start.6 = (f32[48,1024]{1,0:T(8,128)S(1)}, f32[48,1024]{1,0:T(8,128)S(1)}, u32[]{:S(2)}, u32[]{:S(2)}) collective-permute-start(f32[48,1024]{1,0:T(8,128)S(1)} %dynamic-slice_add_fusion.1), channel_id=1, source_target_pairs={{0,32},{1,33},{2,34},{3,35},{4,36},{5,37},{6,38},{7,39},{8,40},{9,... | collective-permute-start | bytes 589832 | tf_op jit(solution)/shard_map/ppermute | solution.py:22
  92.9 37.3 %copy-start.2 = (f32[384,768]{1,0:T(8,128)S(1)}, f32[384,768]{1,0:T(8,128)}, u32[]{:S(2)}) copy-start(f32[384,768]{1,0:T(8,128)} %param.2) | copy-start | bytes 3538948
  93.9 9.8 %collective-permute-start.8 = (f32[24,1024]{1,0:T(8,128)S(1)}, f32[24,1024]{1,0:T(8,128)S(1)}, u32[]{:S(2)}, u32[]{:S(2)}) collective-permute-start(f32[24,1024]{1,0:T(8,128)S(1)} %constant_dynamic-slice_fusion), channel_id=1, source_target_pairs={{0,0},{1,32},{2,2},{3,34},{4,4},{5,36},{6,6},{7,38},{8,8},{9,40},{... | collective-permute-start | bytes 294920 | tf_op jit(solution)/shard_map/ppermute | solution.py:22
  103.7 0.7 collective-permute-start.9
  127.0 9.7 %collective-permute-start.10 = (f32[96,1024]{1,0:T(8,128)S(1)}, f32[96,1024]{1,0:T(8,128)S(1)}, u32[]{:S(2)}, u32[]{:S(2)}) collective-permute-start(f32[96,1024]{1,0:T(8,128)S(1)} %maximum_select_fusion.2), channel_id=1, source_target_pairs={{0,4},{1,5},{2,6},{3,7},{4,0},{5,1},{6,2},{7,3},{8,12},{9,13},{10,... | collective-permute-start | bytes 1179656 | tf_op jit(solution)/shard_map/ppermute | solution.py:22
  131.6 25.1 %collective-permute-start.12 = (f32[384,1024]{1,0:T(8,128)}, f32[384,1024]{1,0:T(8,128)}, u32[]{:S(2)}, u32[]{:S(2)}) collective-permute-start(f32[384,1024]{1,0:T(8,128)} %all-gather.5.cloned.1.call-done), channel_id=1, source_target_pairs={{0,16},{1,17},{2,18},{3,19},{4,20},{5,21},{6,22},{7,23},{8,24},{9,... | collective-permute-start | bytes 4718600 | tf_op jit(solution)/shard_map/ppermute | solution.py:22
  136.7 19.8 %collective-permute-start.11 = (f32[192,1024]{1,0:T(8,128)S(1)}, f32[192,1024]{1,0:T(8,128)S(1)}, u32[]{:S(2)}, u32[]{:S(2)}) collective-permute-start(f32[192,1024]{1,0:T(8,128)S(1)} %maximum_select_fusion.1), channel_id=1, source_target_pairs={{0,12},{1,13},{2,14},{3,15},{4,8},{5,9},{6,10},{7,11},{8,4},{9,5},... | collective-permute-start | bytes 2359304 | tf_op jit(solution)/shard_map/ppermute | solution.py:22
  146.7 1.4 copy-start.1
  146.7 1.8 slice-start
  146.7 1.8 slice-start.1
  149.0 2.6 %copy-start.4 = (f32[384,1024]{1,0:T(8,128)S(1)}, f32[384,1024]{1,0:T(8,128)}, u32[]{:S(2)}) copy-start(f32[384,1024]{1,0:T(8,128)} %all-gather.5.cloned.1.call-done) | copy-start | bytes 4718596
  149.0 11.9 %collective-permute-start.7 = (f32[384,1024]{1,0:T(8,128)S(1)}, f32[384,1024]{1,0:T(8,128)S(1)}, u32[]{:S(2)}, u32[]{:S(2)}) collective-permute-start(f32[384,1024]{1,0:T(8,128)S(1)} %get-tuple-element.19), channel_id=1, source_target_pairs={{0,16},{1,17},{2,18},{3,19},{4,20},{5,21},{6,22},{7,23},{8,24},{9,... | collective-permute-start | bytes 4718600 | tf_op jit(solution)/shard_map/ppermute | solution.py:22
  160.9 1.3 copy-start.5
  165.5 2.3 %copy-start.3 = (f32[384,768]{0,1:T(8,128)}, f32[384,768]{0,1:T(8,128)S(1)}, u32[]{:S(2)}) copy-start(f32[384,768]{0,1:T(8,128)S(1)} %compare_select_fusion) | copy-start | bytes 3538948
  190.0 14.2 %all-to-all-start.1 = ((f32[4,24,1024]{2,1,0:T(8,128)}), f32[4,24,1024]{2,1,0:T(8,128)S(1)}, u32[]{:S(2)}, u32[]{:S(2)}) async-start(f32[4,24,1024]{2,1,0:T(8,128)} %bitcast.2), calls=%async_computation.1 | async-start | bytes 786432 | tf_op jit(solution)/shard_map/all_to_all | solution.py:89
Sparse Core Ops, SparseCore 0:
  50.1 47.4 all-gather.4
  99.6 41.2 all-gather.2

commit v4 on v3

--- a/solution.py
+++ b/solution.py
@@ -136,8 +136,7 @@
     passed = pair_swap(sending, "y", 1)
     data = transpose_data(share)
     passed = pair_swap(sums(near) + passed, "y", 0)
-    sending, data = together(sums(other) + passed, data)
-    data_half = lax.all_gather(data, "y", axis=0, tiled=True)
+    sending = sums(other) + passed
     passed = pair_swap(sending, "y", 1)
     mine = sums(pair) + passed
     passed = pair_swap(take(mine, (1 - odd) * block, block), "y", 0)
@@ -145,15 +144,16 @@
     product = product + swap_zh(product)
 
     own = take(product, zh * (block // 2), block // 2)
-    product_half = lax.all_gather(product, "y", axis=0, tiled=True)
+    pieces = lax.all_gather(jnp.stack([product, data]), "y", axis=1, tiled=True)
     own = transpose_along_y(transpose_in_plane(own))
     own = lax.all_gather(own, "zl", axis=0, tiled=True)
     own = in_pair(own[:block], own[block:], row_chip // 2 % 2)
-    own, data_half = together(own, data_half)
     x_odd = (x - c) % 2
     rows0 = in_pair(own, pair_swap(own, "x", 0), x_odd)
-    data_cols = both_cores(data_half, c)
     rows1 = pair_swap(rows0, "x", 1)
+    pieces, _ = together(pieces, rows0)
+    data_cols = both_cores(pieces[1], c)
+    product_half = pieces[0]
     shifted = jnp.concatenate([product_half[block:], product_half[:block]])
     product_cols = both_cores(jnp.where(c == 0, product_half, shifted), c)
     product_rows = jnp.zeros_like(sample_rows)

time: 213 us -> 214 us (level)
  the two profiles are of different devices: /device:TPU:40 before, /device:TPU:24 now
where the time goes in v4:
time: 214 us; the launch traced here: 213 us
  waiting for transfers between devices  62.8 us (29%)
  starting transfers between devices  62.3 us (29%)
  blocking collectives  37.9 us (18%)
  between operations  14.8 us (7%)
  matrix products  14.5 us (7%)
  local copies, waits for them, and re-layouts  12.9 us (6%)
  other arithmetic  7.62 us (4%)
    ppermute x13, starting transfers between devices, permute(): return lax.ppermute(v, AXES, pairs)  57 us
    ppermute x13, waiting for transfers between devices, permute(): return lax.ppermute(v, AXES, pairs)  56.3 us
    all_to_all x1, blocking collectives, scatter_sum(): parts = lax.all_to_all(v.reshape(n, -1, v.shape[1]), axis, 0, 0, tiled=True)  23.6 us
    dot_general x5, matrix products, dot(): lax.dot_general(a, b, (contract, ((), ())), precision=PREC, preferred_ele...  14.5 us
    all_gather x1, blocking collectives, on_device(): own = lax.all_gather(own, 'zl', axis=0, tiled=True)  14.3 us
    unnamed x12, local copies, waits for them, and re-layouts  6.54 us
    all_to_all x1, waiting for transfers between devices, scatter_sum(): parts = lax.all_to_all(v.reshape(n, -1, v.shape[1]), axis, 0, 0, tiled=True)  6.46 us
    all_to_all x1, starting transfers between devices, scatter_sum(): parts = lax.all_to_all(v.reshape(n, -1, v.shape[1]), axis, 0, 0, tiled=True)  5.2 us
  transfers between devices with their start and end apart: 15, of which 10 were waited for; matrix products, arithmetic and copies ran while one was open for 8% of the time, Pallas kernels for 0%

profile of v4, /device:TPU:24, one launch (start us, length us, event | category | flops | bytes accessed | tf_op | source)
XLA Modules:
  0.0 212.7 jit_solution(11761255464161160870)
XLA Ops:
  8.6 3.6 %fusion.6 = f32[384,1024]{1,0:T(8,128)} fusion(f32[384,1024]{1,0:T(8,128)S(1)} %copy-done, f32[384,768]{1,0:T(8,128)} %param.2, s32[]{:T(128)S(6)} %select_n.165), kind=kOutput, calls=%fused_computation.14 | convolution fusion | flops 905969664 | bytes 3735556 | tf_op jit(solution)/shard_map/dot_general | solution.py:104
  12.2 1.9 collective-permute-start
  14.2 2.5 %fusion.8 = f32[384,1024]{1,0:T(8,128)S(1)} fusion(f32[384,1024]{1,0:T(8,128)S(1)} %copy-done, f32[384,768]{1,0:T(8,128)} %param.2, s32[]{:T(128)S(6)} %select_n.160), kind=kOutput, calls=%fused_computation.16 | convolution fusion | flops 905969664 | bytes 3735556 | tf_op jit(solution)/shard_map/dot_general | solution.py:104
  18.9 4.7 %collective-permute-start.1 = (f32[96,1024]{1,0:T(8,128)S(1)}, f32[96,1024]{1,0:T(8,128)}, u32[]{:S(2)}, u32[]{:S(2)}) collective-permute-start(f32[96,1024]{1,0:T(8,128)S(1)} %dynamic-slice_add_fusion), channel_id=1, source_target_pairs={{0,448},{1,449},{2,450},{3,451},{4,452},{5,453},{6,454},{7,455},{8... | collective-permute-start | bytes 1179656 | tf_op jit(solution)/shard_map/ppermute | solution.py:22
  23.6 6.2 %collective-permute-done.1 = f32[96,1024]{1,0:T(8,128)} collective-permute-done((f32[96,1024]{1,0:T(8,128)S(1)}, f32[96,1024]{1,0:T(8,128)}, u32[]{:S(2)}, u32[]{:S(2)}) %collective-permute-start.1) | collective-permute-done | bytes 393248 | tf_op jit(solution)/shard_map/ppermute | solution.py:22
  31.1 1.9 collective-permute-start.2
  33.0 7.8 %collective-permute-done.2 = f32[96,1024]{1,0:T(8,128)} collective-permute-done((f32[96,1024]{1,0:T(8,128)S(1)}, f32[96,1024]{1,0:T(8,128)}, u32[]{:S(2)}, u32[]{:S(2)}) %collective-permute-start.2) | collective-permute-done | bytes 393248 | tf_op jit(solution)/shard_map/ppermute | solution.py:22
  42.0 4.7 %collective-permute-start.3 = (f32[96,1024]{1,0:T(8,128)S(1)}, f32[96,1024]{1,0:T(8,128)}, u32[]{:S(2)}, u32[]{:S(2)}) collective-permute-start(f32[96,1024]{1,0:T(8,128)S(1)} %add_add_fusion.1), channel_id=1, source_target_pairs={{0,448},{1,449},{2,450},{3,451},{4,452},{5,453},{6,454},{7,455},{8... | collective-permute-start | bytes 1179656 | tf_op jit(solution)/shard_map/ppermute | solution.py:22
  46.8 6.2 %collective-permute-done.3 = f32[96,1024]{1,0:T(8,128)} collective-permute-done((f32[96,1024]{1,0:T(8,128)S(1)}, f32[96,1024]{1,0:T(8,128)}, u32[]{:S(2)}, u32[]{:S(2)}) %collective-permute-start.3) | collective-permute-done | bytes 393248 | tf_op jit(solution)/shard_map/ppermute | solution.py:22
  54.2 3.4 %collective-permute-start.4 = (f32[48,1024]{1,0:T(8,128)S(1)}, f32[48,1024]{1,0:T(8,128)S(1)}, u32[]{:S(2)}, u32[]{:S(2)}) collective-permute-start(f32[48,1024]{1,0:T(8,128)S(1)} %constant_dynamic-slice_fusion.1), channel_id=1, source_target_pairs={{0,64},{1,65},{2,66},{3,67},{4,68},{5,69},{6,70},{7,71},{8,72},{9,... | collective-permute-start | bytes 589832 | tf_op jit(solution)/shard_map/ppermute | solution.py:22
  57.7 4.2 %collective-permute-done.4 = f32[48,1024]{1,0:T(8,128)S(1)} collective-permute-done((f32[48,1024]{1,0:T(8,128)S(1)}, f32[48,1024]{1,0:T(8,128)S(1)}, u32[]{:S(2)}, u32[]{:S(2)}) %collective-permute-start.4) | collective-permute-done | bytes 196640 | tf_op jit(solution)/shard_map/ppermute | solution.py:22
  61.8 10.9 %collective-permute-start.5 = (f32[48,1024]{1,0:T(8,128)S(1)}, f32[48,1024]{1,0:T(8,128)S(1)}, u32[]{:S(2)}, u32[]{:S(2)}) collective-permute-start(f32[48,1024]{1,0:T(8,128)S(1)} %dynamic-slice_add_fusion.1), channel_id=1, source_target_pairs={{0,32},{1,33},{2,34},{3,35},{4,36},{5,37},{6,38},{7,39},{8,40},{9,... | collective-permute-start | bytes 589832 | tf_op jit(solution)/shard_map/ppermute | solution.py:22
  72.8 6.9 %collective-permute-start.6 = (f32[48,1024]{1,0:T(8,128)}, f32[48,1024]{1,0:T(8,128)S(1)}, u32[]{:S(2)}, u32[]{:S(2)}) collective-permute-start(f32[48,1024]{1,0:T(8,128)} %constant_dynamic-slice_fusion.2), channel_id=1, source_target_pairs={{0,0},{1,32},{2,64},{3,96},{4,128},{5,160},{6,192},{7,224},{8,256}... | collective-permute-start | bytes 589832 | tf_op jit(solution)/shard_map/ppermute | solution.py:22
  79.7 7.0 %collective-permute-done.6 = f32[48,1024]{1,0:T(8,128)S(1)} collective-permute-done((f32[48,1024]{1,0:T(8,128)}, f32[48,1024]{1,0:T(8,128)S(1)}, u32[]{:S(2)}, u32[]{:S(2)}) %collective-permute-start.6) | collective-permute-done | bytes 196640 | tf_op jit(solution)/shard_map/ppermute | solution.py:22
  87.5 6.9 %collective-permute-start.7 = (f32[24,1024]{1,0:T(8,128)S(1)}, f32[24,1024]{1,0:T(8,128)S(1)}, u32[]{:S(2)}, u32[]{:S(2)}) collective-permute-start(f32[24,1024]{1,0:T(8,128)S(1)} %constant_dynamic-slice_fusion), channel_id=1, source_target_pairs={{0,0},{1,32},{2,2},{3,34},{4,4},{5,36},{6,6},{7,38},{8,8},{9,40},{... | collective-permute-start | bytes 294920 | tf_op jit(solution)/shard_map/ppermute | solution.py:22
  94.5 5.1 %collective-permute-done.7 = f32[24,1024]{1,0:T(8,128)S(1)} collective-permute-done((f32[24,1024]{1,0:T(8,128)S(1)}, f32[24,1024]{1,0:T(8,128)S(1)}, u32[]{:S(2)}, u32[]{:S(2)}) %collective-permute-start.7) | collective-permute-done | bytes 98336 | tf_op jit(solution)/shard_map/ppermute | solution.py:22
  99.6 3.6 %collective-permute-start.8 = (f32[24,1024]{1,0:T(8,128)S(1)}, f32[24,1024]{1,0:T(8,128)S(1)}, u32[]{:S(2)}, u32[]{:S(2)}) collective-permute-start(f32[24,1024]{1,0:T(8,128)S(1)} %collective-permute-done.7), channel_id=1, source_target_pairs={{0,0},{1,1},{2,66},{3,67},{4,132},{5,133},{6,198},{7,199},{8,264},... | collective-permute-start | bytes 294920 | tf_op jit(solution)/shard_map/ppermute | solution.py:22
  103.2 8.8 %collective-permute-done.8 = f32[24,1024]{1,0:T(8,128)S(1)} collective-permute-done((f32[24,1024]{1,0:T(8,128)S(1)}, f32[24,1024]{1,0:T(8,128)S(1)}, u32[]{:S(2)}, u32[]{:S(2)}) %collective-permute-start.8) | collective-permute-done | bytes 98336 | tf_op jit(solution)/shard_map/ppermute | solution.py:22
  112.1 14.3 %all_gather.7 = f32[96,1024]{1,0:T(8,128)S(1)} all-gather(f32[24,1024]{1,0:T(8,128)S(1)} %collective-permute-done.8), channel_id=1, replica_groups=mesh['y'=8,'zh'=2,'c'=2,'x'=4,'zl'=4] {'zl'}, dimensions={0}, use_global_device_ids=true | all-gather | bytes 491520 | tf_op jit(solution)/shard_map/all_gather | solution.py:149
  126.4 1.9 collective-permute-start.9
  129.9 10.5 %collective-permute-done.9 = f32[96,1024]{1,0:T(8,128)S(1)} collective-permute-done((f32[96,1024]{1,0:T(8,128)S(1)}, f32[96,1024]{1,0:T(8,128)S(1)}, u32[]{:S(2)}, u32[]{:S(2)}) %collective-permute-start.9) | collective-permute-done | bytes 393248 | tf_op jit(solution)/shard_map/ppermute | solution.py:22
  140.4 5.4 %collective-permute-start.11 = (f32[192,1024]{1,0:T(8,128)S(1)}, f32[192,1024]{1,0:T(8,128)S(1)}, u32[]{:S(2)}, u32[]{:S(2)}) collective-permute-start(f32[192,1024]{1,0:T(8,128)S(1)} %maximum_select_fusion.1), channel_id=1, source_target_pairs={{0,12},{1,13},{2,14},{3,15},{4,8},{5,9},{6,10},{7,11},{8,4},{9,5},... | collective-permute-start | bytes 2359304 | tf_op jit(solution)/shard_map/ppermute | solution.py:22
  148.3 1.6 slice_bitcast_fusion
  149.9 2.2 %collective-permute-start.12 = (f32[384,1024]{1,0:T(8,128)S(1)}, f32[384,1024]{1,0:T(8,128)S(1)}, u32[]{:S(2)}, u32[]{:S(2)}) collective-permute-start(f32[384,1024]{1,0:T(8,128)S(1)} %slice_bitcast_fusion), channel_id=1, source_target_pairs={{0,16},{1,17},{2,18},{3,19},{4,20},{5,21},{6,22},{7,23},{8,24},{9,... | collective-permute-start | bytes 4718600 | tf_op jit(solution)/shard_map/ppermute | solution.py:22
  153.0 2.6 %collective-permute-start.10 = (f32[384,1024]{1,0:T(8,128)S(1)}, f32[384,1024]{1,0:T(8,128)S(1)}, u32[]{:S(2)}, u32[]{:S(2)}) collective-permute-start(f32[384,1024]{1,0:T(8,128)S(1)} %get-tuple-element.13), channel_id=1, source_target_pairs={{0,16},{1,17},{2,18},{3,19},{4,20},{5,21},{6,22},{7,23},{8,24},{9,... | collective-permute-start | bytes 4718600 | tf_op jit(solution)/shard_map/ppermute | solution.py:22
  156.8 2.7 %fusion.13 = f32[384,768]{0,1:T(8,128)S(1)} fusion(f32[384,1024]{1,0:T(8,128)S(1)} %slice_dynamic-update-slice_fusion, f32[768,1024]{1,0:T(8,128)S(1)} %constant_dynamic-update-slice_fusion.2), kind=kOutput, calls=%fused_computation.42 | convolution fusion | flops 1811939328 | bytes 5898240 | tf_op jit(solution)/shard_map/dot_general | solution.py:104
  160.8 3.3 %compare_select_fusion = f32[384,768]{0,1:T(8,128)S(1)} fusion(f32[384,768]{0,1:T(8,128)S(1)} %copy-done.4, f32[384,768]{0,1:T(8,128)S(1)} %fusion.13, f32[768,1024]{1,0:T(8,128)S(1)} %constant_dynamic-update-slice_fusion, f32[384,1024]{1,0:T(8,128)S(1)} %copy-done, s32[384]{0:T(512)S(1)} %iota_add_fusion.1, s32[768]{0:T(1024)S(1)} %iota_add_fusion), kind=kOutput, calls=%fused_computation | convolution fusion | flops 1816363008 | bytes 8262144 | tf_op jit(solution)/shard_map/dot_general | solution.py:104
  164.1 2.3 %fusion.14 = f32[384,1024]{1,0:T(8,128)S(1)} fusion(f32[384,768]{0,1:T(8,128)S(1)} %compare_select_fusion, f32[768,1024]{1,0:T(8,128)S(1)} %constant_dynamic-update-slice_fusion.2), kind=kOutput, calls=%fused_computation.43 | convolution fusion | flops 1811939328 | bytes 5898240 | tf_op jit(solution)/shard_map/dot_general | solution.py:104
  166.4 23.6 %all_to_all.10 = f32[4,96,1024]{2,1,0:T(8,128)S(1)} all-to-all(f32[4,96,1024]{2,1,0:T(8,128)S(1)} %bitcast.37), channel_id=1, replica_groups=mesh['y'=8,'zh'=2,'c'=2,'x'=4,'zl'=4] {'x'}, dimensions={0} | all-to-all | bytes 3145728 | tf_op jit(solution)/shard_map/all_to_all | solution.py:89
  190.9 5.2 %all-to-all-start.1 = ((f32[4,24,1024]{2,1,0:T(8,128)}), f32[4,24,1024]{2,1,0:T(8,128)S(1)}, u32[]{:S(2)}, u32[]{:S(2)}) async-start(f32[4,24,1024]{2,1,0:T(8,128)} %bitcast.8), calls=%async_computation.1 | async-start | bytes 786432 | tf_op jit(solution)/shard_map/all_to_all | solution.py:89
  196.1 2.7 %copy.11 = f32[384,768]{1,0:T(8,128)} copy(f32[384,768]{0,1:T(8,128)} %copy-done.3) | data formatting | bytes 2359296
  198.8 6.5 %all-to-all-done.1 = f32[4,24,1024]{2,1,0:T(8,128)S(1)} async-done(((f32[4,24,1024]{2,1,0:T(8,128)}), f32[4,24,1024]{2,1,0:T(8,128)S(1)}, u32[]{:S(2)}, u32[]{:S(2)}) %all-to-all-start.1) | async-done | bytes 393248 | tf_op jit(solution)/shard_map/all_to_all | solution.py:89
  (49 shorter events, 16.8 us)
Async XLA Ops:
  7.2 1.4 copy-start
  7.2 138.7 %all-gather.2.cloned.1.call-start = ((), (), s32[]{:S(2)}) async-start(), calls=%async_computation.2 | async-start | bytes 3538944 | tf_op jit(solution)/shard_map/all_gather | solution.py:147
  12.2 5.6 %collective-permute-start = (f32[384,1024]{1,0:T(8,128)}, f32[384,1024]{1,0:T(8,128)}, u32[]{:S(2)}, u32[]{:S(2)}) collective-permute-start(f32[384,1024]{1,0:T(8,128)} %fusion.6), channel_id=1, source_target_pairs={{0,16},{1,17},{2,18},{3,19},{4,20},{5,21},{6,22},{7,23},{8,24},{9,... | collective-permute-start | bytes 4718600 | tf_op jit(solution)/shard_map/ppermute | solution.py:22
  18.9 11.0 %collective-permute-start.1 = (f32[96,1024]{1,0:T(8,128)S(1)}, f32[96,1024]{1,0:T(8,128)}, u32[]{:S(2)}, u32[]{:S(2)}) collective-permute-start(f32[96,1024]{1,0:T(8,128)S(1)} %dynamic-slice_add_fusion), channel_id=1, source_target_pairs={{0,448},{1,449},{2,450},{3,451},{4,452},{5,453},{6,454},{7,455},{8... | collective-permute-start | bytes 1179656 | tf_op jit(solution)/shard_map/ppermute | solution.py:22
  31.1 9.8 %collective-permute-start.2 = (f32[96,1024]{1,0:T(8,128)S(1)}, f32[96,1024]{1,0:T(8,128)}, u32[]{:S(2)}, u32[]{:S(2)}) collective-permute-start(f32[96,1024]{1,0:T(8,128)S(1)} %add_add_fusion), channel_id=1, source_target_pairs={{0,64},{1,65},{2,66},{3,67},{4,68},{5,69},{6,70},{7,71},{8,72},{9,... | collective-permute-start | bytes 1179656 | tf_op jit(solution)/shard_map/ppermute | solution.py:22
  42.0 11.0 %collective-permute-start.3 = (f32[96,1024]{1,0:T(8,128)S(1)}, f32[96,1024]{1,0:T(8,128)}, u32[]{:S(2)}, u32[]{:S(2)}) collective-permute-start(f32[96,1024]{1,0:T(8,128)S(1)} %add_add_fusion.1), channel_id=1, source_target_pairs={{0,448},{1,449},{2,450},{3,451},{4,452},{5,453},{6,454},{7,455},{8... | collective-permute-start | bytes 1179656 | tf_op jit(solution)/shard_map/ppermute | solution.py:22
  54.2 7.6 %collective-permute-start.4 = (f32[48,1024]{1,0:T(8,128)S(1)}, f32[48,1024]{1,0:T(8,128)S(1)}, u32[]{:S(2)}, u32[]{:S(2)}) collective-permute-start(f32[48,1024]{1,0:T(8,128)S(1)} %constant_dynamic-slice_fusion.1), channel_id=1, source_target_pairs={{0,64},{1,65},{2,66},{3,67},{4,68},{5,69},{6,70},{7,71},{8,72},{9,... | collective-permute-start | bytes 589832 | tf_op jit(solution)/shard_map/ppermute | solution.py:22
  61.8 17.8 %collective-permute-start.5 = (f32[48,1024]{1,0:T(8,128)S(1)}, f32[48,1024]{1,0:T(8,128)S(1)}, u32[]{:S(2)}, u32[]{:S(2)}) collective-permute-start(f32[48,1024]{1,0:T(8,128)S(1)} %dynamic-slice_add_fusion.1), channel_id=1, source_target_pairs={{0,32},{1,33},{2,34},{3,35},{4,36},{5,37},{6,38},{7,39},{8,40},{9,... | collective-permute-start | bytes 589832 | tf_op jit(solution)/shard_map/ppermute | solution.py:22
  72.8 13.9 %collective-permute-start.6 = (f32[48,1024]{1,0:T(8,128)}, f32[48,1024]{1,0:T(8,128)S(1)}, u32[]{:S(2)}, u32[]{:S(2)}) collective-permute-start(f32[48,1024]{1,0:T(8,128)} %constant_dynamic-slice_fusion.2), channel_id=1, source_target_pairs={{0,0},{1,32},{2,64},{3,96},{4,128},{5,160},{6,192},{7,224},{8,256}... | collective-permute-start | bytes 589832 | tf_op jit(solution)/shard_map/ppermute | solution.py:22
  87.5 41.0 %copy-start.2 = (f32[384,768]{1,0:T(8,128)S(1)}, f32[384,768]{1,0:T(8,128)}, u32[]{:S(2)}) copy-start(f32[384,768]{1,0:T(8,128)} %param.2) | copy-start | bytes 3538948
  87.5 12.1 %collective-permute-start.7 = (f32[24,1024]{1,0:T(8,128)S(1)}, f32[24,1024]{1,0:T(8,128)S(1)}, u32[]{:S(2)}, u32[]{:S(2)}) collective-permute-start(f32[24,1024]{1,0:T(8,128)S(1)} %constant_dynamic-slice_fusion), channel_id=1, source_target_pairs={{0,0},{1,32},{2,2},{3,34},{4,4},{5,36},{6,6},{7,38},{8,8},{9,40},{... | collective-permute-start | bytes 294920 | tf_op jit(solution)/shard_map/ppermute | solution.py:22
  99.6 12.5 %collective-permute-start.8 = (f32[24,1024]{1,0:T(8,128)S(1)}, f32[24,1024]{1,0:T(8,128)S(1)}, u32[]{:S(2)}, u32[]{:S(2)}) collective-permute-start(f32[24,1024]{1,0:T(8,128)S(1)} %collective-permute-done.7), channel_id=1, source_target_pairs={{0,0},{1,1},{2,66},{3,67},{4,132},{5,133},{6,198},{7,199},{8,264},... | collective-permute-start | bytes 294920 | tf_op jit(solution)/shard_map/ppermute | solution.py:22
  126.4 13.9 %collective-permute-start.9 = (f32[96,1024]{1,0:T(8,128)S(1)}, f32[96,1024]{1,0:T(8,128)S(1)}, u32[]{:S(2)}, u32[]{:S(2)}) collective-permute-start(f32[96,1024]{1,0:T(8,128)S(1)} %maximum_select_fusion.2), channel_id=1, source_target_pairs={{0,4},{1,5},{2,6},{3,7},{4,0},{5,1},{6,2},{7,3},{8,12},{9,13},{10,... | collective-permute-start | bytes 1179656 | tf_op jit(solution)/shard_map/ppermute | solution.py:22
  140.4 15.4 %collective-permute-start.11 = (f32[192,1024]{1,0:T(8,128)S(1)}, f32[192,1024]{1,0:T(8,128)S(1)}, u32[]{:S(2)}, u32[]{:S(2)}) collective-permute-start(f32[192,1024]{1,0:T(8,128)S(1)} %maximum_select_fusion.1), channel_id=1, source_target_pairs={{0,12},{1,13},{2,14},{3,15},{4,8},{5,9},{6,10},{7,11},{8,4},{9,5},... | collective-permute-start | bytes 2359304 | tf_op jit(solution)/shard_map/ppermute | solution.py:22
  149.9 2.6 %copy-start.1 = (f32[2,384,1024]{2,1,0:T(8,128)S(1)}, f32[2,384,1024]{2,1,0:T(8,128)}, u32[]{:S(2)}) copy-start(f32[2,384,1024]{2,1,0:T(8,128)} %all-gather.2.cloned.1.call-done) | copy-start | bytes 9437188
  149.9 6.7 %collective-permute-start.12 = (f32[384,1024]{1,0:T(8,128)S(1)}, f32[384,1024]{1,0:T(8,128)S(1)}, u32[]{:S(2)}, u32[]{:S(2)}) collective-permute-start(f32[384,1024]{1,0:T(8,128)S(1)} %slice_bitcast_fusion), channel_id=1, source_target_pairs={{0,16},{1,17},{2,18},{3,19},{4,20},{5,21},{6,22},{7,23},{8,24},{9,... | collective-permute-start | bytes 4718600 | tf_op jit(solution)/shard_map/ppermute | solution.py:22
  153.0 6.5 %collective-permute-start.10 = (f32[384,1024]{1,0:T(8,128)S(1)}, f32[384,1024]{1,0:T(8,128)S(1)}, u32[]{:S(2)}, u32[]{:S(2)}) collective-permute-start(f32[384,1024]{1,0:T(8,128)S(1)} %get-tuple-element.13), channel_id=1, source_target_pairs={{0,16},{1,17},{2,18},{3,19},{4,20},{5,21},{6,22},{7,23},{8,24},{9,... | collective-permute-start | bytes 4718600 | tf_op jit(solution)/shard_map/ppermute | solution.py:22
  159.5 1.3 copy-start.4
  164.1 2.3 %copy-start.3 = (f32[384,768]{0,1:T(8,128)}, f32[384,768]{0,1:T(8,128)S(1)}, u32[]{:S(2)}) copy-start(f32[384,768]{0,1:T(8,128)S(1)} %compare_select_fusion) | copy-start | bytes 3538948
  190.9 14.3 %all-to-all-start.1 = ((f32[4,24,1024]{2,1,0:T(8,128)}), f32[4,24,1024]{2,1,0:T(8,128)S(1)}, u32[]{:S(2)}, u32[]{:S(2)}) async-start(f32[4,24,1024]{2,1,0:T(8,128)} %bitcast.8), calls=%async_computation.1 | async-start | bytes 786432 | tf_op jit(solution)/shard_map/all_to_all | solution.py:89
Sparse Core Ops, SparseCore 0:
  87.6 49.7 all-gather.1

commit v5 on v3

--- a/solution.py
+++ b/solution.py
@@ -42,10 +42,10 @@
     return permute(v, move)
 
 
-def transpose_in_plane(v):
+def transpose_in_plane(v, flip):
     def move(y, zh, c, x, zl):
         p = (y - c) % 8
-        return (y, zl % 2, c, (p // 2 + x) % 4, 2 * (p % 2 ^ zl // 2) + zh)
+        return (y, zl % 2, c, (p // 2 + x) % 4, 2 * (p % 2 ^ zl // 2) + (zh ^ flip))
 
     return permute(v, move)
 
@@ -142,11 +142,15 @@
     mine = sums(pair) + passed
     passed = pair_swap(take(mine, (1 - odd) * block, block), "y", 0)
     product = take(mine, odd * block, block) + passed
-    product = product + swap_zh(product)
-
-    own = take(product, zh * (block // 2), block // 2)
+    half_block = block // 2
+    parts = [take(product, (zh ^ f) * half_block, half_block) for f in range(2)]
+    product, *parts = together(product, *parts)
+    moved = [transpose_in_plane(v, f) for f, v in enumerate(parts)]
+    zh_got, *moved = together(swap_zh(product), *moved)
+    own = moved[0] + moved[1]
+    product = product + zh_got
     product_half = lax.all_gather(product, "y", axis=0, tiled=True)
-    own = transpose_along_y(transpose_in_plane(own))
+    own = transpose_along_y(own)
     own = lax.all_gather(own, "zl", axis=0, tiled=True)
     own = in_pair(own[:block], own[block:], row_chip // 2 % 2)
     own, data_half = together(own, data_half)

time: 213 us -> 213 us (level)
  the two profiles are of different devices: /device:TPU:40 before, /device:TPU:8 now
where the time goes in v5:
time: 213 us; the launch traced here: 212 us
  starting transfers between devices  64.7 us (30%)
  waiting for transfers between devices  55.1 us (26%)
  blocking collectives  44 us (21%)
  between operations  14.8 us (7%)
  matrix products  14.6 us (7%)
  local copies, waits for them, and re-layouts  11.7 us (5%)
  other arithmetic  7.48 us (4%)
    ppermute x14, starting transfers between devices, permute(): return lax.ppermute(v, AXES, pairs)  59.5 us
    ppermute x14, waiting for transfers between devices, permute(): return lax.ppermute(v, AXES, pairs)  43.2 us
    all_to_all x1, blocking collectives, scatter_sum(): parts = lax.all_to_all(v.reshape(n, -1, v.shape[1]), axis, 0, 0, tiled=True)  24.3 us
    all_gather x1, blocking collectives, on_device(): own = lax.all_gather(own, 'zl', axis=0, tiled=True)  19.8 us
    dot_general x5, matrix products, dot(): lax.dot_general(a, b, (contract, ((), ())), precision=PREC, preferred_ele...  14.6 us
    all_to_all x1, waiting for transfers between devices, scatter_sum(): parts = lax.all_to_all(v.reshape(n, -1, v.shape[1]), axis, 0, 0, tiled=True)  8.58 us
    unnamed x14, local copies, waits for them, and re-layouts  7.56 us
    all_to_all x1, starting transfers between devices, scatter_sum(): parts = lax.all_to_all(v.reshape(n, -1, v.shape[1]), axis, 0, 0, tiled=True)  5.08 us
  transfers between devices with their start and end apart: 17, of which 11 were waited for; matrix products, arithmetic and copies ran while one was open for 8% of the time, Pallas kernels for 0%

profile of v5, /device:TPU:8, one launch (start us, length us, event | category | flops | bytes accessed | tf_op | source)
XLA Modules:
  0.0 212.3 jit_solution(14149006656775878083)
XLA Ops:
  8.6 3.7 %fusion.6 = f32[384,1024]{1,0:T(8,128)} fusion(f32[384,1024]{1,0:T(8,128)S(1)} %copy-done, f32[384,768]{1,0:T(8,128)} %param.2, s32[]{:T(128)S(6)} %select_n.168), kind=kOutput, calls=%fused_computation.12 | convolution fusion | flops 905969664 | bytes 3735556 | tf_op jit(solution)/shard_map/dot_general | solution.py:104
  12.3 1.9 collective-permute-start
  14.3 2.5 %fusion.8 = f32[384,1024]{1,0:T(8,128)S(1)} fusion(f32[384,1024]{1,0:T(8,128)S(1)} %copy-done, f32[384,768]{1,0:T(8,128)} %param.2, s32[]{:T(128)S(6)} %select_n.163), kind=kOutput, calls=%fused_computation.14 | convolution fusion | flops 905969664 | bytes 3735556 | tf_op jit(solution)/shard_map/dot_general | solution.py:104
  19.0 3.5 %collective-permute-start.1 = (f32[96,1024]{1,0:T(8,128)S(1)}, f32[96,1024]{1,0:T(8,128)}, u32[]{:S(2)}, u32[]{:S(2)}) collective-permute-start(f32[96,1024]{1,0:T(8,128)S(1)} %dynamic-slice_add_fusion), channel_id=1, source_target_pairs={{0,448},{1,449},{2,450},{3,451},{4,452},{5,453},{6,454},{7,455},{8... | collective-permute-start | bytes 1179656 | tf_op jit(solution)/shard_map/ppermute | solution.py:22
  22.5 6.2 %collective-permute-done.1 = f32[96,1024]{1,0:T(8,128)} collective-permute-done((f32[96,1024]{1,0:T(8,128)S(1)}, f32[96,1024]{1,0:T(8,128)}, u32[]{:S(2)}, u32[]{:S(2)}) %collective-permute-start.1) | collective-permute-done | bytes 393248 | tf_op jit(solution)/shard_map/ppermute | solution.py:22
  29.9 8.9 %collective-permute-start.2 = (f32[96,1024]{1,0:T(8,128)S(1)}, f32[96,1024]{1,0:T(8,128)}, u32[]{:S(2)}, u32[]{:S(2)}) collective-permute-start(f32[96,1024]{1,0:T(8,128)S(1)} %add_add_fusion), channel_id=1, source_target_pairs={{0,64},{1,65},{2,66},{3,67},{4,68},{5,69},{6,70},{7,71},{8,72},{9,... | collective-permute-start | bytes 1179656 | tf_op jit(solution)/shard_map/ppermute | solution.py:22
  38.9 3.2 %collective-permute-start.3 = (f32[48,1024]{1,0:T(8,128)}, f32[48,1024]{1,0:T(8,128)}, u32[]{:S(2)}, u32[]{:S(2)}) collective-permute-start(f32[48,1024]{1,0:T(8,128)} %constant_dynamic-slice_fusion.3), channel_id=1, source_target_pairs={{0,0},{1,32},{2,64},{3,96},{4,128},{5,160},{6,192},{7,224},{8,256}... | collective-permute-start | bytes 589832 | tf_op jit(solution)/shard_map/ppermute | solution.py:22
  42.1 10.6 %collective-permute-done.2 = f32[96,1024]{1,0:T(8,128)} collective-permute-done((f32[96,1024]{1,0:T(8,128)S(1)}, f32[96,1024]{1,0:T(8,128)}, u32[]{:S(2)}, u32[]{:S(2)}) %collective-permute-start.2) | collective-permute-done | bytes 393248 | tf_op jit(solution)/shard_map/ppermute | solution.py:22
  54.0 1.9 collective-permute-start.4
  56.0 8.5 %collective-permute-done.4 = f32[96,1024]{1,0:T(8,128)} collective-permute-done((f32[96,1024]{1,0:T(8,128)S(1)}, f32[96,1024]{1,0:T(8,128)}, u32[]{:S(2)}, u32[]{:S(2)}) %collective-permute-start.4) | collective-permute-done | bytes 393248 | tf_op jit(solution)/shard_map/ppermute | solution.py:22
  65.7 3.5 %collective-permute-start.5 = (f32[48,1024]{1,0:T(8,128)S(1)}, f32[48,1024]{1,0:T(8,128)S(1)}, u32[]{:S(2)}, u32[]{:S(2)}) collective-permute-start(f32[48,1024]{1,0:T(8,128)S(1)} %constant_dynamic-slice_fusion.2), channel_id=1, source_target_pairs={{0,64},{1,65},{2,66},{3,67},{4,68},{5,69},{6,70},{7,71},{8,72},{9,... | collective-permute-start | bytes 589832 | tf_op jit(solution)/shard_map/ppermute | solution.py:22
  69.2 6.1 %collective-permute-done.5 = f32[48,1024]{1,0:T(8,128)S(1)} collective-permute-done((f32[48,1024]{1,0:T(8,128)S(1)}, f32[48,1024]{1,0:T(8,128)S(1)}, u32[]{:S(2)}, u32[]{:S(2)}) %collective-permute-start.5) | collective-permute-done | bytes 196640 | tf_op jit(solution)/shard_map/ppermute | solution.py:22
  75.3 4.6 %collective-permute-start.6 = (f32[48,1024]{1,0:T(8,128)S(1)}, f32[48,1024]{1,0:T(8,128)S(1)}, u32[]{:S(2)}, u32[]{:S(2)}) collective-permute-start(f32[48,1024]{1,0:T(8,128)S(1)} %dynamic-slice_add_fusion.1), channel_id=1, source_target_pairs={{0,32},{1,33},{2,34},{3,35},{4,36},{5,37},{6,38},{7,39},{8,40},{9,... | collective-permute-start | bytes 589832 | tf_op jit(solution)/shard_map/ppermute | solution.py:22
  80.0 7.7 %collective-permute-start.7 = (f32[24,1024]{1,0:T(8,128)S(1)}, f32[24,1024]{1,0:T(8,128)S(1)}, u32[]{:S(2)}, u32[]{:S(2)}) collective-permute-start(f32[24,1024]{1,0:T(8,128)S(1)} %get-tuple-element.18), channel_id=1, source_target_pairs={{0,0},{1,32},{2,2},{3,34},{4,4},{5,36},{6,6},{7,38},{8,8},{9,40},{... | collective-permute-start | bytes 294920 | tf_op jit(solution)/shard_map/ppermute | solution.py:22
  87.7 1.9 collective-permute-start.8
  89.6 3.6 %collective-permute-done.7 = f32[24,1024]{1,0:T(8,128)S(1)} collective-permute-done((f32[24,1024]{1,0:T(8,128)S(1)}, f32[24,1024]{1,0:T(8,128)S(1)}, u32[]{:S(2)}, u32[]{:S(2)}) %collective-permute-start.7) | collective-permute-done | bytes 98336 | tf_op jit(solution)/shard_map/ppermute | solution.py:22
  93.2 4.2 %collective-permute-done.8 = f32[24,1024]{1,0:T(8,128)S(1)} collective-permute-done((f32[24,1024]{1,0:T(8,128)S(1)}, f32[24,1024]{1,0:T(8,128)S(1)}, u32[]{:S(2)}, u32[]{:S(2)}) %collective-permute-start.8) | collective-permute-done | bytes 98336 | tf_op jit(solution)/shard_map/ppermute | solution.py:22
  99.0 19.8 %all_gather.10 = f32[96,1024]{1,0:T(8,128)S(1)} all-gather(f32[24,1024]{1,0:T(8,128)S(1)} %collective-permute-done.10), channel_id=1, replica_groups=mesh['y'=8,'zh'=2,'c'=2,'x'=4,'zl'=4] {'zl'}, dimensions={0}, use_global_device_ids=true | all-gather | bytes 491520 | tf_op jit(solution)/shard_map/all_gather | solution.py:154
  118.9 7.5 %collective-permute-start.11 = (f32[96,1024]{1,0:T(8,128)S(1)}, f32[96,1024]{1,0:T(8,128)S(1)}, u32[]{:S(2)}, u32[]{:S(2)}) collective-permute-start(f32[96,1024]{1,0:T(8,128)S(1)} %maximum_select_fusion.2), channel_id=1, source_target_pairs={{0,4},{1,5},{2,6},{3,7},{4,0},{5,1},{6,2},{7,3},{8,12},{9,13},{10,... | collective-permute-start | bytes 1179656 | tf_op jit(solution)/shard_map/ppermute | solution.py:22
  128.0 1.9 collective-permute-start.13
  129.9 2.3 %collective-permute-done.11 = f32[96,1024]{1,0:T(8,128)S(1)} collective-permute-done((f32[96,1024]{1,0:T(8,128)S(1)}, f32[96,1024]{1,0:T(8,128)S(1)}, u32[]{:S(2)}, u32[]{:S(2)}) %collective-permute-start.11) | collective-permute-done | bytes 393248 | tf_op jit(solution)/shard_map/ppermute | solution.py:22
  132.2 9.9 %collective-permute-start.12 = (f32[192,1024]{1,0:T(8,128)S(1)}, f32[192,1024]{1,0:T(8,128)S(1)}, u32[]{:S(2)}, u32[]{:S(2)}) collective-permute-start(f32[192,1024]{1,0:T(8,128)S(1)} %maximum_select_fusion.1), channel_id=1, source_target_pairs={{0,12},{1,13},{2,14},{3,15},{4,8},{5,9},{6,10},{7,11},{8,4},{9,5},... | collective-permute-start | bytes 2359304 | tf_op jit(solution)/shard_map/ppermute | solution.py:22
  142.2 3.3 %all-gather.3.cloned.1.call-done = f32[384,1024]{1,0:T(8,128)} async-done(((f32[48,1024]{1,0:T(8,128)}), f32[384,1024]{1,0:T(8,128)}) %all-gather.3.cloned.1.call-update) | async-done | bytes 1572880 | tf_op jit(solution)/shard_map/all_gather | solution.py:152
  147.8 2.2 %collective-permute-start.9 = (f32[384,1024]{1,0:T(8,128)S(1)}, f32[384,1024]{1,0:T(8,128)S(1)}, u32[]{:S(2)}, u32[]{:S(2)}) collective-permute-start(f32[384,1024]{1,0:T(8,128)S(1)} %get-tuple-element.31), channel_id=1, source_target_pairs={{0,16},{1,17},{2,18},{3,19},{4,20},{5,21},{6,22},{7,23},{8,24},{9,... | collective-permute-start | bytes 4718600 | tf_op jit(solution)/shard_map/ppermute | solution.py:22
  152.2 1.5 constant_dynamic-update-slice_fusion.2
  153.8 2.7 %fusion.13 = f32[384,768]{0,1:T(8,128)S(1)} fusion(f32[384,1024]{1,0:T(8,128)S(1)} %slice_dynamic-update-slice_fusion, f32[768,1024]{1,0:T(8,128)S(1)} %constant_dynamic-update-slice_fusion.2), kind=kOutput, calls=%fused_computation.39 | convolution fusion | flops 1811939328 | bytes 5898240 | tf_op jit(solution)/shard_map/dot_general | solution.py:104
  157.7 3.3 %compare_select_fusion = f32[384,768]{0,1:T(8,128)S(1)} fusion(f32[384,768]{0,1:T(8,128)S(1)} %copy-done.5, f32[384,768]{0,1:T(8,128)S(1)} %fusion.13, f32[768,1024]{1,0:T(8,128)S(1)} %constant_dynamic-update-slice_fusion, f32[384,1024]{1,0:T(8,128)S(1)} %copy-done, s32[384]{0:T(512)S(1)} %iota_add_fusion.1, s32[768]{0:T(1024)S(1)} %iota_add_fusion), kind=kOutput, calls=%fused_computation | convolution fusion | flops 1816363008 | bytes 8262144 | tf_op jit(solution)/shard_map/dot_general | solution.py:104
  161.1 2.3 %fusion.14 = f32[384,1024]{1,0:T(8,128)S(1)} fusion(f32[384,768]{0,1:T(8,128)S(1)} %compare_select_fusion, f32[768,1024]{1,0:T(8,128)S(1)} %constant_dynamic-update-slice_fusion.2), kind=kOutput, calls=%fused_computation.40 | convolution fusion | flops 1811939328 | bytes 5898240 | tf_op jit(solution)/shard_map/dot_general | solution.py:104
  163.4 24.3 %all_to_all.10 = f32[4,96,1024]{2,1,0:T(8,128)S(1)} all-to-all(f32[4,96,1024]{2,1,0:T(8,128)S(1)} %bitcast.24), channel_id=1, replica_groups=mesh['y'=8,'zh'=2,'c'=2,'x'=4,'zl'=4] {'x'}, dimensions={0} | all-to-all | bytes 3145728 | tf_op jit(solution)/shard_map/all_to_all | solution.py:89
  188.5 5.1 %all-to-all-start.1 = ((f32[4,24,1024]{2,1,0:T(8,128)}), f32[4,24,1024]{2,1,0:T(8,128)S(1)}, u32[]{:S(2)}, u32[]{:S(2)}) async-start(f32[4,24,1024]{2,1,0:T(8,128)} %bitcast.2), calls=%async_computation.1 | async-start | bytes 786432 | tf_op jit(solution)/shard_map/all_to_all | solution.py:89
  193.6 2.7 %copy.11 = f32[384,768]{1,0:T(8,128)} copy(f32[384,768]{0,1:T(8,128)} %copy-done.3) | data formatting | bytes 2359296
  196.3 8.6 %all-to-all-done.1 = f32[4,24,1024]{2,1,0:T(8,128)S(1)} async-done(((f32[4,24,1024]{2,1,0:T(8,128)}), f32[4,24,1024]{2,1,0:T(8,128)S(1)}, u32[]{:S(2)}, u32[]{:S(2)}) %all-to-all-start.1) | async-done | bytes 393248 | tf_op jit(solution)/shard_map/all_to_all | solution.py:89
  (57 shorter events, 17.5 us)
Async XLA Ops:
  7.2 1.4 copy-start
  7.2 111.7 %all-gather.5.cloned.1.call-start = ((), (), s32[]{:S(2)}) async-start(), calls=%async_computation.3 | async-start | bytes 1769472 | tf_op jit(solution)/shard_map/all_gather | solution.py:140
  12.3 5.6 %collective-permute-start = (f32[384,1024]{1,0:T(8,128)}, f32[384,1024]{1,0:T(8,128)}, u32[]{:S(2)}, u32[]{:S(2)}) collective-permute-start(f32[384,1024]{1,0:T(8,128)} %fusion.6), channel_id=1, source_target_pairs={{0,16},{1,17},{2,18},{3,19},{4,20},{5,21},{6,22},{7,23},{8,24},{9,... | collective-permute-start | bytes 4718600 | tf_op jit(solution)/shard_map/ppermute | solution.py:22
  19.0 9.8 %collective-permute-start.1 = (f32[96,1024]{1,0:T(8,128)S(1)}, f32[96,1024]{1,0:T(8,128)}, u32[]{:S(2)}, u32[]{:S(2)}) collective-permute-start(f32[96,1024]{1,0:T(8,128)S(1)} %dynamic-slice_add_fusion), channel_id=1, source_target_pairs={{0,448},{1,449},{2,450},{3,451},{4,452},{5,453},{6,454},{7,455},{8... | collective-permute-start | bytes 1179656 | tf_op jit(solution)/shard_map/ppermute | solution.py:22
  29.9 22.8 %collective-permute-start.2 = (f32[96,1024]{1,0:T(8,128)S(1)}, f32[96,1024]{1,0:T(8,128)}, u32[]{:S(2)}, u32[]{:S(2)}) collective-permute-start(f32[96,1024]{1,0:T(8,128)S(1)} %add_add_fusion), channel_id=1, source_target_pairs={{0,64},{1,65},{2,66},{3,67},{4,68},{5,69},{6,70},{7,71},{8,72},{9,... | collective-permute-start | bytes 1179656 | tf_op jit(solution)/shard_map/ppermute | solution.py:22
  38.9 15.0 %collective-permute-start.3 = (f32[48,1024]{1,0:T(8,128)}, f32[48,1024]{1,0:T(8,128)}, u32[]{:S(2)}, u32[]{:S(2)}) collective-permute-start(f32[48,1024]{1,0:T(8,128)} %constant_dynamic-slice_fusion.3), channel_id=1, source_target_pairs={{0,0},{1,32},{2,64},{3,96},{4,128},{5,160},{6,192},{7,224},{8,256}... | collective-permute-start | bytes 589832 | tf_op jit(solution)/shard_map/ppermute | solution.py:22
  54.0 91.5 %all-gather.3.cloned.1.call-start = ((), (), s32[]{:S(2)}) async-start(), calls=%async_computation.2 | async-start | bytes 1769472 | tf_op jit(solution)/shard_map/all_gather | solution.py:152
  54.0 10.5 %collective-permute-start.4 = (f32[96,1024]{1,0:T(8,128)S(1)}, f32[96,1024]{1,0:T(8,128)}, u32[]{:S(2)}, u32[]{:S(2)}) collective-permute-start(f32[96,1024]{1,0:T(8,128)S(1)} %add_add_fusion.1), channel_id=1, source_target_pairs={{0,448},{1,449},{2,450},{3,451},{4,452},{5,453},{6,454},{7,455},{8... | collective-permute-start | bytes 1179656 | tf_op jit(solution)/shard_map/ppermute | solution.py:22
  65.7 9.5 %collective-permute-start.5 = (f32[48,1024]{1,0:T(8,128)S(1)}, f32[48,1024]{1,0:T(8,128)S(1)}, u32[]{:S(2)}, u32[]{:S(2)}) collective-permute-start(f32[48,1024]{1,0:T(8,128)S(1)} %constant_dynamic-slice_fusion.2), channel_id=1, source_target_pairs={{0,64},{1,65},{2,66},{3,67},{4,68},{5,69},{6,70},{7,71},{8,72},{9,... | collective-permute-start | bytes 589832 | tf_op jit(solution)/shard_map/ppermute | solution.py:22
  75.3 22.1 %collective-permute-start.6 = (f32[48,1024]{1,0:T(8,128)S(1)}, f32[48,1024]{1,0:T(8,128)S(1)}, u32[]{:S(2)}, u32[]{:S(2)}) collective-permute-start(f32[48,1024]{1,0:T(8,128)S(1)} %dynamic-slice_add_fusion.1), channel_id=1, source_target_pairs={{0,32},{1,33},{2,34},{3,35},{4,36},{5,37},{6,38},{7,39},{8,40},{9,... | collective-permute-start | bytes 589832 | tf_op jit(solution)/shard_map/ppermute | solution.py:22
  80.0 13.2 %collective-permute-start.7 = (f32[24,1024]{1,0:T(8,128)S(1)}, f32[24,1024]{1,0:T(8,128)S(1)}, u32[]{:S(2)}, u32[]{:S(2)}) collective-permute-start(f32[24,1024]{1,0:T(8,128)S(1)} %get-tuple-element.18), channel_id=1, source_target_pairs={{0,0},{1,32},{2,2},{3,34},{4,4},{5,36},{6,6},{7,38},{8,8},{9,40},{... | collective-permute-start | bytes 294920 | tf_op jit(solution)/shard_map/ppermute | solution.py:22
  87.7 9.7 %collective-permute-start.8 = (f32[24,1024]{1,0:T(8,128)S(1)}, f32[24,1024]{1,0:T(8,128)S(1)}, u32[]{:S(2)}, u32[]{:S(2)}) collective-permute-start(f32[24,1024]{1,0:T(8,128)S(1)} %get-tuple-element.19), channel_id=1, source_target_pairs={{0,1},{1,33},{2,3},{3,35},{4,5},{5,37},{6,7},{7,39},{8,9},{9,41},{... | collective-permute-start | bytes 294920 | tf_op jit(solution)/shard_map/ppermute | solution.py:22
  98.1 28.4 %copy-start.2 = (f32[384,768]{1,0:T(8,128)S(1)}, f32[384,768]{1,0:T(8,128)}, u32[]{:S(2)}) copy-start(f32[384,768]{1,0:T(8,128)} %param.2) | copy-start | bytes 3538948
  98.2 0.8 collective-permute-start.10
  118.9 13.2 %collective-permute-start.11 = (f32[96,1024]{1,0:T(8,128)S(1)}, f32[96,1024]{1,0:T(8,128)S(1)}, u32[]{:S(2)}, u32[]{:S(2)}) collective-permute-start(f32[96,1024]{1,0:T(8,128)S(1)} %maximum_select_fusion.2), channel_id=1, source_target_pairs={{0,4},{1,5},{2,6},{3,7},{4,0},{5,1},{6,2},{7,3},{8,12},{9,13},{10,... | collective-permute-start | bytes 1179656 | tf_op jit(solution)/shard_map/ppermute | solution.py:22
  128.0 24.3 %collective-permute-start.13 = (f32[384,1024]{1,0:T(8,128)}, f32[384,1024]{1,0:T(8,128)}, u32[]{:S(2)}, u32[]{:S(2)}) collective-permute-start(f32[384,1024]{1,0:T(8,128)} %all-gather.5.cloned.1.call-done), channel_id=1, source_target_pairs={{0,16},{1,17},{2,18},{3,19},{4,20},{5,21},{6,22},{7,23},{8,24},{9,... | collective-permute-start | bytes 4718600 | tf_op jit(solution)/shard_map/ppermute | solution.py:22
  132.2 19.9 %collective-permute-start.12 = (f32[192,1024]{1,0:T(8,128)S(1)}, f32[192,1024]{1,0:T(8,128)S(1)}, u32[]{:S(2)}, u32[]{:S(2)}) collective-permute-start(f32[192,1024]{1,0:T(8,128)S(1)} %maximum_select_fusion.1), channel_id=1, source_target_pairs={{0,12},{1,13},{2,14},{3,15},{4,8},{5,9},{6,10},{7,11},{8,4},{9,5},... | collective-permute-start | bytes 2359304 | tf_op jit(solution)/shard_map/ppermute | solution.py:22
  145.4 1.4 copy-start.1
  145.4 1.8 slice-start
  145.4 1.9 slice-start.1
  147.8 2.6 %copy-start.4 = (f32[384,1024]{1,0:T(8,128)S(1)}, f32[384,1024]{1,0:T(8,128)}, u32[]{:S(2)}) copy-start(f32[384,1024]{1,0:T(8,128)} %all-gather.5.cloned.1.call-done) | copy-start | bytes 4718596
  147.8 8.6 %collective-permute-start.9 = (f32[384,1024]{1,0:T(8,128)S(1)}, f32[384,1024]{1,0:T(8,128)S(1)}, u32[]{:S(2)}, u32[]{:S(2)}) collective-permute-start(f32[384,1024]{1,0:T(8,128)S(1)} %get-tuple-element.31), channel_id=1, source_target_pairs={{0,16},{1,17},{2,18},{3,19},{4,20},{5,21},{6,22},{7,23},{8,24},{9,... | collective-permute-start | bytes 4718600 | tf_op jit(solution)/shard_map/ppermute | solution.py:22
  156.5 1.3 copy-start.5
  161.1 2.3 %copy-start.3 = (f32[384,768]{0,1:T(8,128)}, f32[384,768]{0,1:T(8,128)S(1)}, u32[]{:S(2)}) copy-start(f32[384,768]{0,1:T(8,128)S(1)} %compare_select_fusion) | copy-start | bytes 3538948
  188.5 16.3 %all-to-all-start.1 = ((f32[4,24,1024]{2,1,0:T(8,128)}), f32[4,24,1024]{2,1,0:T(8,128)S(1)}, u32[]{:S(2)}, u32[]{:S(2)}) async-start(f32[4,24,1024]{2,1,0:T(8,128)} %bitcast.2), calls=%async_computation.1 | async-start | bytes 786432 | tf_op jit(solution)/shard_map/all_to_all | solution.py:89
Sparse Core Ops, SparseCore 0:
  54.1 45.2 all-gather.4
  101.4 43.9 all-gather.2

commit v6 on v5

--- a/solution.py
+++ b/solution.py
@@ -136,8 +136,7 @@
     passed = pair_swap(sending, "y", 1)
     data = transpose_data(share)
     passed = pair_swap(sums(near) + passed, "y", 0)
-    sending, data = together(sums(other) + passed, data)
-    data_half = lax.all_gather(data, "y", axis=0, tiled=True)
+    sending = sums(other) + passed
     passed = pair_swap(sending, "y", 1)
     mine = sums(pair) + passed
     passed = pair_swap(take(mine, (1 - odd) * block, block), "y", 0)
@@ -149,15 +148,16 @@
     zh_got, *moved = together(swap_zh(product), *moved)
     own = moved[0] + moved[1]
     product = product + zh_got
-    product_half = lax.all_gather(product, "y", axis=0, tiled=True)
+    pieces = lax.all_gather(jnp.stack([product, data]), "y", axis=1, tiled=True)
     own = transpose_along_y(own)
     own = lax.all_gather(own, "zl", axis=0, tiled=True)
     own = in_pair(own[:block], own[block:], row_chip // 2 % 2)
-    own, data_half = together(own, data_half)
     x_odd = (x - c) % 2
     rows0 = in_pair(own, pair_swap(own, "x", 0), x_odd)
-    data_cols = both_cores(data_half, c)
     rows1 = pair_swap(rows0, "x", 1)
+    pieces, _ = together(pieces, rows0)
+    data_cols = both_cores(pieces[1], c)
+    product_half = pieces[0]
     shifted = jnp.concatenate([product_half[block:], product_half[:block]])
     product_cols = both_cores(jnp.where(c == 0, product_half, shifted), c)
     product_rows = jnp.zeros_like(sample_rows)

time: 213 us -> 217 us (1.019)
  starting transfers between devices: 64.7 us -> 69.2 us
  waiting for transfers between devices: 55.1 us -> 52.5 us
    ppermute x14, waiting for transfers between devices: 43.2 us -> 34.4 us  [permute(): return lax.ppermute(v, AXES, pairs)]
    all_gather x2 -> x1, waiting for transfers between devices: 3.27 us -> 10.3 us  [on_device(): pieces = lax.all_gather(jnp.stack([product, data]), 'y', axis=1, tiled=True)]
    ppermute x14, starting transfers between devices: 59.5 us -> 64 us  [permute(): return lax.ppermute(v, AXES, pairs)]
    unnamed x14 -> x12, local copies, waits for them, and re-layouts: 7.56 us -> 6.54 us
  transfers between devices with their start and end apart: 17 -> 16, of which waited for: 11 -> 10; matrix products, arithmetic and copies ran while one was open for 8% -> 7% of each run, Pallas kernels for 0% -> 0%
where the time goes in v6:
time: 217 us; the launch traced here: 216 us
  starting transfers between devices  69.2 us (32%)
  waiting for transfers between devices  52.5 us (24%)
  blocking collectives  45 us (21%)
  between operations  14.8 us (7%)
  matrix products  14.5 us (7%)
  local copies, waits for them, and re-layouts  12.9 us (6%)
  other arithmetic  7.59 us (3%)
    ppermute x14, starting transfers between devices, permute(): return lax.ppermute(v, AXES, pairs)  64 us
    ppermute x14, waiting for transfers between devices, permute(): return lax.ppermute(v, AXES, pairs)  34.4 us
    all_to_all x1, blocking collectives, scatter_sum(): parts = lax.all_to_all(v.reshape(n, -1, v.shape[1]), axis, 0, 0, tiled=True)  24.9 us
    all_gather x1, blocking collectives, on_device(): own = lax.all_gather(own, 'zl', axis=0, tiled=True)  20 us
    dot_general x5, matrix products, dot(): lax.dot_general(a, b, (contract, ((), ())), precision=PREC, preferred_ele...  14.5 us
    all_gather x1, waiting for transfers between devices, on_device(): pieces = lax.all_gather(jnp.stack([product, data]), 'y', axis=1, tiled=True)  10.3 us
    all_to_all x1, waiting for transfers between devices, scatter_sum(): parts = lax.all_to_all(v.reshape(n, -1, v.shape[1]), axis, 0, 0, tiled=True)  7.76 us
    unnamed x12, local copies, waits for them, and re-layouts  6.54 us
  transfers between devices with their start and end apart: 16, of which 10 were waited for; matrix products, arithmetic and copies ran while one was open for 7% of the time, Pallas kernels for 0%

profile of v6, /device:TPU:8, one launch (start us, length us, event | category | flops | bytes accessed | tf_op | source)
XLA Modules:
  0.0 216.4 jit_solution(513794312542049814)
XLA Ops:
  8.6 3.7 %fusion.6 = f32[384,1024]{1,0:T(8,128)} fusion(f32[384,1024]{1,0:T(8,128)S(1)} %copy-done, f32[384,768]{1,0:T(8,128)} %param.2, s32[]{:T(128)S(6)} %select_n.168), kind=kOutput, calls=%fused_computation.14 | convolution fusion | flops 905969664 | bytes 3735556 | tf_op jit(solution)/shard_map/dot_general | solution.py:104
  12.2 1.9 collective-permute-start
  14.2 2.5 %fusion.8 = f32[384,1024]{1,0:T(8,128)S(1)} fusion(f32[384,1024]{1,0:T(8,128)S(1)} %copy-done, f32[384,768]{1,0:T(8,128)} %param.2, s32[]{:T(128)S(6)} %select_n.163), kind=kOutput, calls=%fused_computation.16 | convolution fusion | flops 905969664 | bytes 3735556 | tf_op jit(solution)/shard_map/dot_general | solution.py:104
  18.9 3.5 %collective-permute-start.1 = (f32[96,1024]{1,0:T(8,128)S(1)}, f32[96,1024]{1,0:T(8,128)}, u32[]{:S(2)}, u32[]{:S(2)}) collective-permute-start(f32[96,1024]{1,0:T(8,128)S(1)} %dynamic-slice_add_fusion), channel_id=1, source_target_pairs={{0,448},{1,449},{2,450},{3,451},{4,452},{5,453},{6,454},{7,455},{8... | collective-permute-start | bytes 1179656 | tf_op jit(solution)/shard_map/ppermute | solution.py:22
  22.4 6.2 %collective-permute-done.1 = f32[96,1024]{1,0:T(8,128)} collective-permute-done((f32[96,1024]{1,0:T(8,128)S(1)}, f32[96,1024]{1,0:T(8,128)}, u32[]{:S(2)}, u32[]{:S(2)}) %collective-permute-start.1) | collective-permute-done | bytes 393248 | tf_op jit(solution)/shard_map/ppermute | solution.py:22
  29.9 8.9 %collective-permute-start.2 = (f32[96,1024]{1,0:T(8,128)S(1)}, f32[96,1024]{1,0:T(8,128)}, u32[]{:S(2)}, u32[]{:S(2)}) collective-permute-start(f32[96,1024]{1,0:T(8,128)S(1)} %add_add_fusion), channel_id=1, source_target_pairs={{0,64},{1,65},{2,66},{3,67},{4,68},{5,69},{6,70},{7,71},{8,72},{9,... | collective-permute-start | bytes 1179656 | tf_op jit(solution)/shard_map/ppermute | solution.py:22
  38.8 5.8 %collective-permute-done.2 = f32[96,1024]{1,0:T(8,128)} collective-permute-done((f32[96,1024]{1,0:T(8,128)S(1)}, f32[96,1024]{1,0:T(8,128)}, u32[]{:S(2)}, u32[]{:S(2)}) %collective-permute-start.2) | collective-permute-done | bytes 393248 | tf_op jit(solution)/shard_map/ppermute | solution.py:22
  45.9 1.9 collective-permute-start.3
  47.8 7.8 %collective-permute-done.3 = f32[96,1024]{1,0:T(8,128)} collective-permute-done((f32[96,1024]{1,0:T(8,128)S(1)}, f32[96,1024]{1,0:T(8,128)}, u32[]{:S(2)}, u32[]{:S(2)}) %collective-permute-start.3) | collective-permute-done | bytes 393248 | tf_op jit(solution)/shard_map/ppermute | solution.py:22
  56.8 5.1 %collective-permute-start.4 = (f32[48,1024]{1,0:T(8,128)S(1)}, f32[48,1024]{1,0:T(8,128)S(1)}, u32[]{:S(2)}, u32[]{:S(2)}) collective-permute-start(f32[48,1024]{1,0:T(8,128)S(1)} %constant_dynamic-slice_fusion.2), channel_id=1, source_target_pairs={{0,64},{1,65},{2,66},{3,67},{4,68},{5,69},{6,70},{7,71},{8,72},{9,... | collective-permute-start | bytes 589832 | tf_op jit(solution)/shard_map/ppermute | solution.py:22
  62.0 3.6 %collective-permute-done.4 = f32[48,1024]{1,0:T(8,128)S(1)} collective-permute-done((f32[48,1024]{1,0:T(8,128)S(1)}, f32[48,1024]{1,0:T(8,128)S(1)}, u32[]{:S(2)}, u32[]{:S(2)}) %collective-permute-start.4) | collective-permute-done | bytes 196640 | tf_op jit(solution)/shard_map/ppermute | solution.py:22
  65.7 5.8 %collective-permute-start.5 = (f32[48,1024]{1,0:T(8,128)S(1)}, f32[48,1024]{1,0:T(8,128)S(1)}, u32[]{:S(2)}, u32[]{:S(2)}) collective-permute-start(f32[48,1024]{1,0:T(8,128)S(1)} %dynamic-slice_add_fusion.1), channel_id=1, source_target_pairs={{0,32},{1,33},{2,34},{3,35},{4,36},{5,37},{6,38},{7,39},{8,40},{9,... | collective-permute-start | bytes 589832 | tf_op jit(solution)/shard_map/ppermute | solution.py:22
  71.5 4.3 %collective-permute-start.6 = (f32[24,1024]{1,0:T(8,128)S(1)}, f32[24,1024]{1,0:T(8,128)S(1)}, u32[]{:S(2)}, u32[]{:S(2)}) collective-permute-start(f32[24,1024]{1,0:T(8,128)S(1)} %get-tuple-element.13), channel_id=1, source_target_pairs={{0,0},{1,32},{2,2},{3,34},{4,4},{5,36},{6,6},{7,38},{8,8},{9,40},{... | collective-permute-start | bytes 294920 | tf_op jit(solution)/shard_map/ppermute | solution.py:22
  75.8 2.8 %collective-permute-start.7 = (f32[24,1024]{1,0:T(8,128)S(1)}, f32[24,1024]{1,0:T(8,128)S(1)}, u32[]{:S(2)}, u32[]{:S(2)}) collective-permute-start(f32[24,1024]{1,0:T(8,128)S(1)} %get-tuple-element.14), channel_id=1, source_target_pairs={{0,1},{1,33},{2,3},{3,35},{4,5},{5,37},{6,7},{7,39},{8,9},{9,41},{... | collective-permute-start | bytes 294920 | tf_op jit(solution)/shard_map/ppermute | solution.py:22
  78.6 8.1 %collective-permute-start.8 = (f32[48,1024]{1,0:T(8,128)}, f32[48,1024]{1,0:T(8,128)S(1)}, u32[]{:S(2)}, u32[]{:S(2)}) collective-permute-start(f32[48,1024]{1,0:T(8,128)} %constant_dynamic-slice_fusion.3), channel_id=1, source_target_pairs={{0,0},{1,32},{2,64},{3,96},{4,128},{5,160},{6,192},{7,224},{8,256}... | collective-permute-start | bytes 589832 | tf_op jit(solution)/shard_map/ppermute | solution.py:22
  87.1 4.2 %collective-permute-done.8 = f32[48,1024]{1,0:T(8,128)S(1)} collective-permute-done((f32[48,1024]{1,0:T(8,128)}, f32[48,1024]{1,0:T(8,128)S(1)}, u32[]{:S(2)}, u32[]{:S(2)}) %collective-permute-start.8) | collective-permute-done | bytes 196640 | tf_op jit(solution)/shard_map/ppermute | solution.py:22
  93.0 20.0 %all_gather.7 = f32[96,1024]{1,0:T(8,128)S(1)} all-gather(f32[24,1024]{1,0:T(8,128)S(1)} %collective-permute-done.9), channel_id=1, replica_groups=mesh['y'=8,'zh'=2,'c'=2,'x'=4,'zl'=4] {'zl'}, dimensions={0}, use_global_device_ids=true | all-gather | bytes 491520 | tf_op jit(solution)/shard_map/all_gather | solution.py:153
  113.1 6.5 %collective-permute-start.10 = (f32[96,1024]{1,0:T(8,128)S(1)}, f32[96,1024]{1,0:T(8,128)S(1)}, u32[]{:S(2)}, u32[]{:S(2)}) collective-permute-start(f32[96,1024]{1,0:T(8,128)S(1)} %maximum_select_fusion.2), channel_id=1, source_target_pairs={{0,4},{1,5},{2,6},{3,7},{4,0},{5,1},{6,2},{7,3},{8,12},{9,13},{10,... | collective-permute-start | bytes 1179656 | tf_op jit(solution)/shard_map/ppermute | solution.py:22
  121.1 6.1 %collective-permute-done.10 = f32[96,1024]{1,0:T(8,128)S(1)} collective-permute-done((f32[96,1024]{1,0:T(8,128)S(1)}, f32[96,1024]{1,0:T(8,128)S(1)}, u32[]{:S(2)}, u32[]{:S(2)}) %collective-permute-start.10) | collective-permute-done | bytes 393248 | tf_op jit(solution)/shard_map/ppermute | solution.py:22
  127.2 9.6 %collective-permute-start.12 = (f32[192,1024]{1,0:T(8,128)S(1)}, f32[192,1024]{1,0:T(8,128)S(1)}, u32[]{:S(2)}, u32[]{:S(2)}) collective-permute-start(f32[192,1024]{1,0:T(8,128)S(1)} %maximum_select_fusion.1), channel_id=1, source_target_pairs={{0,12},{1,13},{2,14},{3,15},{4,8},{5,9},{6,10},{7,11},{8,4},{9,5},... | collective-permute-start | bytes 2359304 | tf_op jit(solution)/shard_map/ppermute | solution.py:22
  136.8 10.3 %all-gather.2.cloned.1.call-done = f32[2,384,1024]{2,1,0:T(8,128)} async-done(((f32[2,48,1024]{2,1,0:T(8,128)}), f32[2,384,1024]{2,1,0:T(8,128)}) %all-gather.2.cloned.1.call-update) | async-done | bytes 3145744 | tf_op jit(solution)/shard_map/all_gather | solution.py:151
  147.1 1.5 slice_bitcast_fusion.1
  149.5 1.6 slice_bitcast_fusion
  151.1 2.2 %collective-permute-start.13 = (f32[384,1024]{1,0:T(8,128)S(1)}, f32[384,1024]{1,0:T(8,128)S(1)}, u32[]{:S(2)}, u32[]{:S(2)}) collective-permute-start(f32[384,1024]{1,0:T(8,128)S(1)} %slice_bitcast_fusion), channel_id=1, source_target_pairs={{0,16},{1,17},{2,18},{3,19},{4,20},{5,21},{6,22},{7,23},{8,24},{9,... | collective-permute-start | bytes 4718600 | tf_op jit(solution)/shard_map/ppermute | solution.py:22
  154.2 2.6 %collective-permute-start.11 = (f32[384,1024]{1,0:T(8,128)S(1)}, f32[384,1024]{1,0:T(8,128)S(1)}, u32[]{:S(2)}, u32[]{:S(2)}) collective-permute-start(f32[384,1024]{1,0:T(8,128)S(1)} %get-tuple-element.25), channel_id=1, source_target_pairs={{0,16},{1,17},{2,18},{3,19},{4,20},{5,21},{6,22},{7,23},{8,24},{9,... | collective-permute-start | bytes 4718600 | tf_op jit(solution)/shard_map/ppermute | solution.py:22
  158.0 2.7 %fusion.13 = f32[384,768]{0,1:T(8,128)S(1)} fusion(f32[384,1024]{1,0:T(8,128)S(1)} %slice_dynamic-update-slice_fusion, f32[768,1024]{1,0:T(8,128)S(1)} %constant_dynamic-update-slice_fusion.2), kind=kOutput, calls=%fused_computation.44 | convolution fusion | flops 1811939328 | bytes 5898240 | tf_op jit(solution)/shard_map/dot_general | solution.py:104
  162.0 3.3 %compare_select_fusion = f32[384,768]{0,1:T(8,128)S(1)} fusion(f32[384,768]{0,1:T(8,128)S(1)} %copy-done.4, f32[384,768]{0,1:T(8,128)S(1)} %fusion.13, f32[768,1024]{1,0:T(8,128)S(1)} %constant_dynamic-update-slice_fusion, f32[384,1024]{1,0:T(8,128)S(1)} %copy-done, s32[384]{0:T(512)S(1)} %iota_add_fusion.1, s32[768]{0:T(1024)S(1)} %iota_add_fusion), kind=kOutput, calls=%fused_computation | convolution fusion | flops 1816363008 | bytes 8262144 | tf_op jit(solution)/shard_map/dot_general | solution.py:104
  165.3 2.3 %fusion.14 = f32[384,1024]{1,0:T(8,128)S(1)} fusion(f32[384,768]{0,1:T(8,128)S(1)} %compare_select_fusion, f32[768,1024]{1,0:T(8,128)S(1)} %constant_dynamic-update-slice_fusion.2), kind=kOutput, calls=%fused_computation.45 | convolution fusion | flops 1811939328 | bytes 5898240 | tf_op jit(solution)/shard_map/dot_general | solution.py:104
  167.6 24.9 %all_to_all.10 = f32[4,96,1024]{2,1,0:T(8,128)S(1)} all-to-all(f32[4,96,1024]{2,1,0:T(8,128)S(1)} %bitcast.38), channel_id=1, replica_groups=mesh['y'=8,'zh'=2,'c'=2,'x'=4,'zl'=4] {'x'}, dimensions={0} | all-to-all | bytes 3145728 | tf_op jit(solution)/shard_map/all_to_all | solution.py:89
  193.4 5.1 %all-to-all-start.1 = ((f32[4,24,1024]{2,1,0:T(8,128)}), f32[4,24,1024]{2,1,0:T(8,128)S(1)}, u32[]{:S(2)}, u32[]{:S(2)}) async-start(f32[4,24,1024]{2,1,0:T(8,128)} %bitcast.8), calls=%async_computation.1 | async-start | bytes 786432 | tf_op jit(solution)/shard_map/all_to_all | solution.py:89
  198.5 2.7 %copy.11 = f32[384,768]{1,0:T(8,128)} copy(f32[384,768]{0,1:T(8,128)} %copy-done.3) | data formatting | bytes 2359296
  201.2 7.8 %all-to-all-done.1 = f32[4,24,1024]{2,1,0:T(8,128)S(1)} async-done(((f32[4,24,1024]{2,1,0:T(8,128)}), f32[4,24,1024]{2,1,0:T(8,128)S(1)}, u32[]{:S(2)}, u32[]{:S(2)}) %all-to-all-start.1) | async-done | bytes 393248 | tf_op jit(solution)/shard_map/all_to_all | solution.py:89
  (52 shorter events, 16.4 us)
Async XLA Ops:
  7.2 1.4 copy-start
  7.2 139.9 %all-gather.2.cloned.1.call-start = ((), (), s32[]{:S(2)}) async-start(), calls=%async_computation.2 | async-start | bytes 3538944 | tf_op jit(solution)/shard_map/all_gather | solution.py:151
  12.2 5.6 %collective-permute-start = (f32[384,1024]{1,0:T(8,128)}, f32[384,1024]{1,0:T(8,128)}, u32[]{:S(2)}, u32[]{:S(2)}) collective-permute-start(f32[384,1024]{1,0:T(8,128)} %fusion.6), channel_id=1, source_target_pairs={{0,16},{1,17},{2,18},{3,19},{4,20},{5,21},{6,22},{7,23},{8,24},{9,... | collective-permute-start | bytes 4718600 | tf_op jit(solution)/shard_map/ppermute | solution.py:22
  18.9 9.8 %collective-permute-start.1 = (f32[96,1024]{1,0:T(8,128)S(1)}, f32[96,1024]{1,0:T(8,128)}, u32[]{:S(2)}, u32[]{:S(2)}) collective-permute-start(f32[96,1024]{1,0:T(8,128)S(1)} %dynamic-slice_add_fusion), channel_id=1, source_target_pairs={{0,448},{1,449},{2,450},{3,451},{4,452},{5,453},{6,454},{7,455},{8... | collective-permute-start | bytes 1179656 | tf_op jit(solution)/shard_map/ppermute | solution.py:22
  29.9 14.8 %collective-permute-start.2 = (f32[96,1024]{1,0:T(8,128)S(1)}, f32[96,1024]{1,0:T(8,128)}, u32[]{:S(2)}, u32[]{:S(2)}) collective-permute-start(f32[96,1024]{1,0:T(8,128)S(1)} %add_add_fusion), channel_id=1, source_target_pairs={{0,64},{1,65},{2,66},{3,67},{4,68},{5,69},{6,70},{7,71},{8,72},{9,... | collective-permute-start | bytes 1179656 | tf_op jit(solution)/shard_map/ppermute | solution.py:22
  45.9 9.8 %collective-permute-start.3 = (f32[96,1024]{1,0:T(8,128)S(1)}, f32[96,1024]{1,0:T(8,128)}, u32[]{:S(2)}, u32[]{:S(2)}) collective-permute-start(f32[96,1024]{1,0:T(8,128)S(1)} %add_add_fusion.1), channel_id=1, source_target_pairs={{0,448},{1,449},{2,450},{3,451},{4,452},{5,453},{6,454},{7,455},{8... | collective-permute-start | bytes 1179656 | tf_op jit(solution)/shard_map/ppermute | solution.py:22
  56.8 8.8 %collective-permute-start.4 = (f32[48,1024]{1,0:T(8,128)S(1)}, f32[48,1024]{1,0:T(8,128)S(1)}, u32[]{:S(2)}, u32[]{:S(2)}) collective-permute-start(f32[48,1024]{1,0:T(8,128)S(1)} %constant_dynamic-slice_fusion.2), channel_id=1, source_target_pairs={{0,64},{1,65},{2,66},{3,67},{4,68},{5,69},{6,70},{7,71},{8,72},{9,... | collective-permute-start | bytes 589832 | tf_op jit(solution)/shard_map/ppermute | solution.py:22
  65.7 21.4 %collective-permute-start.5 = (f32[48,1024]{1,0:T(8,128)S(1)}, f32[48,1024]{1,0:T(8,128)S(1)}, u32[]{:S(2)}, u32[]{:S(2)}) collective-permute-start(f32[48,1024]{1,0:T(8,128)S(1)} %dynamic-slice_add_fusion.1), channel_id=1, source_target_pairs={{0,32},{1,33},{2,34},{3,35},{4,36},{5,37},{6,38},{7,39},{8,40},{9,... | collective-permute-start | bytes 589832 | tf_op jit(solution)/shard_map/ppermute | solution.py:22
  71.5 15.3 %collective-permute-start.6 = (f32[24,1024]{1,0:T(8,128)S(1)}, f32[24,1024]{1,0:T(8,128)S(1)}, u32[]{:S(2)}, u32[]{:S(2)}) collective-permute-start(f32[24,1024]{1,0:T(8,128)S(1)} %get-tuple-element.13), channel_id=1, source_target_pairs={{0,0},{1,32},{2,2},{3,34},{4,4},{5,36},{6,6},{7,38},{8,8},{9,40},{... | collective-permute-start | bytes 294920 | tf_op jit(solution)/shard_map/ppermute | solution.py:22
  75.8 11.3 %collective-permute-start.7 = (f32[24,1024]{1,0:T(8,128)S(1)}, f32[24,1024]{1,0:T(8,128)S(1)}, u32[]{:S(2)}, u32[]{:S(2)}) collective-permute-start(f32[24,1024]{1,0:T(8,128)S(1)} %get-tuple-element.14), channel_id=1, source_target_pairs={{0,1},{1,33},{2,3},{3,35},{4,5},{5,37},{6,7},{7,39},{8,9},{9,41},{... | collective-permute-start | bytes 294920 | tf_op jit(solution)/shard_map/ppermute | solution.py:22
  78.6 12.7 %collective-permute-start.8 = (f32[48,1024]{1,0:T(8,128)}, f32[48,1024]{1,0:T(8,128)S(1)}, u32[]{:S(2)}, u32[]{:S(2)}) collective-permute-start(f32[48,1024]{1,0:T(8,128)} %constant_dynamic-slice_fusion.3), channel_id=1, source_target_pairs={{0,0},{1,32},{2,64},{3,96},{4,128},{5,160},{6,192},{7,224},{8,256}... | collective-permute-start | bytes 589832 | tf_op jit(solution)/shard_map/ppermute | solution.py:22
  92.1 27.6 %copy-start.2 = (f32[384,768]{1,0:T(8,128)S(1)}, f32[384,768]{1,0:T(8,128)}, u32[]{:S(2)}) copy-start(f32[384,768]{1,0:T(8,128)} %param.2) | copy-start | bytes 3538948
  92.1 0.8 collective-permute-start.9
  113.1 14.1 %collective-permute-start.10 = (f32[96,1024]{1,0:T(8,128)S(1)}, f32[96,1024]{1,0:T(8,128)S(1)}, u32[]{:S(2)}, u32[]{:S(2)}) collective-permute-start(f32[96,1024]{1,0:T(8,128)S(1)} %maximum_select_fusion.2), channel_id=1, source_target_pairs={{0,4},{1,5},{2,6},{3,7},{4,0},{5,1},{6,2},{7,3},{8,12},{9,13},{10,... | collective-permute-start | bytes 1179656 | tf_op jit(solution)/shard_map/ppermute | solution.py:22
  127.2 29.9 %collective-permute-start.12 = (f32[192,1024]{1,0:T(8,128)S(1)}, f32[192,1024]{1,0:T(8,128)S(1)}, u32[]{:S(2)}, u32[]{:S(2)}) collective-permute-start(f32[192,1024]{1,0:T(8,128)S(1)} %maximum_select_fusion.1), channel_id=1, source_target_pairs={{0,12},{1,13},{2,14},{3,15},{4,8},{5,9},{6,10},{7,11},{8,4},{9,5},... | collective-permute-start | bytes 2359304 | tf_op jit(solution)/shard_map/ppermute | solution.py:22
  151.1 2.6 %copy-start.1 = (f32[2,384,1024]{2,1,0:T(8,128)S(1)}, f32[2,384,1024]{2,1,0:T(8,128)}, u32[]{:S(2)}) copy-start(f32[2,384,1024]{2,1,0:T(8,128)} %all-gather.2.cloned.1.call-done) | copy-start | bytes 9437188
  151.1 6.7 %collective-permute-start.13 = (f32[384,1024]{1,0:T(8,128)S(1)}, f32[384,1024]{1,0:T(8,128)S(1)}, u32[]{:S(2)}, u32[]{:S(2)}) collective-permute-start(f32[384,1024]{1,0:T(8,128)S(1)} %slice_bitcast_fusion), channel_id=1, source_target_pairs={{0,16},{1,17},{2,18},{3,19},{4,20},{5,21},{6,22},{7,23},{8,24},{9,... | collective-permute-start | bytes 4718600 | tf_op jit(solution)/shard_map/ppermute | solution.py:22
  154.2 6.5 %collective-permute-start.11 = (f32[384,1024]{1,0:T(8,128)S(1)}, f32[384,1024]{1,0:T(8,128)S(1)}, u32[]{:S(2)}, u32[]{:S(2)}) collective-permute-start(f32[384,1024]{1,0:T(8,128)S(1)} %get-tuple-element.25), channel_id=1, source_target_pairs={{0,16},{1,17},{2,18},{3,19},{4,20},{5,21},{6,22},{7,23},{8,24},{9,... | collective-permute-start | bytes 4718600 | tf_op jit(solution)/shard_map/ppermute | solution.py:22
  160.7 1.3 copy-start.4
  165.3 2.3 %copy-start.3 = (f32[384,768]{0,1:T(8,128)}, f32[384,768]{0,1:T(8,128)S(1)}, u32[]{:S(2)}) copy-start(f32[384,768]{0,1:T(8,128)S(1)} %compare_select_fusion) | copy-start | bytes 3538948
  193.4 15.5 %all-to-all-start.1 = ((f32[4,24,1024]{2,1,0:T(8,128)}), f32[4,24,1024]{2,1,0:T(8,128)S(1)}, u32[]{:S(2)}, u32[]{:S(2)}) async-start(f32[4,24,1024]{2,1,0:T(8,128)} %bitcast.8), calls=%async_computation.1 | async-start | bytes 786432 | tf_op jit(solution)/shard_map/all_to_all | solution.py:89
Sparse Core Ops, SparseCore 0:
  92.2 54.8 all-gather.1
